TPU v7x, 128 devices: a whole 4x4x4 slice. The times are simulated.
128 devices in a mesh: row: 8 (over y, x_lo), col: 16 (over z, x_hi, core).
Axes of the slice: x: 4 (x_hi: 2, x_lo: 2; x = x_hi * 2 + x_lo), y: 4, z: 4, core: 2. Of those that a mesh axis runs over, the one named last changes fastest.
Arguments:
- inputs: bfloat16 [1024, 8192], P('row', 'col'), may hold values from -6 to 6
- out_grad: bfloat16 [1024, 8192], P('row', 'col'), may hold values from -6 to 6
- gain: float32 [8192], P('col'), may hold values from 0.1 to 1.9
- w_gate: bfloat16 [8192, 28672], P('col', 'row'), may hold values from -0.0625 to 0.0625
- w_up: bfloat16 [8192, 28672], P('col', 'row'), may hold values from -0.0625 to 0.0625
- w_down: bfloat16 [28672, 8192], P('row', 'col'), may hold values from -0.03125 to 0.03125
- gate_pre: bfloat16 [1024, 28672], P('col', 'row'), may hold values from -8 to 8
- up_pre: bfloat16 [1024, 28672], P('col', 'row'), may hold values from -6 to 6
Outputs:
- d_input: bfloat16 [1024, 8192], P('row', 'col')
- grad_gain: float32 [8192], P('col')
- grad_gate: bfloat16 [8192, 28672], P('col', 'row')
- grad_up: bfloat16 [8192, 28672], P('col', 'row')
- grad_down: bfloat16 [28672, 8192], P('row', 'col')
All inputs are finite; a program needn't handle non-finite values.
Results may differ from a plain program's by a relative error of at most 0.0058.
Values may be sent and summed in bfloat16 or wider, within the bound.
No kernel may reach another device: no remote copies, remote signals or barrier semaphores. Data moves between devices by JAX's collectives and lax.ppermute only.
A program may use at most 128 MiB of HBM per device.

v0:
```python
import jax
import jax.numpy as jnp
from jax import lax
from jax.sharding import PartitionSpec as P

D = 8192


EPS = 1e-05


def contract_rows(left, right):
    return lax.dot_general(
        left, right, (((0,), (0,)), ((), ())), preferred_element_type=jnp.float32
    )


def contract_cols(left, right):
    return lax.dot_general(
        left, right, (((1,), (1,)), ((), ())), preferred_element_type=jnp.float32
    )


def input_grads(gate_all, up_all, w_gate, w_up):
    term = contract_cols(gate_all, w_gate) + contract_cols(up_all, w_up)
    return lax.psum_scatter(term, "row", scatter_dimension=0, tiled=True)


def local(inputs, out_grad, gain, w_gate, w_up, w_down, gate_pre, up_pre):
    values = inputs.astype(jnp.float32)
    squares = lax.psum(jnp.sum(values * values, axis=1), "col")
    rstd = lax.rsqrt(squares / D + EPS)
    normed = (values * rstd[:, None] * gain[None, :]).astype(jnp.bfloat16)
    out_all, normed_all = (
        lax.all_gather(out_grad, "row", axis=0, tiled=True),
        lax.all_gather(normed, "row", axis=0, tiled=True),
    )
    d_hidden = lax.psum_scatter(
        contract_cols(out_all, w_down), "col", scatter_dimension=0, tiled=True
    )
    gates = gate_pre.astype(jnp.float32)
    ups = up_pre.astype(jnp.float32)
    sig = jax.nn.sigmoid(gates)
    silu = gates * sig
    hidden = (silu * ups).astype(jnp.bfloat16)
    d_gate = (d_hidden * ups * sig * (1.0 + gates * (1.0 - sig))).astype(jnp.bfloat16)
    d_up = (d_hidden * silu).astype(jnp.bfloat16)
    hidden_all, gate_all, up_all = (
        lax.all_gather(hidden, "col", axis=0, tiled=True),
        lax.all_gather(d_gate, "col", axis=0, tiled=True),
        lax.all_gather(d_up, "col", axis=0, tiled=True),
    )
    d_normed = input_grads(gate_all, up_all, w_gate, w_up)
    grad_down = contract_rows(hidden_all, out_all).astype(jnp.bfloat16)
    grad_gate = contract_rows(normed_all, gate_all).astype(jnp.bfloat16)
    grad_up = contract_rows(normed_all, up_all).astype(jnp.bfloat16)
    grad_gain = lax.psum(jnp.sum(d_normed * values * rstd[:, None], axis=0), "row")
    proj = lax.psum(jnp.sum(d_normed * gain[None, :] * values, axis=1), "col")
    scaled = rstd * rstd * rstd * proj / D
    d_input = (
        out_grad.astype(jnp.float32)
        + rstd[:, None] * d_normed * gain[None, :]
        - values * scaled[:, None]
    ).astype(jnp.bfloat16)
    return (d_input, grad_gain, grad_gate, grad_up, grad_down)


def solution(mesh):
    in_specs = (
        P("row", "col"),
        P("row", "col"),
        P("col"),
        P("col", "row"),
        P("col", "row"),
        P("row", "col"),
        P("col", "row"),
        P("col", "row"),
    )
    out_specs = (P("row", "col"), P("col"), P("col", "row"), P("col", "row"), P("row", "col"))
    return jax.shard_map(local, mesh=mesh, in_specs=in_specs, out_specs=out_specs, check_vma=False)
```

profile of v0, /device:TPU:6, one launch (start us, length us, event | category | flops | bytes accessed | tf_op | source)
XLA Modules:
  0.0 529.4 jit_solution(10323713904499213299)
XLA Ops:
  7.2 0.0 all-gather.6.cloned.1.call-start
  7.2 0.7 all-gather.6.cloned.1.call-update
  7.9 0.0 reduce-scatter.3.cloned.1.call-start
  7.9 42.3 %all-gather.6.cloned.1.call-done = bf16[1024,512]{1,0:T(8,128)(2,1)} async-done(((bf16[128,512]{1,0:T(8,128)(2,1)}), bf16[1024,512]{1,0:T(8,128)(2,1)}) %all-gather.6.cloned.1.call-update) | async-done | bytes 1048592 | tf_op jit(solution)/shard_map/all_gather | solution.py:35
  50.3 11.6 %fusion.18 = f32[1024,3584]{1,0:T(8,128)} fusion(bf16[1024,512]{1,0:T(8,128)(2,1)} %all-gather.6.cloned.1.call-done, bf16[3584,512]{1,0:T(8,128)(2,1)} %param.13), kind=kOutput, calls=%fused_computation.35 | convolution fusion | flops 3758096384 | bytes 19398656 | tf_op jit(solution)/shard_map/dot_general | solution.py:19
  61.8 0.0 copy-start.2
  61.8 0.0 copy-start.3
  61.8 0.0 reduce-scatter.3.cloned.1.call-update
  61.9 0.0 all-gather.8.cloned.1.call-start
  61.9 132.7 %reduce-scatter.3.cloned.1.call-done = f32[64,3584]{1,0:T(8,128)} async-done(((f32[1024,3584]{1,0:T(8,128)}), f32[64,3584]{1,0:T(8,128)}) %reduce-scatter.3.cloned.1.call-update) | async-done | bytes 917520 | tf_op jit(solution)/shard_map/reduce_scatter | solution.py:38
  194.6 0.0 copy-done.2
  194.6 0.0 copy-done.3
  194.6 2.7 multiply_convert_fusion
  197.3 0.0 all-gather.8.cloned.1.call-update
  197.3 0.0 all-gather.10.cloned.1.call-start
  197.4 0.5 all-gather.10.cloned.1.call-update
  197.9 0.0 reduce-scatter.5.cloned.1.call-start
  197.9 66.2 %all-gather.8.cloned.1.call-done = bf16[1024,3584]{1,0:T(8,128)(2,1)} async-done(((bf16[64,3584]{1,0:T(8,128)(2,1)}), bf16[1024,3584]{1,0:T(8,128)(2,1)}) %all-gather.8.cloned.1.call-update) | async-done | bytes 7340048 | tf_op jit(solution)/shard_map/all_gather | solution.py:50
  264.2 7.3 %fusion.19 = f32[1024,512]{1,0:T(8,128)S(1)} fusion(bf16[1024,3584]{1,0:T(8,128)(2,1)} %all-gather.8.cloned.1.call-done, bf16[512,3584]{1,0:T(8,128)(2,1)} %param.11), kind=kOutput, calls=%fused_computation.36 | convolution fusion | flops 3758096384 | bytes 13107200 | tf_op jit(solution)/shard_map/dot_general | solution.py:19
  271.5 0.0 copy-start
  271.5 0.0 copy-start.4
  271.6 0.0 copy-start.1
  271.6 61.9 %all-gather.10.cloned.1.call-done = bf16[1024,3584]{1,0:T(8,128)(2,1)} async-done(((bf16[64,3584]{1,0:T(8,128)(2,1)}), bf16[1024,3584]{1,0:T(8,128)(2,1)}) %all-gather.10.cloned.1.call-update) | async-done | bytes 7340048 | tf_op jit(solution)/shard_map/all_gather | solution.py:51
  333.5 9.5 %convolution_add_fusion = f32[1024,512]{1,0:T(8,128)} fusion(f32[1024,512]{1,0:T(8,128)S(1)} %fusion.19, bf16[1024,3584]{1,0:T(8,128)(2,1)} %all-gather.10.cloned.1.call-done, bf16[512,3584]{1,0:T(8,128)(2,1)} %param.12), kind=kOutput, calls=%fused_computation.3 | convolution fusion | flops 3758620672 | bytes 15204352 | tf_op jit(solution)/shard_map/dot_general | solution.py:19
  343.0 0.0 copy-start.5
  343.0 0.0 reduce-scatter.5.cloned.1.call-update
  343.0 0.0 all-gather.14.cloned.1.call-start
  343.0 0.5 all-gather.14.cloned.1.call-update
  343.6 0.0 all-gather.12.cloned.1.call-start
  343.6 0.0 copy-done
  343.6 0.1 fusion.8
  343.7 31.9 %psum.21 = f32[128]{0:T(128)S(1)} all-reduce(f32[128]{0:T(128)S(1)} %fusion.8), channel_id=1, replica_groups=mesh['row'=8,'col'=16] {'col'}, use_global_device_ids=true, to_apply=%region_1.0 | all-reduce | flops 128 | bytes 1024 | tf_op jit(solution)/shard_map/psum | solution.py:31
  375.7 18.2 %reduce-scatter.5.cloned.1.call-done = f32[128,512]{1,0:T(8,128)} async-done(((f32[1024,512]{1,0:T(8,128)}), f32[128,512]{1,0:T(8,128)}) %reduce-scatter.5.cloned.1.call-update) | async-done | bytes 262160 | tf_op jit(solution)/shard_map/reduce_scatter | solution.py:26
  393.9 0.0 copy-done.4
  393.9 1.1 fusion.13
  395.0 32.9 %psum.22 = f32[128]{0:T(128)S(1)} all-reduce(f32[128]{0:T(128)S(1)} %get-tuple-element.6), channel_id=1, replica_groups=mesh['row'=8,'col'=16] {'col'}, use_global_device_ids=true, to_apply=%region_5.0 | all-reduce | flops 128 | bytes 1024 | tf_op jit(solution)/shard_map/psum | solution.py:58
  427.9 0.0 copy-done.1
  427.9 1.8 fusion.15
  429.7 0.0 all-gather.12.cloned.1.call-update
  429.7 35.1 %all-gather.14.cloned.1.call-done = bf16[1024,3584]{1,0:T(8,128)(2,1)} async-done(((bf16[64,3584]{1,0:T(8,128)(2,1)}), bf16[1024,3584]{1,0:T(8,128)(2,1)}) %all-gather.14.cloned.1.call-update) | async-done | bytes 7340048 | tf_op jit(solution)/shard_map/all_gather | solution.py:49
  464.8 0.0 copy-done.5
  464.8 8.6 %convolution_convert_fusion = bf16[3584,512]{1,0:T(8,128)(2,1)} fusion(bf16[1024,3584]{1,0:T(8,128)(2,1)} %all-gather.14.cloned.1.call-done, bf16[1024,512]{1,0:T(8,128)(2,1)S(1)} %copy-done.5), kind=kOutput, calls=%fused_computation | convolution fusion | flops 3759931392 | bytes 12058624 | tf_op jit(solution)/shard_map/dot_general | solution.py:13
  473.4 16.8 %psum.23 = f32[512]{0:T(512)} all-reduce(f32[512]{0:T(512)S(1)} %get-tuple-element.5), channel_id=1, replica_groups=mesh['row'=8,'col'=16] {'row'}, use_global_device_ids=true, to_apply=%region_7.0 | all-reduce | flops 512 | bytes 4096 | tf_op jit(solution)/shard_map/psum | solution.py:57
  490.2 14.5 %all-gather.12.cloned.1.call-done = bf16[1024,512]{1,0:T(8,128)(2,1)} async-done(((bf16[128,512]{1,0:T(8,128)(2,1)}), bf16[1024,512]{1,0:T(8,128)(2,1)}) %all-gather.12.cloned.1.call-update) | async-done | bytes 1048592 | tf_op jit(solution)/shard_map/all_gather | solution.py:36
  504.7 0.0 copy-start.6
  504.7 9.3 %convolution_convert_fusion.2 = bf16[512,3584]{1,0:T(8,128)(2,1)} fusion(bf16[1024,512]{1,0:T(8,128)(2,1)} %all-gather.12.cloned.1.call-done, bf16[1024,3584]{1,0:T(8,128)(2,1)} %all-gather.8.cloned.1.call-done), kind=kOutput, calls=%fused_computation.2 | convolution fusion | flops 3759931392 | bytes 12058624 | tf_op jit(solution)/shard_map/dot_general | solution.py:13
  514.1 0.0 copy-done.6
  514.1 8.5 %convolution_convert_fusion.1 = bf16[512,3584]{1,0:T(8,128)(2,1)} fusion(bf16[1024,512]{1,0:T(8,128)(2,1)S(1)} %copy-done.6, bf16[1024,3584]{1,0:T(8,128)(2,1)} %all-gather.10.cloned.1.call-done), kind=kOutput, calls=%fused_computation.1 | convolution fusion | flops 3759931392 | bytes 12058624 | tf_op jit(solution)/shard_map/dot_general | solution.py:13
  (2 shorter events, 0.0 us)
Async XLA Ops:
  7.2 43.1 %all-gather.6.cloned.1.call-start = ((), (), s32[]{:S(2)}) async-start(), calls=%async_computation.2 | async-start | bytes 1179648 | tf_op jit(solution)/shard_map/all_gather | solution.py:35
  7.9 186.7 %reduce-scatter.3.cloned.1.call-start = ((), (), s32[]{:S(2)}) async-start(), calls=%async_computation.3 | async-start | bytes 15597568 | tf_op jit(solution)/shard_map/reduce_scatter | solution.py:38
  61.8 132.8 %copy-start.2 = (bf16[64,3584]{1,0:T(8,128)(2,1)S(1)}, bf16[64,3584]{1,0:T(8,128)(2,1)}, u32[]{:S(2)}) copy-start(bf16[64,3584]{1,0:T(8,128)(2,1)} %param.14) | copy-start | bytes 1376260
  61.8 132.8 %copy-start.3 = (bf16[64,3584]{1,0:T(8,128)(2,1)S(1)}, bf16[64,3584]{1,0:T(8,128)(2,1)}, u32[]{:S(2)}) copy-start(bf16[64,3584]{1,0:T(8,128)(2,1)} %param.15) | copy-start | bytes 1376260
  61.9 202.3 %all-gather.8.cloned.1.call-start = ((), (), s32[]{:S(2)}) async-start(), calls=%async_computation.4 | async-start | bytes 7798784 | tf_op jit(solution)/shard_map/all_gather | solution.py:50
  197.3 136.2 %all-gather.10.cloned.1.call-start = ((), (), s32[]{:S(2)}) async-start(), calls=%async_computation.5 | async-start | bytes 7798784 | tf_op jit(solution)/shard_map/all_gather | solution.py:51
  197.9 196.0 %reduce-scatter.5.cloned.1.call-start = ((), (), s32[]{:S(2)}) async-start(), calls=%async_computation.6 | async-start | bytes 2359296 | tf_op jit(solution)/shard_map/reduce_scatter | solution.py:26
  271.5 72.1 %copy-start = (bf16[128,512]{1,0:T(8,128)(2,1)S(1)}, bf16[128,512]{1,0:T(8,128)(2,1)}, u32[]{:S(2)}) copy-start(bf16[128,512]{1,0:T(8,128)(2,1)} %param.8) | copy-start | bytes 393220
  271.5 122.4 %copy-start.4 = (f32[512]{0:T(512)S(1)}, f32[512]{0:T(512)}, u32[]{:S(2)}) copy-start(f32[512]{0:T(512)} %param.10) | copy-start | bytes 6148
  271.6 156.3 %copy-start.1 = (bf16[128,512]{1,0:T(8,128)(2,1)S(1)}, bf16[128,512]{1,0:T(8,128)(2,1)}, u32[]{:S(2)}) copy-start(bf16[128,512]{1,0:T(8,128)(2,1)} %param.9) | copy-start | bytes 393220
  343.0 121.9 %copy-start.5 = (bf16[1024,512]{1,0:T(8,128)(2,1)S(1)}, bf16[1024,512]{1,0:T(8,128)(2,1)}, u32[]{:S(2)}) copy-start(bf16[1024,512]{1,0:T(8,128)(2,1)} %all-gather.6.cloned.1.call-done) | copy-start | bytes 3145732
  343.0 121.8 %all-gather.14.cloned.1.call-start = ((), (), s32[]{:S(2)}) async-start(), calls=%async_computation.8 | async-start | bytes 7798784 | tf_op jit(solution)/shard_map/all_gather | solution.py:49
  343.6 161.2 %all-gather.12.cloned.1.call-start = ((), (), s32[]{:S(2)}) async-start(), calls=%async_computation.7 | async-start | bytes 1179648 | tf_op jit(solution)/shard_map/all_gather | solution.py:36
  504.7 9.3 %copy-start.6 = (bf16[1024,512]{1,0:T(8,128)(2,1)S(1)}, bf16[1024,512]{1,0:T(8,128)(2,1)}, u32[]{:S(2)}) copy-start(bf16[1024,512]{1,0:T(8,128)(2,1)} %all-gather.12.cloned.1.call-done) | copy-start | bytes 3145732
Sparse Core Ops, SparseCore 0:
  9.6 40.5 all-gather.5
  62.0 132.5 reduce-scatter.2
  197.7 66.4 all-gather.7
  267.1 66.3 all-gather.9
  343.1 50.7 reduce-scatter.4
  396.8 67.9 all-gather.13
  467.0 37.6 all-gather.11
where the time goes:
time: 532 us; the launch traced here: 529 us
  waiting for transfers between devices  373 us (70%)
  blocking collectives  81.6 us (15%)
  matrix products  54.8 us (10%)
  between operations  14.2 us (3%)
  other arithmetic  5.7 us (1%)
    reduce_scatter x1, waiting for transfers between devices, local(): lax.psum_scatter(contract_cols(out_all, w_down), 'col', scatter_dimension...  133 us
    all_gather x1, waiting for transfers between devices, local(): lax.all_gather(d_gate, 'col', axis=0, tiled=True)  66.2 us
    all_gather x1, waiting for transfers between devices, local(): lax.all_gather(d_up, 'col', axis=0, tiled=True)  61.9 us
    all_gather x1, waiting for transfers between devices, local(): lax.all_gather(out_grad, 'row', axis=0, tiled=True)  42.3 us
    all_gather x1, waiting for transfers between devices, local(): lax.all_gather(hidden, 'col', axis=0, tiled=True)  35.1 us
    psum x1, blocking collectives, local(): proj = lax.psum(jnp.sum(d_normed * gain[None, :] * values, axis=1), 'col')  32.9 us
    psum x1, blocking collectives, local(): squares = lax.psum(jnp.sum(values * values, axis=1), 'col')  31.9 us
    dot_general x3, matrix products, contract_cols(): lax.dot_general(left, right, (((1,), (1,)), ((), ())), preferred_element_...  28.4 us
  transfers between devices with their start and end apart: 7, of which 7 were waited for; matrix products, arithmetic and copies ran while one was open for 4% of the time, Pallas kernels for 0%

commit v1 on v0

v1 whole, which is shorter than its diff:
```python
import jax
import jax.numpy as jnp
from jax import lax
from jax.experimental import pallas as pl
from jax.experimental.pallas import tpu as pltpu
from jax.sharding import PartitionSpec as P

EPS = 1e-05
NZ, NX, NC = 4, 2, 2
NY, NL = 4, 2
F32, BF16 = jnp.float32, jnp.bfloat16


def dot(left, right, a, b):
    return lax.dot_general(left, right, (((a,), (b,)), ((), ())), preferred_element_type=F32)


def kernel_call(body, name, steps, in_specs, out_specs, out_shape, scratch, args):
    return pl.pallas_call(
        body,
        grid=(steps,),
        in_specs=in_specs,
        out_specs=out_specs,
        out_shape=out_shape,
        scratch_shapes=scratch,
        compiler_params=pltpu.CompilerParams(vmem_limit_bytes=60 * 2**20),
        name=name,
    )(*args)


def hidden_units(left, left_other, w, w_other, steps):
    m, f = left.shape
    width = w.shape[0]
    n = width // steps

    def body(l, lo, w, wo, out):
        out[...] = dot(l[...], w[...], 1, 1) + dot(lo[...], wo[...], 1, 1)

    lefts = [pl.BlockSpec((m, f), lambda i: (0, 0))] * 2
    rights = [pl.BlockSpec((n, f), lambda i: (i, 0))] * 2
    return kernel_call(
        body, "hidden_units", steps, lefts + rights, pl.BlockSpec((m, n), lambda i: (0, i)),
        jax.ShapeDtypeStruct((m, width), F32), [], (left, left_other, w, w_other),
    )


def input_grads(pieces, w_gate, w_up, steps):
    f, width = w_gate.shape
    tok, k, count = pieces[0].shape[0] // 2, width // steps, len(pieces)

    def body(*refs):
        parts, (wg, wu, out) = refs[:count], refs[count:]
        gate = jnp.concatenate([p[:tok] for p in parts], axis=0)
        up = jnp.concatenate([p[tok:] for p in parts], axis=0)
        total = dot(gate, wg[...], 1, 1) + dot(up, wu[...], 1, 1)

        @pl.when(pl.program_id(0) == 0)
        def _():
            out[...] = total

        @pl.when(pl.program_id(0) > 0)
        def _():
            out[...] += total

    specs = [pl.BlockSpec((2 * tok, k), lambda i: (0, i))] * count + [pl.BlockSpec((f, k), lambda i: (0, i))] * 2
    m = tok * count
    return kernel_call(
        body, "input_grads", steps, specs, pl.BlockSpec((m, f), lambda i: (0, 0)),
        jax.ShapeDtypeStruct((m, f), F32), [], (*pieces, w_gate, w_up),
    )


def gate_up_grads(normed_t, pieces, steps):
    f, t = normed_t.shape
    tok, width, count = pieces[0].shape[0] // 2, pieces[0].shape[1], len(pieces)
    n = width // steps

    def body(left, *refs):
        parts, (gate_out, up_out) = refs[:count], refs[count:]
        left = left[...]
        gate_out[...] = dot(left, jnp.concatenate([p[:tok] for p in parts], axis=0), 1, 0).astype(BF16)
        up_out[...] = dot(left, jnp.concatenate([p[tok:] for p in parts], axis=0), 1, 0).astype(BF16)

    specs = [pl.BlockSpec((f, t), lambda i: (0, 0))] + [pl.BlockSpec((2 * tok, n), lambda i: (0, i))] * count
    return kernel_call(
        body, "gate_up_grads", steps, specs, [pl.BlockSpec((f, n), lambda i: (0, i))] * 2,
        [jax.ShapeDtypeStruct((f, width), BF16)] * 2, [], (normed_t, *pieces),
    )


def down_grads(hid, hid_other, out, steps):
    f, (t, width) = out.shape[1], hid.shape
    n = width // steps

    def body(left, left_other, right, total):
        total[...] = (dot(left[...], right[:t], 0, 0) + dot(left_other[...], right[t:], 0, 0)).astype(BF16)

    specs = [pl.BlockSpec((t, n), lambda i: (0, i))] * 2 + [pl.BlockSpec((2 * t, f), lambda i: (0, 0))]
    return kernel_call(
        body, "down_grads", steps, specs, pl.BlockSpec((n, f), lambda i: (i, 0)),
        jax.ShapeDtypeStruct((width, f), BF16), [], (hid, hid_other, out),
    )


def col_to(x, name, dz=0, dx=0, dc=0):
    pairs = []
    for z in range(NZ):
        for h in range(NX):
            for c in range(NC):
                dst = (((z + dz) % NZ) * NX + (h + dx) % NX) * NC + (c + dc) % NC
                pairs.append(((z * NX + h) * NC + c, dst))
    with jax.named_scope(name):
        return lax.ppermute(x, "col", pairs)


def row_to(x, name, dy=0, dl=0):
    pairs = []
    for y in range(NY):
        for l in range(NL):
            pairs.append((y * NL + l, ((y + dy) % NY) * NL + (l + dl) % NL))
    with jax.named_scope(name):
        return lax.ppermute(x, "row", pairs)


def phase(*arrays):
    return lax.optimization_barrier(arrays)


def local(inputs, out_grad, gain, w_gate, w_up, w_down, gate_pre, up_pre):
    rows, feats = inputs.shape
    width = gate_pre.shape[1]
    tok = gate_pre.shape[0]
    half = tok // 2
    total_feats = feats * NZ * NX * NC
    halves = width // 2 if width // 2 % 128 == 0 else width
    steps = width // halves
    col, row = lax.axis_index("col"), lax.axis_index("row")
    z, h, c = col // (NX * NC), (col // NC) % NX, col % NC
    y, l = row // NL, row % NL

    same = (l + h) % NX == 0

    def order(mine, other):
        f = mine.shape[1]
        mine, other = mine.reshape(NC, tok, f), other.reshape(NC, tok, f)
        pair = jnp.stack([jnp.where(same, mine, other), jnp.where(same, other, mine)])
        return jnp.where(c == 0, pair, pair[:, ::-1])[:, :, None]

    def assemble(pairs):
        full = jnp.zeros((NX, NC, NZ, *pairs[0].shape[3:]), pairs[0].dtype)
        for ky, pair in enumerate(pairs):
            full = lax.dynamic_update_slice(full, pair, (0, 0, (y + ky - z) % NZ, 0, 0))
        return full

    def swap(pieces, name):
        return [col_to(piece, name, dc=1) for piece in pieces]

    def neighbour(x, name):
        with jax.named_scope(name):
            return lax.ppermute(x, "col", [(i, i ^ NC * NX) for i in range(NZ * NX * NC)])

    def neighbour_row(x, name):
        with jax.named_scope(name):
            return lax.ppermute(x, "row", [(i, i ^ NL) for i in range(NY * NL)])

    def gather_hidden(x, name):
        groups = [[chip * NC + core for chip in range(NZ * NX)] for core in range(NC)]
        copies = jnp.broadcast_to(x[None], (NZ * NX, *x.shape))
        with jax.named_scope(name):
            return lax.all_to_all(copies, "col", 0, 0, axis_index_groups=groups, tiled=True).reshape(-1, x.shape[1])

    out_xl = row_to(out_grad, "out_xl", dl=1)
    w_down_other = col_to(w_down, "w_down", dc=1)
    gates = gate_pre.astype(F32)
    ups = up_pre.astype(F32)
    sig = jax.nn.sigmoid(gates)
    hidden = (gates * sig * ups).astype(BF16)
    hidden_a, hidden_b = hidden[:, :halves], hidden[:, halves:]
    pair = order(out_grad, out_xl)
    pair, hidden_a, hidden_b = phase(pair, hidden_a, hidden_b)

    out_y = [row_to(pair, "out_y", -ky) for ky in range(1, NY)]
    hid_a = gather_hidden(hidden_a, "hid_a")
    out_all = assemble([pair] + out_y)
    out_mine = out_all[:, 0].reshape(-1, feats)
    out_theirs = out_all[:, 1].reshape(-1, feats)
    out_mine, out_theirs, w_down_other = phase(out_mine, out_theirs, w_down_other)

    out_other = col_to(out_theirs, "out_core", dc=1)
    cut = NZ * tok
    far = hidden_units(out_mine[cut:], out_other[cut:], w_down, w_down_other, steps)
    far = [far[k * tok:(k + 1) * tok] for k in range(NZ)]
    far = [far[0]] + [p.astype(BF16) for p in far[1:]]
    *far, hid_a, out_mine, out_other = phase(*far, hid_a, out_mine, out_other)

    x_in = col_to(far[2], "rs_x", dx=1)
    b_in = col_to(far[1], "rs_b", dz=1)
    a_in = col_to(far[3], "rs_a", dz=-1)
    near = hidden_units(out_mine[:cut], out_other[:cut], w_down, w_down_other, steps)
    near = [near[k * tok:(k + 1) * tok] for k in range(NZ)]
    x_sum = (far[0] + b_in.astype(F32) + a_in.astype(F32)).astype(BF16)
    x_in, x_sum = phase(x_in, x_sum)
    pair = (near[2] + x_in.astype(F32)).astype(BF16)
    pair, x_sum, near0, near1, near3 = phase(pair, x_sum, near[0], near[1], near[3])
    b_half = col_to(pair[:half], "rs_fb", dz=1)
    a_half = col_to(pair[half:], "rs_fa", dz=-1)
    x_last = col_to(x_sum, "rs_xl", dx=1)
    b_sum = jnp.concatenate([near1[:half] + b_half.astype(F32), near1[half:]], axis=0).astype(BF16)
    a_sum = jnp.concatenate([near3[:half], near3[half:] + a_half.astype(F32)], axis=0).astype(BF16)
    b_sum, a_sum = phase(b_sum, a_sum)
    b_last = col_to(b_sum, "rs_bl", dz=1)
    a_last = col_to(a_sum, "rs_al", dz=-1)
    d_hidden = near0 + x_last.astype(F32) + b_last.astype(F32) + a_last.astype(F32)
    silu = gates * sig
    d_gate = (d_hidden * ups * sig * (1.0 + gates * (1.0 - sig))).astype(BF16)
    d_up = (d_hidden * silu).astype(BF16)
    both, own = phase(jnp.concatenate([d_gate, d_up], axis=0), inputs)

    both_x = col_to(both, "ag_x", dx=1)
    both_b = col_to(both, "ag_b", dz=1)
    both_a = col_to(both, "ag_a", dz=-1)
    copies = jnp.broadcast_to(own[None], (NY * NL, rows, feats))
    with jax.named_scope("input_rows"):
        whole = lax.all_to_all(copies, "row", 0, 0, tiled=True)
    both_x = phase(both_x, both_b, both_a)[0]
    both, both_x, both_b, both_a, hid_a = phase(both, both_x, both_b, both_a, hid_a)

    far_b = col_to(both_b[:tok], "ag_fb", dz=1)
    far_a = col_to(both_a[tok:], "ag_fa", dz=-1)
    swapped = swap([both], "ag_core")
    both_f = jnp.concatenate([far_b, far_a], axis=0)
    values_all = whole.astype(F32)
    squares = jnp.sum(values_all * values_all, axis=2)
    squares = squares + col_to(squares, "squares", dc=1)
    squares = squares + col_to(squares, "squares", dx=1)
    both, *swapped, both_f, both_x, both_a, both_b, whole, squares, hid_a = phase(
        both, *swapped, both_f, both_x, both_a, both_b, whole, squares, hid_a
    )

    both_xb = col_to(both_x, "ag_xb", dz=1)
    both_xa = col_to(both_x, "ag_xa", dz=-1)
    both_xf = col_to(both_f, "ag_xf", dx=1)
    swapped += swap([both_a, both_f, both_b, both_x], "ag_core")
    first = [both, both_a, both_f, both_b, *swapped[:4], both_x, swapped[4]]
    term_first = input_grads(first, w_gate, w_up, steps)
    hid_a_other = col_to(hid_a, "hid_core", dc=1)
    out_down = jnp.where(h == 0, out_all, out_all[::-1]).transpose(1, 2, 0, 3, 4)
    out_down = lax.dynamic_slice_in_dim(jnp.concatenate([out_down, out_down], axis=1), (NZ - z) % NZ, NZ, axis=1)
    out_down = out_down.reshape(-1, feats)
    down_a = down_grads(hid_a, hid_a_other, out_down, 1)
    pairs = []
    for at in range(NY):
        even, odd = whole[at * NL].reshape(NC, tok, feats), whole[at * NL + 1].reshape(NC, tok, feats)
        one = jnp.stack([jnp.where(h == 0, even, odd), jnp.where(h == 0, odd, even)])
        pairs.append(jnp.where(c == 0, one, one[:, ::-1])[:, :, None])
    in_all = jnp.zeros((NX, NC, NZ, tok, feats), BF16)
    for at, one in enumerate(pairs):
        in_all = lax.dynamic_update_slice(in_all, one, (0, 0, (at - z) % NZ, 0, 0))
    in_t = in_all.reshape(-1, feats).T
    squares = squares + neighbour(squares, "squares")
    both_xb, both_xa, both_xf, term_first, in_t, down_a, squares, hidden_b = phase(
        both_xb, both_xa, both_xf, term_first, in_t, down_a, squares, hidden_b
    )

    hid_b = gather_hidden(hidden_b, "hid_b")
    squares = squares + col_to(squares, "squares", dz=2)
    rstd_all = lax.rsqrt(squares / total_feats + EPS)
    rstd = lax.dynamic_index_in_dim(rstd_all, row, 0, keepdims=False)
    rstd_all = rstd_all.reshape(NY, NL, NC, tok)
    rstd_all = lax.dynamic_slice_in_dim(jnp.concatenate([rstd_all, rstd_all]), z, NZ).transpose(1, 2, 0, 3)
    rstd_all = jnp.where(h == 0, rstd_all, rstd_all[::-1])
    rstd_all = jnp.where(c == 0, rstd_all, rstd_all[:, ::-1]).reshape(1, -1)
    normed_t = (in_t.astype(F32) * rstd_all * gain[:, None]).astype(BF16)
    swapped_x = swap([both_xa, both_xf, both_xb], "ag_core")
    second = [both_xa, both_xf, both_xb, *swapped_x]
    term_second = input_grads(second, w_gate, w_up, steps)
    order_of = first[:8] + [first[8]] + second[:3] + [first[9]] + second[3:]
    term = jnp.concatenate([
        term_first[:9 * tok], term_second[:3 * tok], term_first[9 * tok:], term_second[3 * tok:]
    ], axis=0).reshape(NX, NC, NZ, tok, feats)

    def term_of(ky):
        return lax.dynamic_slice(term, (0, 0, (y + ky - z) % NZ, 0, 0), (NX, NC, 1, tok, feats))[:, :, 0]

    mine, normed_t, rstd, *sent = phase(
        term_of(0), normed_t, rstd, *[term_of(ky).astype(BF16) for ky in range(1, NY)]
    )
    received = [row_to(piece, "dn_y", ky + 1) for ky, piece in enumerate(sent)]
    grad_gate, grad_up = gate_up_grads(normed_t, order_of, steps)
    d_normed = mine
    for piece in received:
        d_normed = d_normed + piece.astype(F32)
    near, far = (jnp.where(same, d_normed[i], d_normed[1 - i]) for i in range(2))
    near, far, grad_gate, grad_up, hid_b = phase(near, far.astype(BF16), grad_gate, grad_up, hid_b)

    d_normed = near + row_to(far, "dn_xl", dl=1).astype(F32)
    d_normed = jnp.where(c == 0, d_normed, d_normed[::-1]).reshape(rows, feats)
    hid_b_other = col_to(hid_b, "hid_core", dc=1)
    values = inputs.astype(F32)
    proj = jnp.sum(d_normed * gain[None, :] * values, axis=1).reshape(1, rows)
    grad_gain = jnp.sum(d_normed * values * rstd[:, None], axis=0).reshape(1, feats)
    proj, grad_gain, hid_b_other = phase(proj, grad_gain, hid_b_other)

    proj = proj + col_to(proj, "proj", dc=1)
    grad_gain = grad_gain + row_to(grad_gain, "gain", dl=1)
    proj, grad_gain = phase(proj, grad_gain)
    proj = proj + col_to(proj, "proj", dx=1)
    grad_gain = grad_gain + neighbour_row(grad_gain, "gain")
    proj, grad_gain = phase(proj, grad_gain)
    proj = proj + neighbour(proj, "proj")
    grad_gain = grad_gain + row_to(grad_gain, "gain", dy=2)
    proj, grad_gain = phase(proj, grad_gain)
    down_b = down_grads(hid_b, hid_b_other, out_down, 1)
    grad_down = jnp.concatenate([down_a, down_b], axis=0)
    proj = (proj + col_to(proj, "proj", dz=2)).reshape(rows)
    scaled = rstd * rstd * rstd * proj / total_feats
    d_input = (
        out_grad.astype(F32) + rstd[:, None] * d_normed * gain[None, :] - values * scaled[:, None]
    ).astype(BF16)
    return (d_input, grad_gain.reshape(feats), grad_gate, grad_up, grad_down)


def solution(mesh):
    in_specs = (
        P("row", "col"),
        P("row", "col"),
        P("col"),
        P("col", "row"),
        P("col", "row"),
        P("row", "col"),
        P("col", "row"),
        P("col", "row"),
    )
    out_specs = (P("row", "col"), P("col"), P("col", "row"), P("col", "row"), P("row", "col"))
    return jax.shard_map(local, mesh=mesh, in_specs=in_specs, out_specs=out_specs, check_vma=False)
```

time: 532 us -> 230 us (0.43)
  waiting for transfers between devices: 373 us -> 74.2 us
  blocking collectives: 81.6 us -> 0 us
  starting transfers between devices: 0.28 us -> 67.1 us
  matrix products: 54.8 us -> 0 us
  Pallas kernels: 0 us -> 52.7 us
  local copies, waits for them, and re-layouts: 0.03 us -> 15.6 us
  between operations: 14.2 us -> 1.24 us
  other arithmetic: 5.7 us -> 18.5 us
    all_gather x5 -> x0, waiting for transfers between devices: 220 us -> none  [the longest x1 66.2 us: local(): lax.all_gather(d_gate, 'col', axis=0, tiled=True)]
    reduce_scatter x2 -> x0, waiting for transfers between devices: 151 us -> none  [the longest x1 133 us: local(): lax.psum_scatter(contract_cols(out_all, w_down), 'col', scatter_dimension...]
    psum x3 -> x0, blocking collectives: 81.6 us -> none  [the longest x1 32.9 us: local(): proj = lax.psum(jnp.sum(d_normed * gain[None, :] * values, axis=1), 'col')]
    ppermute x0 -> x47, waiting for transfers between devices: none -> 66.5 us  [the longest x34 50.1 us: col_to(): return lax.ppermute(x, 'col', pairs)]
    dot_general x6 -> x0, matrix products: 54.8 us -> none  [the longest x3 28.4 us: contract_cols(): lax.dot_general(left, right, (((1,), (1,)), ((), ())), preferred_element_...]
    pallas_call x0 -> x7, Pallas kernels: none -> 52.7 us  [kernel_call(): pl.pallas_call(body, grid=(steps,), in_specs=in_specs, out_specs=out_spec...]
    ppermute x0 -> x47, starting transfers between devices: none -> 45.4 us  [the longest x34 27.5 us: col_to(): return lax.ppermute(x, 'col', pairs)]
    all_to_all x0 -> x3, starting transfers between devices: none -> 21.8 us  [the longest x2 16.2 us: gather_hidden(): lax.all_to_all(copies, 'col', 0, 0, axis_index_groups=groups, tiled=True)]
  transfers between devices with their start and end apart: 7 -> 50, of which waited for: 7 -> 23; matrix products, arithmetic and copies ran while one was open for 4% -> 13% of each run, Pallas kernels for 0% -> 23%
where the time goes in v1:
time: 230 us; the launch traced here: 229 us
  waiting for transfers between devices  74.2 us (32%)
  starting transfers between devices  67.1 us (29%)
  Pallas kernels  52.7 us (23%)
  other arithmetic  18.5 us (8%)
  local copies, waits for them, and re-layouts  15.6 us (7%)
    pallas_call x7, Pallas kernels, kernel_call(): pl.pallas_call(body, grid=(steps,), in_specs=in_specs, out_specs=out_spec...  52.7 us
    ppermute x34, waiting for transfers between devices, col_to(): return lax.ppermute(x, 'col', pairs)  50.1 us
    ppermute x34, starting transfers between devices, col_to(): return lax.ppermute(x, 'col', pairs)  27.5 us
    all_to_all x2, starting transfers between devices, gather_hidden(): lax.all_to_all(copies, 'col', 0, 0, axis_index_groups=groups, tiled=True)  16.2 us
    ppermute x10, starting transfers between devices, row_to(): return lax.ppermute(x, 'row', pairs)  14.6 us
    ppermute x10, waiting for transfers between devices, row_to(): return lax.ppermute(x, 'row', pairs)  13.5 us
    all_to_all x2, waiting for transfers between devices, gather_hidden(): lax.all_to_all(copies, 'col', 0, 0, axis_index_groups=groups, tiled=True)  7.71 us
    all_to_all x1, starting transfers between devices, local(): whole = lax.all_to_all(copies, 'row', 0, 0, tiled=True)  5.58 us
  transfers between devices with their start and end apart: 50, of which 23 were waited for; matrix products, arithmetic and copies ran while one was open for 13% of the time, Pallas kernels for 23%

profile of v1, /device:TPU:6, one launch (start us, length us, event | category | flops | bytes accessed | tf_op | source)
XLA Modules:
  0.0 229.3 jit_solution(14609639634755248066)
XLA Ops:
  1.6 1.4 fusion.2
  3.8 3.1 %collective-permute-done = bf16[128,512]{1,0:T(8,128)(2,1)S(1)} collective-permute-done((bf16[128,512]{1,0:T(8,128)(2,1)}, bf16[128,512]{1,0:T(8,128)(2,1)S(1)}, u32[]{:S(2)}, u32[]{:S(2)}) %collective-permute-start) | collective-permute-done | bytes 131104 | tf_op jit(solution)/shard_map/out_xl/ppermute | solution.py:122
  7.0 3.1 %collective-permute-start.1 = (bf16[2,2,1,64,512]{4,3,1,0,2:T(8,128)(2,1)S(1)}, bf16[2,2,1,64,512]{4,3,1,0,2:T(8,128)(2,1)S(1)}, u32[]{:S(2)}, u32[]{:S(2)}) collective-permute-start(bf16[2,2,1,64,512]{4,3,1,0,2:T(8,128)(2,1)S(1)} %fusion.11), channel_id=1, source_target_pairs={{0,96},{16,112},{32,0},{48,16},{64,32},{80,48},{96,64},{112,80},{1... | collective-permute-start | bytes 786440 | tf_op jit(solution)/shard_map/out_y/ppermute | solution.py:122
  11.7 1.4 broadcast_in_dim.17
  13.0 8.3 %all-to-all-start = ((bf16[8,64,1792]{2,1,0:T(8,128)(2,1)}), bf16[8,64,1792]{2,1,0:T(8,128)(2,1)}, u32[]{:S(2)}, u32[]{:S(2)}) async-start(bf16[8,64,1792]{2,1,0:T(8,128)(2,1)} %broadcast_in_dim.17), calls=%async_computation | async-start | bytes 3670016 | tf_op jit(solution)/shard_map/hid_a/all_to_all | solution.py:170
  21.5 3.2 %collective-permute-done.3 = bf16[2,2,1,64,512]{4,3,1,0,2:T(8,128)(2,1)S(1)} collective-permute-done((bf16[2,2,1,64,512]{4,3,1,0,2:T(8,128)(2,1)S(1)}, bf16[2,2,1,64,512]{4,3,1,0,2:T(8,128)(2,1)S(1)}, u32[]{:S(2)}, u32[]{:S(2)}) %collective-permute-start.3) | collective-permute-done | bytes 262176 | tf_op jit(solution)/shard_map/out_y/ppermute | solution.py:122
  27.6 5.7 %hidden_units.2 = f32[256,3584]{1,0:T(8,128)} custom-call(bf16[256,512]{1,0:T(8,128)(2,1)} %slice.125.l, bf16[256,512]{1,0:T(8,128)(2,1)} %slice.163.lo, bf16[3584,512]{1,0:T(8,128)(2,1)} %w.3, bf16[3584,512]{1,0:T(8,128)(2,1)} %collective-permute-done.4.wo), custom_call_target="tpu_custom_call" | custom-call | tf_op jit(solution)/shard_map/hidden_units/pallas_call | solution.py:19
  33.3 2.2 convert.19
  35.6 7.7 %all-to-all-done = bf16[8,64,1792]{2,1,0:T(8,128)(2,1)} async-done(((bf16[8,64,1792]{2,1,0:T(8,128)(2,1)}), bf16[8,64,1792]{2,1,0:T(8,128)(2,1)}, u32[]{:S(2)}, u32[]{:S(2)}) %all-to-all-start) | async-done | bytes 1835040 | tf_op jit(solution)/shard_map/hid_a/all_to_all | solution.py:170
  46.8 2.7 %collective-permute-start.6 = (bf16[64,3584]{1,0:T(8,128)(2,1)S(1)}, bf16[64,3584]{1,0:T(8,128)(2,1)S(1)}, u32[]{:S(2)}, u32[]{:S(2)}) collective-permute-start(bf16[64,3584]{1,0:T(8,128)(2,1)S(1)} %get-tuple-element.81), channel_id=1, source_target_pairs={{0,2},{1,3},{2,0},{3,1},{4,6},{5,7},{6,4},{7,5},{8,10},{9,11},{10,... | collective-permute-start | bytes 1376264 | tf_op jit(solution)/shard_map/rs_x/ppermute | solution.py:113
  49.5 5.7 %hidden_units.3 = f32[256,3584]{1,0:T(8,128)} custom-call(bf16[256,512]{1,0:T(8,128)(2,1)} %slice.131.l, bf16[256,512]{1,0:T(8,128)(2,1)} %slice.132.lo, bf16[3584,512]{1,0:T(8,128)(2,1)} %w.3, bf16[3584,512]{1,0:T(8,128)(2,1)} %collective-permute-done.4.wo), custom_call_target="tpu_custom_call" | custom-call | tf_op jit(solution)/shard_map/hidden_units/pallas_call | solution.py:19
  55.2 2.8 %collective-permute-done.7 = bf16[64,3584]{1,0:T(8,128)(2,1)} collective-permute-done((bf16[64,3584]{1,0:T(8,128)(2,1)S(1)}, bf16[64,3584]{1,0:T(8,128)(2,1)}, u32[]{:S(2)}, u32[]{:S(2)}) %collective-permute-start.7) | collective-permute-done | bytes 458784 | tf_op jit(solution)/shard_map/rs_b/ppermute | solution.py:113
  59.6 2.3 fusion.36
  63.2 2.2 collective-permute-start.11
  66.0 3.3 %collective-permute-done.10 = bf16[32,3584]{1,0:T(8,128)(2,1)S(1)} collective-permute-done((bf16[32,3584]{1,0:T(8,128)(2,1)S(1)}, bf16[32,3584]{1,0:T(8,128)(2,1)S(1)}, u32[]{:S(2)}, u32[]{:S(2)}) %collective-permute-start.10) | collective-permute-done | bytes 229408 | tf_op jit(solution)/shard_map/rs_fb/ppermute | solution.py:113
  69.5 3.3 %collective-permute-start.13 = (bf16[64,3584]{1,0:T(8,128)(2,1)S(1)}, bf16[64,3584]{1,0:T(8,128)(2,1)S(1)}, u32[]{:S(2)}, u32[]{:S(2)}) collective-permute-start(bf16[64,3584]{1,0:T(8,128)(2,1)S(1)} %pad_maximum_fusion.5), channel_id=1, source_target_pairs={{0,12},{1,13},{2,14},{3,15},{4,0},{5,1},{6,2},{7,3},{8,4},{9,5},{1... | collective-permute-start | bytes 1376264 | tf_op jit(solution)/shard_map/rs_al/ppermute | solution.py:113
  72.8 4.6 %collective-permute-done.9 = bf16[64,3584]{1,0:T(8,128)(2,1)S(1)} collective-permute-done((bf16[64,3584]{1,0:T(8,128)(2,1)S(1)}, bf16[64,3584]{1,0:T(8,128)(2,1)S(1)}, u32[]{:S(2)}, u32[]{:S(2)}) %collective-permute-start.9) | collective-permute-done | bytes 458784 | tf_op jit(solution)/shard_map/rs_xl/ppermute | solution.py:113
  77.4 2.4 %collective-permute-done.13 = bf16[64,3584]{1,0:T(8,128)(2,1)S(1)} collective-permute-done((bf16[64,3584]{1,0:T(8,128)(2,1)S(1)}, bf16[64,3584]{1,0:T(8,128)(2,1)S(1)}, u32[]{:S(2)}, u32[]{:S(2)}) %collective-permute-start.13) | collective-permute-done | bytes 458784 | tf_op jit(solution)/shard_map/rs_al/ppermute | solution.py:113
  79.8 3.4 %collective-permute-done.12 = bf16[64,3584]{1,0:T(8,128)(2,1)S(1)} collective-permute-done((bf16[64,3584]{1,0:T(8,128)(2,1)S(1)}, bf16[64,3584]{1,0:T(8,128)(2,1)S(1)}, u32[]{:S(2)}, u32[]{:S(2)}) %collective-permute-start.12) | collective-permute-done | bytes 458784 | tf_op jit(solution)/shard_map/rs_bl/ppermute | solution.py:113
  84.2 3.2 %collective-permute-start.16 = (bf16[128,3584]{1,0:T(8,128)(2,1)S(1)}, bf16[128,3584]{1,0:T(8,128)(2,1)}, u32[]{:S(2)}, u32[]{:S(2)}) collective-permute-start(bf16[128,3584]{1,0:T(8,128)(2,1)S(1)} %pad_maximum_fusion.2.refs_0_), channel_id=1, source_target_pairs={{0,12},{1,13},{2,14},{3,15},{4,0},{5,1},{6,2},{7,3},{8,4},{9,5},{1... | collective-permute-start | bytes 2752520 | tf_op jit(solution)/shard_map/ag_a/ppermute | solution.py:113
  88.5 5.6 %all-to-all-start.1 = ((bf16[8,128,512]{2,1,0:T(8,128)(2,1)}), bf16[8,128,512]{2,1,0:T(8,128)(2,1)S(1)}, u32[]{:S(2)}, u32[]{:S(2)}) async-start(bf16[8,128,512]{2,1,0:T(8,128)(2,1)} %broadcast_in_dim.18), calls=%async_computation.1 | async-start | bytes 2097152 | tf_op jit(solution)/shard_map/input_rows/all_to_all | solution.py:224
  94.1 14.9 %collective-permute-done.14.refs_8_ = bf16[128,3584]{1,0:T(8,128)(2,1)} collective-permute-done((bf16[128,3584]{1,0:T(8,128)(2,1)S(1)}, bf16[128,3584]{1,0:T(8,128)(2,1)}, u32[]{:S(2)}, u32[]{:S(2)}) %collective-permute-start.14) | collective-permute-done | bytes 917536 | tf_op jit(solution)/shard_map/ag_x/ppermute | solution.py:113
  109.0 1.8 slice.144
  111.1 1.8 slice.143
  112.9 1.7 collective-permute-start.18
  115.5 1.6 collective-permute-done.20
  118.3 4.0 %collective-permute-done.21 = f32[8,128]{1,0:T(8,128)S(1)} collective-permute-done((f32[8,128]{1,0:T(8,128)S(1)}, f32[8,128]{1,0:T(8,128)S(1)}, u32[]{:S(2)}, u32[]{:S(2)}) %collective-permute-start.21) | collective-permute-done | bytes 4128 | tf_op jit(solution)/shard_map/squares/ppermute | solution.py:113
  122.9 2.2 pad_maximum_fusion.3.refs_2_
  128.5 2.8 %collective-permute-done.30 = f32[8,128]{1,0:T(8,128)S(1)} collective-permute-done((f32[8,128]{1,0:T(8,128)S(1)}, f32[8,128]{1,0:T(8,128)S(1)}, u32[]{:S(2)}, u32[]{:S(2)}) %collective-permute-start.30) | collective-permute-done | bytes 4128 | tf_op jit(solution)/shard_map/squares/ppermute | solution.py:160
  131.9 2.7 %collective-permute-start.23 = (bf16[128,3584]{1,0:T(8,128)(2,1)}, bf16[128,3584]{1,0:T(8,128)(2,1)}, u32[]{:S(2)}, u32[]{:S(2)}) collective-permute-start(bf16[128,3584]{1,0:T(8,128)(2,1)} %collective-permute-done.14.refs_8_), channel_id=1, source_target_pairs={{0,12},{1,13},{2,14},{3,15},{4,0},{5,1},{6,2},{7,3},{8,4},{9,5},{1... | collective-permute-start | bytes 2752520 | tf_op jit(solution)/shard_map/ag_xa/ppermute | solution.py:113
  136.6 1.3 collective-permute-done.28.refs_9_.refs_12_
  137.9 9.9 %input_grads.2 = f32[640,512]{1,0:T(8,128)} custom-call(bf16[128,3584]{1,0:T(8,128)(2,1)} %copy-done, bf16[128,3584]{1,0:T(8,128)(2,1)} %collective-permute-done.16.refs_1_, bf16[128,3584]{1,0:T(8,128)(2,1)} %pad_maximum_fusion.3.refs_2_, bf16[128,3584]{1,0:T(8,128)(2,1)} %collective-permute-done.15.refs_3_, ...), custom_call_target="tpu_custom_call" | custom-call | tf_op jit(solution)/shard_map/input_grads/pallas_call | solution.py:19
  147.8 5.7 %down_grads.2 = bf16[1792,512]{1,0:T(8,128)(2,1)} custom-call(bf16[512,1792]{1,0:T(8,128)(2,1)} %bitcast.9.left, bf16[512,1792]{1,0:T(8,128)(2,1)} %collective-permute-done.29.left_other, bf16[1024,512]{1,0:T(8,128)(2,1)} %bitcast.95), custom_call_target="tpu_custom_call" | custom-call | tf_op jit(solution)/shard_map/down_grads/pallas_call | solution.py:19
  154.0 3.0 %collective-permute-done.24.refs_1_.refs_10_ = bf16[128,3584]{1,0:T(8,128)(2,1)} collective-permute-done((bf16[128,3584]{1,0:T(8,128)(2,1)}, bf16[128,3584]{1,0:T(8,128)(2,1)}, u32[]{:S(2)}, u32[]{:S(2)}) %collective-permute-start.24) | collective-permute-done | bytes 917536 | tf_op jit(solution)/shard_map/ag_xf/ppermute | solution.py:113
  157.5 1.4 broadcast_in_dim.46
  158.9 7.9 %all-to-all-start.2 = ((bf16[8,64,1792]{2,1,0:T(8,128)(2,1)}), bf16[8,64,1792]{2,1,0:T(8,128)(2,1)S(1)}, u32[]{:S(2)}, u32[]{:S(2)}) async-start(bf16[8,64,1792]{2,1,0:T(8,128)(2,1)} %broadcast_in_dim.46), calls=%async_computation.2 | async-start | bytes 3670016 | tf_op jit(solution)/shard_map/hid_b/all_to_all | solution.py:170
  168.3 7.4 %input_grads.3 = f32[384,512]{1,0:T(8,128)} custom-call(bf16[128,3584]{1,0:T(8,128)(2,1)} %collective-permute-done.23.refs_0_.refs_9_, bf16[128,3584]{1,0:T(8,128)(2,1)} %collective-permute-done.24.refs_1_.refs_10_, bf16[128,3584]{1,0:T(8,128)(2,1)} %collective-permute-done.22.refs_2_.refs_11_, bf16[128,3584]{1,0:T(8,128)(2,1)} %collective-permute-done.31.refs_3_.refs_13_, ...), custom_call_target="tpu_custom_call" | custom-call | tf_op jit(solution)/shard_map/input_grads/pallas_call | solution.py:19
  177.5 2.6 %collective-permute-start.37 = (bf16[2,2,64,512]{3,2,1,0:T(8,128)(2,1)S(1)}, bf16[2,2,64,512]{3,2,1,0:T(8,128)(2,1)S(1)}, u32[]{:S(2)}, u32[]{:S(2)}) collective-permute-start(bf16[2,2,64,512]{3,2,1,0:T(8,128)(2,1)S(1)} %get-tuple-element.123), channel_id=1, source_target_pairs={{0,96},{16,112},{32,0},{48,16},{64,32},{80,48},{96,64},{112,80},{1... | collective-permute-start | bytes 786440 | tf_op jit(solution)/shard_map/dn_y/ppermute | solution.py:122
  180.1 1.7 collective-permute-start.36
  181.7 12.7 %gate_up_grads.1 = (bf16[512,3584]{1,0:T(8,128)(2,1)}, bf16[512,3584]{1,0:T(8,128)(2,1)}) custom-call(bf16[512,1024]{1,0:T(8,128)(2,1)} %multiply_convert_fusion.left, bf16[128,3584]{1,0:T(8,128)(2,1)} %copy-done, bf16[128,3584]{1,0:T(8,128)(2,1)} %collective-permute-done.16.refs_1_, bf16[128,3584]{1,0:T(8,128)(2,1)} %pad_maximum_fusion.3.refs_2_, ...), custom_call_target="tpu_custom_call" | custom-call | tf_op jit(solution)/shard_map/gate_up_grads/pallas_call | solution.py:19
  196.3 5.0 %collective-permute-done.38 = bf16[2,64,512]{2,1,0:T(8,128)(2,1)S(1)} collective-permute-done((bf16[2,64,512]{2,1,0:T(8,128)(2,1)S(1)}, bf16[2,64,512]{2,1,0:T(8,128)(2,1)S(1)}, u32[]{:S(2)}, u32[]{:S(2)}) %collective-permute-start.38) | collective-permute-done | bytes 131104 | tf_op jit(solution)/shard_map/dn_xl/ppermute | solution.py:122
  203.6 1.6 collective-permute-done.41
  206.5 5.0 %collective-permute-done.42 = f32[1,128]{1,0:T(1,128)S(1)} collective-permute-done((f32[1,128]{1,0:T(1,128)S(1)}, f32[1,128]{1,0:T(1,128)S(1)}, u32[]{:S(2)}, u32[]{:S(2)}) %collective-permute-start.42) | collective-permute-done | bytes 544 | tf_op jit(solution)/shard_map/proj/ppermute | solution.py:113
  211.5 2.9 %collective-permute-start.45 = (f32[1,512]{1,0:T(1,128)S(1)}, f32[1,512]{1,0:T(1,128)S(1)}, u32[]{:S(2)}, u32[]{:S(2)}) collective-permute-start(f32[1,512]{1,0:T(1,128)S(1)} %add.236), channel_id=1, source_target_pairs={{0,64},{16,80},{32,96},{48,112},{64,0},{80,16},{96,32},{112,48},{1... | collective-permute-start | bytes 6152 | tf_op jit(solution)/shard_map/gain/ppermute | solution.py:122
  214.5 1.5 collective-permute-start.44
  216.0 5.7 %down_grads.3 = bf16[1792,512]{1,0:T(8,128)(2,1)} custom-call(bf16[512,1792]{1,0:T(8,128)(2,1)} %bitcast.98, bf16[512,1792]{1,0:T(8,128)(2,1)} %copy-done.6, bf16[1024,512]{1,0:T(8,128)(2,1)} %bitcast.96), custom_call_target="tpu_custom_call" | custom-call | tf_op jit(solution)/shard_map/down_grads/pallas_call | solution.py:19
  222.2 2.7 %collective-permute-start.46 = (f32[1,128]{1,0:T(1,128)S(1)}, f32[1,128]{1,0:T(1,128)S(1)}, u32[]{:S(2)}, u32[]{:S(2)}) collective-permute-start(f32[1,128]{1,0:T(1,128)S(1)} %add.237), channel_id=1, source_target_pairs={{0,8},{1,9},{2,10},{3,11},{4,12},{5,13},{6,14},{7,15},{8,0},{9,1},... | collective-permute-start | bytes 1544 | tf_op jit(solution)/shard_map/proj/ppermute | solution.py:113
  224.9 3.6 %pad_maximum_fusion = bf16[3584,512]{1,0:T(8,128)(2,1)} fusion(bf16[1792,512]{1,0:T(8,128)(2,1)} %down_grads.3, bf16[1792,512]{1,0:T(8,128)(2,1)S(1)} %copy-done.1), kind=kLoop, calls=%fused_computation | loop fusion | flops 7340032 | bytes 7340032 | tf_op jit(solution)/shard_map/concatenate | solution.py:314
  (173 shorter events, 35.6 us)
Async XLA Ops:
  0.6 24.2 %collective-permute-start.4 = (bf16[3584,512]{1,0:T(8,128)(2,1)}, bf16[3584,512]{1,0:T(8,128)(2,1)}, u32[]{:S(2)}, u32[]{:S(2)}) collective-permute-start(bf16[3584,512]{1,0:T(8,128)(2,1)} %w.3), channel_id=1, source_target_pairs={{0,1},{1,0},{2,3},{3,2},{4,5},{5,4},{6,7},{7,6},{8,9},{9,8},{10,11... | collective-permute-start | bytes 11010056 | tf_op jit(solution)/shard_map/w_down/ppermute | solution.py:113
  0.7 6.1 %collective-permute-start = (bf16[128,512]{1,0:T(8,128)(2,1)}, bf16[128,512]{1,0:T(8,128)(2,1)S(1)}, u32[]{:S(2)}, u32[]{:S(2)}) collective-permute-start(bf16[128,512]{1,0:T(8,128)(2,1)} %param.9), channel_id=1, source_target_pairs={{0,16},{16,0},{32,48},{48,32},{64,80},{80,64},{96,112},{112,96},{1... | collective-permute-start | bytes 393224 | tf_op jit(solution)/shard_map/out_xl/ppermute | solution.py:122
  7.0 14.5 %collective-permute-start.1 = (bf16[2,2,1,64,512]{4,3,1,0,2:T(8,128)(2,1)S(1)}, bf16[2,2,1,64,512]{4,3,1,0,2:T(8,128)(2,1)S(1)}, u32[]{:S(2)}, u32[]{:S(2)}) collective-permute-start(bf16[2,2,1,64,512]{4,3,1,0,2:T(8,128)(2,1)S(1)} %fusion.11), channel_id=1, source_target_pairs={{0,96},{16,112},{32,0},{48,16},{64,32},{80,48},{96,64},{112,80},{1... | collective-permute-start | bytes 786440 | tf_op jit(solution)/shard_map/out_y/ppermute | solution.py:122
  10.1 11.4 %collective-permute-start.2 = (bf16[2,2,1,64,512]{4,3,1,0,2:T(8,128)(2,1)S(1)}, bf16[2,2,1,64,512]{4,3,1,0,2:T(8,128)(2,1)S(1)}, u32[]{:S(2)}, u32[]{:S(2)}) collective-permute-start(bf16[2,2,1,64,512]{4,3,1,0,2:T(8,128)(2,1)S(1)} %fusion.11), channel_id=1, source_target_pairs={{0,64},{16,80},{32,96},{48,112},{64,0},{80,16},{96,32},{112,48},{1... | collective-permute-start | bytes 786440 | tf_op jit(solution)/shard_map/out_y/ppermute | solution.py:122
  10.7 14.1 %collective-permute-start.3 = (bf16[2,2,1,64,512]{4,3,1,0,2:T(8,128)(2,1)S(1)}, bf16[2,2,1,64,512]{4,3,1,0,2:T(8,128)(2,1)S(1)}, u32[]{:S(2)}, u32[]{:S(2)}) collective-permute-start(bf16[2,2,1,64,512]{4,3,1,0,2:T(8,128)(2,1)S(1)} %fusion.11), channel_id=1, source_target_pairs={{0,32},{16,48},{32,64},{48,80},{64,96},{80,112},{96,0},{112,16},{1... | collective-permute-start | bytes 786440 | tf_op jit(solution)/shard_map/out_y/ppermute | solution.py:122
  13.0 30.3 %all-to-all-start = ((bf16[8,64,1792]{2,1,0:T(8,128)(2,1)}), bf16[8,64,1792]{2,1,0:T(8,128)(2,1)}, u32[]{:S(2)}, u32[]{:S(2)}) async-start(bf16[8,64,1792]{2,1,0:T(8,128)(2,1)} %broadcast_in_dim.17), calls=%async_computation | async-start | bytes 3670016 | tf_op jit(solution)/shard_map/hid_a/all_to_all | solution.py:170
  43.3 11.8 %collective-permute-start.8 = (bf16[64,3584]{1,0:T(8,128)(2,1)S(1)}, bf16[64,3584]{1,0:T(8,128)(2,1)}, u32[]{:S(2)}, u32[]{:S(2)}) collective-permute-start(bf16[64,3584]{1,0:T(8,128)(2,1)S(1)} %get-tuple-element.84), channel_id=1, source_target_pairs={{0,12},{1,13},{2,14},{3,15},{4,0},{5,1},{6,2},{7,3},{8,4},{9,5},{1... | collective-permute-start | bytes 1376264 | tf_op jit(solution)/shard_map/rs_a/ppermute | solution.py:113
  44.5 13.5 %collective-permute-start.7 = (bf16[64,3584]{1,0:T(8,128)(2,1)S(1)}, bf16[64,3584]{1,0:T(8,128)(2,1)}, u32[]{:S(2)}, u32[]{:S(2)}) collective-permute-start(bf16[64,3584]{1,0:T(8,128)(2,1)S(1)} %get-tuple-element.83), channel_id=1, source_target_pairs={{0,4},{1,5},{2,6},{3,7},{4,8},{5,9},{6,10},{7,11},{8,12},{9,13},{1... | collective-permute-start | bytes 1376264 | tf_op jit(solution)/shard_map/rs_b/ppermute | solution.py:113
  46.8 12.8 %collective-permute-start.6 = (bf16[64,3584]{1,0:T(8,128)(2,1)S(1)}, bf16[64,3584]{1,0:T(8,128)(2,1)S(1)}, u32[]{:S(2)}, u32[]{:S(2)}) collective-permute-start(bf16[64,3584]{1,0:T(8,128)(2,1)S(1)} %get-tuple-element.81), channel_id=1, source_target_pairs={{0,2},{1,3},{2,0},{3,1},{4,6},{5,7},{6,4},{7,5},{8,10},{9,11},{10,... | collective-permute-start | bytes 1376264 | tf_op jit(solution)/shard_map/rs_x/ppermute | solution.py:113
  61.9 7.3 %collective-permute-start.10 = (bf16[32,3584]{1,0:T(8,128)(2,1)S(1)}, bf16[32,3584]{1,0:T(8,128)(2,1)S(1)}, u32[]{:S(2)}, u32[]{:S(2)}) collective-permute-start(bf16[32,3584]{1,0:T(8,128)(2,1)S(1)} %get-tuple-element.170), channel_id=1, source_target_pairs={{0,4},{1,5},{2,6},{3,7},{4,8},{5,9},{6,10},{7,11},{8,12},{9,13},{1... | collective-permute-start | bytes 688136 | tf_op jit(solution)/shard_map/rs_fb/ppermute | solution.py:113
  63.2 6.2 %collective-permute-start.11 = (bf16[32,3584]{1,0:T(8,128)(2,1)S(1)}, bf16[32,3584]{1,0:T(8,128)(2,1)S(1)}, u32[]{:S(2)}, u32[]{:S(2)}) collective-permute-start(bf16[32,3584]{1,0:T(8,128)(2,1)S(1)} %get-tuple-element.169), channel_id=1, source_target_pairs={{0,12},{1,13},{2,14},{3,15},{4,0},{5,1},{6,2},{7,3},{8,4},{9,5},{1... | collective-permute-start | bytes 688136 | tf_op jit(solution)/shard_map/rs_fa/ppermute | solution.py:113
  65.4 12.0 %collective-permute-start.9 = (bf16[64,3584]{1,0:T(8,128)(2,1)S(1)}, bf16[64,3584]{1,0:T(8,128)(2,1)S(1)}, u32[]{:S(2)}, u32[]{:S(2)}) collective-permute-start(bf16[64,3584]{1,0:T(8,128)(2,1)S(1)} %add_convert_fusion), channel_id=1, source_target_pairs={{0,2},{1,3},{2,0},{3,1},{4,6},{5,7},{6,4},{7,5},{8,10},{9,11},{10,... | collective-permute-start | bytes 1376264 | tf_op jit(solution)/shard_map/rs_xl/ppermute | solution.py:113
  69.5 10.4 %collective-permute-start.13 = (bf16[64,3584]{1,0:T(8,128)(2,1)S(1)}, bf16[64,3584]{1,0:T(8,128)(2,1)S(1)}, u32[]{:S(2)}, u32[]{:S(2)}) collective-permute-start(bf16[64,3584]{1,0:T(8,128)(2,1)S(1)} %pad_maximum_fusion.5), channel_id=1, source_target_pairs={{0,12},{1,13},{2,14},{3,15},{4,0},{5,1},{6,2},{7,3},{8,4},{9,5},{1... | collective-permute-start | bytes 1376264 | tf_op jit(solution)/shard_map/rs_al/ppermute | solution.py:113
  72.8 10.5 %collective-permute-start.12 = (bf16[64,3584]{1,0:T(8,128)(2,1)S(1)}, bf16[64,3584]{1,0:T(8,128)(2,1)S(1)}, u32[]{:S(2)}, u32[]{:S(2)}) collective-permute-start(bf16[64,3584]{1,0:T(8,128)(2,1)S(1)} %pad_maximum_fusion.4), channel_id=1, source_target_pairs={{0,4},{1,5},{2,6},{3,7},{4,8},{5,9},{6,10},{7,11},{8,12},{9,13},{1... | collective-permute-start | bytes 1376264 | tf_op jit(solution)/shard_map/rs_bl/ppermute | solution.py:113
  84.0 25.0 %collective-permute-start.14 = (bf16[128,3584]{1,0:T(8,128)(2,1)S(1)}, bf16[128,3584]{1,0:T(8,128)(2,1)}, u32[]{:S(2)}, u32[]{:S(2)}) collective-permute-start(bf16[128,3584]{1,0:T(8,128)(2,1)S(1)} %pad_maximum_fusion.2.refs_0_), channel_id=1, source_target_pairs={{0,2},{1,3},{2,0},{3,1},{4,6},{5,7},{6,4},{7,5},{8,10},{9,11},{10,... | collective-permute-start | bytes 2752520 | tf_op jit(solution)/shard_map/ag_x/ppermute | solution.py:113
  84.1 24.9 %collective-permute-start.15 = (bf16[128,3584]{1,0:T(8,128)(2,1)S(1)}, bf16[128,3584]{1,0:T(8,128)(2,1)}, u32[]{:S(2)}, u32[]{:S(2)}) collective-permute-start(bf16[128,3584]{1,0:T(8,128)(2,1)S(1)} %pad_maximum_fusion.2.refs_0_), channel_id=1, source_target_pairs={{0,4},{1,5},{2,6},{3,7},{4,8},{5,9},{6,10},{7,11},{8,12},{9,13},{1... | collective-permute-start | bytes 2752520 | tf_op jit(solution)/shard_map/ag_b/ppermute | solution.py:113
  84.2 24.8 %collective-permute-start.16 = (bf16[128,3584]{1,0:T(8,128)(2,1)S(1)}, bf16[128,3584]{1,0:T(8,128)(2,1)}, u32[]{:S(2)}, u32[]{:S(2)}) collective-permute-start(bf16[128,3584]{1,0:T(8,128)(2,1)S(1)} %pad_maximum_fusion.2.refs_0_), channel_id=1, source_target_pairs={{0,12},{1,13},{2,14},{3,15},{4,0},{5,1},{6,2},{7,3},{8,4},{9,5},{1... | collective-permute-start | bytes 2752520 | tf_op jit(solution)/shard_map/ag_a/ppermute | solution.py:113
  88.5 26.2 %all-to-all-start.1 = ((bf16[8,128,512]{2,1,0:T(8,128)(2,1)}), bf16[8,128,512]{2,1,0:T(8,128)(2,1)S(1)}, u32[]{:S(2)}, u32[]{:S(2)}) async-start(bf16[8,128,512]{2,1,0:T(8,128)(2,1)} %broadcast_in_dim.18), calls=%async_computation.1 | async-start | bytes 2097152 | tf_op jit(solution)/shard_map/input_rows/all_to_all | solution.py:224
  110.8 11.4 %collective-permute-start.19 = (bf16[64,3584]{1,0:T(8,128)(2,1)}, bf16[64,3584]{1,0:T(8,128)(2,1)}, u32[]{:S(2)}, u32[]{:S(2)}) collective-permute-start(bf16[64,3584]{1,0:T(8,128)(2,1)} %slice.144), channel_id=1, source_target_pairs={{0,12},{1,13},{2,14},{3,15},{4,0},{5,1},{6,2},{7,3},{8,4},{9,5},{1... | collective-permute-start | bytes 1376264 | tf_op jit(solution)/shard_map/ag_fa/ppermute | solution.py:113
  112.9 10.0 %collective-permute-start.18 = (bf16[64,3584]{1,0:T(8,128)(2,1)}, bf16[64,3584]{1,0:T(8,128)(2,1)}, u32[]{:S(2)}, u32[]{:S(2)}) collective-permute-start(bf16[64,3584]{1,0:T(8,128)(2,1)} %slice.143), channel_id=1, source_target_pairs={{0,4},{1,5},{2,6},{3,7},{4,8},{5,9},{6,10},{7,11},{8,12},{9,13},{1... | collective-permute-start | bytes 1376264 | tf_op jit(solution)/shard_map/ag_fb/ppermute | solution.py:113
  114.7 10.4 %collective-permute-start.17 = (bf16[128,3584]{1,0:T(8,128)(2,1)S(1)}, bf16[128,3584]{1,0:T(8,128)(2,1)}, u32[]{:S(2)}, u32[]{:S(2)}) collective-permute-start(bf16[128,3584]{1,0:T(8,128)(2,1)S(1)} %pad_maximum_fusion.2.refs_0_), channel_id=1, source_target_pairs={{0,1},{1,0},{2,3},{3,2},{4,5},{5,4},{6,7},{7,6},{8,9},{9,8},{10,11... | collective-permute-start | bytes 2752520 | tf_op jit(solution)/shard_map/ag_core/ppermute | solution.py:113
  114.9 2.2 collective-permute-start.20
  117.1 5.1 %collective-permute-start.21 = (f32[8,128]{1,0:T(8,128)S(1)}, f32[8,128]{1,0:T(8,128)S(1)}, u32[]{:S(2)}, u32[]{:S(2)}) collective-permute-start(f32[8,128]{1,0:T(8,128)S(1)} %add.210), channel_id=1, source_target_pairs={{0,2},{1,3},{2,0},{3,1},{4,6},{5,7},{6,4},{7,5},{8,10},{9,11},{10,... | collective-permute-start | bytes 12296 | tf_op jit(solution)/shard_map/squares/ppermute | solution.py:113
  125.1 6.8 %collective-permute-start.25 = (bf16[128,3584]{1,0:T(8,128)(2,1)}, bf16[128,3584]{1,0:T(8,128)(2,1)S(1)}, u32[]{:S(2)}, u32[]{:S(2)}) collective-permute-start(bf16[128,3584]{1,0:T(8,128)(2,1)} %collective-permute-done.16.refs_1_), channel_id=1, source_target_pairs={{0,1},{1,0},{2,3},{3,2},{4,5},{5,4},{6,7},{7,6},{8,9},{9,8},{10,11... | collective-permute-start | bytes 2752520 | tf_op jit(solution)/shard_map/ag_core/ppermute | solution.py:113
  125.1 9.5 %collective-permute-start.26 = (bf16[128,3584]{1,0:T(8,128)(2,1)}, bf16[128,3584]{1,0:T(8,128)(2,1)S(1)}, u32[]{:S(2)}, u32[]{:S(2)}) collective-permute-start(bf16[128,3584]{1,0:T(8,128)(2,1)} %pad_maximum_fusion.3.refs_2_), channel_id=1, source_target_pairs={{0,1},{1,0},{2,3},{3,2},{4,5},{5,4},{6,7},{7,6},{8,9},{9,8},{10,11... | collective-permute-start | bytes 2752520 | tf_op jit(solution)/shard_map/ag_core/ppermute | solution.py:113
  125.6 9.5 %collective-permute-start.27 = (bf16[128,3584]{1,0:T(8,128)(2,1)}, bf16[128,3584]{1,0:T(8,128)(2,1)S(1)}, u32[]{:S(2)}, u32[]{:S(2)}) collective-permute-start(bf16[128,3584]{1,0:T(8,128)(2,1)} %collective-permute-done.15.refs_3_), channel_id=1, source_target_pairs={{0,1},{1,0},{2,3},{3,2},{4,5},{5,4},{6,7},{7,6},{8,9},{9,8},{10,11... | collective-permute-start | bytes 2752520 | tf_op jit(solution)/shard_map/ag_core/ppermute | solution.py:113
  125.6 22.2 %collective-permute-start.29 = (bf16[512,1792]{1,0:T(8,128)(2,1)}, bf16[512,1792]{1,0:T(8,128)(2,1)}, u32[]{:S(2)}, u32[]{:S(2)}) collective-permute-start(bf16[512,1792]{1,0:T(8,128)(2,1)} %bitcast.9.left), channel_id=1, source_target_pairs={{0,1},{1,0},{2,3},{3,2},{4,5},{5,4},{6,7},{7,6},{8,9},{9,8},{10,11... | collective-permute-start | bytes 5505032 | tf_op jit(solution)/shard_map/hid_core/ppermute | solution.py:113
  127.7 3.6 %collective-permute-start.30 = (f32[8,128]{1,0:T(8,128)S(1)}, f32[8,128]{1,0:T(8,128)S(1)}, u32[]{:S(2)}, u32[]{:S(2)}) collective-permute-start(f32[8,128]{1,0:T(8,128)S(1)} %add.211), channel_id=1, source_target_pairs={{0,4},{1,5},{2,6},{3,7},{4,0},{5,1},{6,2},{7,3},{8,12},{9,13},{10,... | collective-permute-start | bytes 12296 | tf_op jit(solution)/shard_map/squares/ppermute | solution.py:160
  131.4 22.6 %collective-permute-start.22 = (bf16[128,3584]{1,0:T(8,128)(2,1)}, bf16[128,3584]{1,0:T(8,128)(2,1)}, u32[]{:S(2)}, u32[]{:S(2)}) collective-permute-start(bf16[128,3584]{1,0:T(8,128)(2,1)} %collective-permute-done.14.refs_8_), channel_id=1, source_target_pairs={{0,4},{1,5},{2,6},{3,7},{4,8},{5,9},{6,10},{7,11},{8,12},{9,13},{1... | collective-permute-start | bytes 2752520 | tf_op jit(solution)/shard_map/ag_xb/ppermute | solution.py:113
  131.9 22.1 %collective-permute-start.23 = (bf16[128,3584]{1,0:T(8,128)(2,1)}, bf16[128,3584]{1,0:T(8,128)(2,1)}, u32[]{:S(2)}, u32[]{:S(2)}) collective-permute-start(bf16[128,3584]{1,0:T(8,128)(2,1)} %collective-permute-done.14.refs_8_), channel_id=1, source_target_pairs={{0,12},{1,13},{2,14},{3,15},{4,0},{5,1},{6,2},{7,3},{8,4},{9,5},{1... | collective-permute-start | bytes 2752520 | tf_op jit(solution)/shard_map/ag_xa/ppermute | solution.py:113
  134.6 22.4 %collective-permute-start.24 = (bf16[128,3584]{1,0:T(8,128)(2,1)}, bf16[128,3584]{1,0:T(8,128)(2,1)}, u32[]{:S(2)}, u32[]{:S(2)}) collective-permute-start(bf16[128,3584]{1,0:T(8,128)(2,1)} %pad_maximum_fusion.3.refs_2_), channel_id=1, source_target_pairs={{0,2},{1,3},{2,0},{3,1},{4,6},{5,7},{6,4},{7,5},{8,10},{9,11},{10,... | collective-permute-start | bytes 2752520 | tf_op jit(solution)/shard_map/ag_xf/ppermute | solution.py:113
  135.1 2.8 %collective-permute-start.28 = (bf16[128,3584]{1,0:T(8,128)(2,1)}, bf16[128,3584]{1,0:T(8,128)(2,1)}, u32[]{:S(2)}, u32[]{:S(2)}) collective-permute-start(bf16[128,3584]{1,0:T(8,128)(2,1)} %collective-permute-done.14.refs_8_), channel_id=1, source_target_pairs={{0,1},{1,0},{2,3},{3,2},{4,5},{5,4},{6,7},{7,6},{8,9},{9,8},{10,11... | collective-permute-start | bytes 2752520 | tf_op jit(solution)/shard_map/ag_core/ppermute | solution.py:113
  157.0 9.8 %collective-permute-start.34 = (f32[8,128]{1,0:T(8,128)S(1)}, f32[8,128]{1,0:T(8,128)S(1)}, u32[]{:S(2)}, u32[]{:S(2)}) collective-permute-start(f32[8,128]{1,0:T(8,128)S(1)} %add.222), channel_id=1, source_target_pairs={{0,8},{1,9},{2,10},{3,11},{4,12},{5,13},{6,14},{7,15},{8,0},{9,1},... | collective-permute-start | bytes 12296 | tf_op jit(solution)/shard_map/squares/ppermute | solution.py:113
  157.0 11.3 %collective-permute-start.31 = (bf16[128,3584]{1,0:T(8,128)(2,1)}, bf16[128,3584]{1,0:T(8,128)(2,1)}, u32[]{:S(2)}, u32[]{:S(2)}) collective-permute-start(bf16[128,3584]{1,0:T(8,128)(2,1)} %collective-permute-done.23.refs_0_.refs_9_), channel_id=1, source_target_pairs={{0,1},{1,0},{2,3},{3,2},{4,5},{5,4},{6,7},{7,6},{8,9},{9,8},{10,11... | collective-permute-start | bytes 2752520 | tf_op jit(solution)/shard_map/ag_core/ppermute | solution.py:113
  157.0 11.3 %collective-permute-start.32 = (bf16[128,3584]{1,0:T(8,128)(2,1)}, bf16[128,3584]{1,0:T(8,128)(2,1)}, u32[]{:S(2)}, u32[]{:S(2)}) collective-permute-start(bf16[128,3584]{1,0:T(8,128)(2,1)} %collective-permute-done.24.refs_1_.refs_10_), channel_id=1, source_target_pairs={{0,1},{1,0},{2,3},{3,2},{4,5},{5,4},{6,7},{7,6},{8,9},{9,8},{10,11... | collective-permute-start | bytes 2752520 | tf_op jit(solution)/shard_map/ag_core/ppermute | solution.py:113
  157.5 10.8 %collective-permute-start.33 = (bf16[128,3584]{1,0:T(8,128)(2,1)}, bf16[128,3584]{1,0:T(8,128)(2,1)}, u32[]{:S(2)}, u32[]{:S(2)}) collective-permute-start(bf16[128,3584]{1,0:T(8,128)(2,1)} %collective-permute-done.22.refs_2_.refs_11_), channel_id=1, source_target_pairs={{0,1},{1,0},{2,3},{3,2},{4,5},{5,4},{6,7},{7,6},{8,9},{9,8},{10,11... | collective-permute-start | bytes 2752520 | tf_op jit(solution)/shard_map/ag_core/ppermute | solution.py:113
  158.9 36.4 %all-to-all-start.2 = ((bf16[8,64,1792]{2,1,0:T(8,128)(2,1)}), bf16[8,64,1792]{2,1,0:T(8,128)(2,1)S(1)}, u32[]{:S(2)}, u32[]{:S(2)}) async-start(bf16[8,64,1792]{2,1,0:T(8,128)(2,1)} %broadcast_in_dim.46), calls=%async_computation.2 | async-start | bytes 3670016 | tf_op jit(solution)/shard_map/hid_b/all_to_all | solution.py:170
  177.5 17.0 %collective-permute-start.37 = (bf16[2,2,64,512]{3,2,1,0:T(8,128)(2,1)S(1)}, bf16[2,2,64,512]{3,2,1,0:T(8,128)(2,1)S(1)}, u32[]{:S(2)}, u32[]{:S(2)}) collective-permute-start(bf16[2,2,64,512]{3,2,1,0:T(8,128)(2,1)S(1)} %get-tuple-element.123), channel_id=1, source_target_pairs={{0,96},{16,112},{32,0},{48,16},{64,32},{80,48},{96,64},{112,80},{1... | collective-permute-start | bytes 786440 | tf_op jit(solution)/shard_map/dn_y/ppermute | solution.py:122
  180.1 14.4 %collective-permute-start.36 = (bf16[2,2,64,512]{3,2,1,0:T(8,128)(2,1)S(1)}, bf16[2,2,64,512]{3,2,1,0:T(8,128)(2,1)S(1)}, u32[]{:S(2)}, u32[]{:S(2)}) collective-permute-start(bf16[2,2,64,512]{3,2,1,0:T(8,128)(2,1)S(1)} %get-tuple-element.122), channel_id=1, source_target_pairs={{0,64},{16,80},{32,96},{48,112},{64,0},{80,16},{96,32},{112,48},{1... | collective-permute-start | bytes 786440 | tf_op jit(solution)/shard_map/dn_y/ppermute | solution.py:122
  181.7 13.3 %collective-permute-start.35 = (bf16[2,2,64,512]{3,2,1,0:T(8,128)(2,1)S(1)}, bf16[2,2,64,512]{3,2,1,0:T(8,128)(2,1)S(1)}, u32[]{:S(2)}, u32[]{:S(2)}) collective-permute-start(bf16[2,2,64,512]{3,2,1,0:T(8,128)(2,1)S(1)} %get-tuple-element.121), channel_id=1, source_target_pairs={{0,32},{16,48},{32,64},{48,80},{64,96},{80,112},{96,0},{112,16},{1... | collective-permute-start | bytes 786440 | tf_op jit(solution)/shard_map/dn_y/ppermute | solution.py:122
  195.3 6.2 %collective-permute-start.39 = (bf16[512,1792]{1,0:T(8,128)(2,1)S(1)}, bf16[512,1792]{1,0:T(8,128)(2,1)S(1)}, u32[]{:S(2)}, u32[]{:S(2)}) collective-permute-start(bf16[512,1792]{1,0:T(8,128)(2,1)S(1)} %bitcast.97), channel_id=1, source_target_pairs={{0,1},{1,0},{2,3},{3,2},{4,5},{5,4},{6,7},{7,6},{8,9},{9,8},{10,11... | collective-permute-start | bytes 5505032 | tf_op jit(solution)/shard_map/hid_core/ppermute | solution.py:113
  195.4 5.9 %collective-permute-start.38 = (bf16[2,64,512]{2,1,0:T(8,128)(2,1)S(1)}, bf16[2,64,512]{2,1,0:T(8,128)(2,1)S(1)}, u32[]{:S(2)}, u32[]{:S(2)}) collective-permute-start(bf16[2,64,512]{2,1,0:T(8,128)(2,1)S(1)} %fusion.30), channel_id=1, source_target_pairs={{0,16},{16,0},{32,48},{48,32},{64,80},{80,64},{96,112},{112,96},{1... | collective-permute-start | bytes 393224 | tf_op jit(solution)/shard_map/dn_xl/ppermute | solution.py:122
  201.5 3.7 %collective-permute-start.41 = (f32[1,512]{1,0:T(1,128)S(1)}, f32[1,512]{1,0:T(1,128)S(1)}, u32[]{:S(2)}, u32[]{:S(2)}) collective-permute-start(f32[1,512]{1,0:T(1,128)S(1)} %bitcast.116), channel_id=1, source_target_pairs={{0,16},{16,0},{32,48},{48,32},{64,80},{80,64},{96,112},{112,96},{1... | collective-permute-start | bytes 6152 | tf_op jit(solution)/shard_map/gain/ppermute | solution.py:122
  205.2 6.3 %collective-permute-start.43 = (f32[1,512]{1,0:T(1,128)S(1)}, f32[1,512]{1,0:T(1,128)S(1)}, u32[]{:S(2)}, u32[]{:S(2)}) collective-permute-start(f32[1,512]{1,0:T(1,128)S(1)} %add.234), channel_id=1, source_target_pairs={{0,32},{16,48},{32,0},{48,16},{64,96},{80,112},{96,64},{112,80},{1... | collective-permute-start | bytes 6152 | tf_op jit(solution)/shard_map/gain/ppermute | solution.py:164
  206.5 5.0 %collective-permute-start.42 = (f32[1,128]{1,0:T(1,128)S(1)}, f32[1,128]{1,0:T(1,128)S(1)}, u32[]{:S(2)}, u32[]{:S(2)}) collective-permute-start(f32[1,128]{1,0:T(1,128)S(1)} %add.233), channel_id=1, source_target_pairs={{0,2},{1,3},{2,0},{3,1},{4,6},{5,7},{6,4},{7,5},{8,10},{9,11},{10,... | collective-permute-start | bytes 1544 | tf_op jit(solution)/shard_map/proj/ppermute | solution.py:113
  211.5 10.1 %collective-permute-start.45 = (f32[1,512]{1,0:T(1,128)S(1)}, f32[1,512]{1,0:T(1,128)S(1)}, u32[]{:S(2)}, u32[]{:S(2)}) collective-permute-start(f32[1,512]{1,0:T(1,128)S(1)} %add.236), channel_id=1, source_target_pairs={{0,64},{16,80},{32,96},{48,112},{64,0},{80,16},{96,32},{112,48},{1... | collective-permute-start | bytes 6152 | tf_op jit(solution)/shard_map/gain/ppermute | solution.py:122
  214.5 7.1 %collective-permute-start.44 = (f32[1,128]{1,0:T(1,128)S(1)}, f32[1,128]{1,0:T(1,128)S(1)}, u32[]{:S(2)}, u32[]{:S(2)}) collective-permute-start(f32[1,128]{1,0:T(1,128)S(1)} %add.235), channel_id=1, source_target_pairs={{0,4},{1,5},{2,6},{3,7},{4,0},{5,1},{6,2},{7,3},{8,12},{9,13},{10,... | collective-permute-start | bytes 1544 | tf_op jit(solution)/shard_map/proj/ppermute | solution.py:160
  222.2 6.3 %collective-permute-start.46 = (f32[1,128]{1,0:T(1,128)S(1)}, f32[1,128]{1,0:T(1,128)S(1)}, u32[]{:S(2)}, u32[]{:S(2)}) collective-permute-start(f32[1,128]{1,0:T(1,128)S(1)} %add.237), channel_id=1, source_target_pairs={{0,8},{1,9},{2,10},{3,11},{4,12},{5,13},{6,14},{7,15},{8,0},{9,1},... | collective-permute-start | bytes 1544 | tf_op jit(solution)/shard_map/proj/ppermute | solution.py:113
  (19 other events, 188.4 us)

commit v2 on v1

v2 whole, which is shorter than its diff:
```python
import jax
import jax.numpy as jnp
from jax import lax
from jax.experimental import pallas as pl
from jax.experimental.pallas import tpu as pltpu
from jax.sharding import PartitionSpec as P

EPS = 1e-05
NZ, NX, NC = 4, 2, 2
NY, NL = 4, 2
F32, BF16 = jnp.float32, jnp.bfloat16


def dot(left, right, a, b):
    return lax.dot_general(left, right, (((a,), (b,)), ((), ())), preferred_element_type=F32)


def kernel_call(body, name, steps, in_specs, out_specs, out_shape, scratch, args):
    return pl.pallas_call(
        body,
        grid=(steps,),
        in_specs=in_specs,
        out_specs=out_specs,
        out_shape=out_shape,
        scratch_shapes=scratch,
        compiler_params=pltpu.CompilerParams(vmem_limit_bytes=60 * 2**20),
        name=name,
    )(*args)


def hidden_units(left, left_other, w, w_other, part, kinds, steps):
    f, (width, m) = left.shape[1], (w.shape[0], left.shape[0] // NX)
    n, tok = width // steps, m // len(kinds)

    def body(l, lo, w, wo, *outs):
        total = dot(l[...], w[...], 1, 1) + dot(lo[...], wo[...], 1, 1)
        for at, out in enumerate(outs):
            out[...] = total[at * tok:(at + 1) * tok].astype(out.dtype)

    lefts = [pl.BlockSpec((m, f), lambda i: (part, 0))] * 2
    rights = [pl.BlockSpec((n, f), lambda i: (i, 0))] * 2
    return kernel_call(
        body, "hidden_units", steps, lefts + rights, [pl.BlockSpec((tok, n), lambda i: (0, i))] * len(kinds),
        [jax.ShapeDtypeStruct((tok, width), kind) for kind in kinds], [], (left, left_other, w, w_other),
    )


def at_block(rows, n, block):
    return pl.BlockSpec((rows, n), lambda i: (block, i))


def input_grads(gate, up, w_gate, w_up, tok, steps):
    f, width = w_gate.shape
    k, count = width // steps, len(gate)

    def body(*refs):
        gates, ups, (wg, wu, out) = refs[:count], refs[count:2 * count], refs[2 * count:]
        total = dot(jnp.concatenate([p[...] for p in gates], axis=0), wg[...], 1, 1)
        total += dot(jnp.concatenate([p[...] for p in ups], axis=0), wu[...], 1, 1)

        @pl.when(pl.program_id(0) == 0)
        def _():
            out[...] = total

        @pl.when(pl.program_id(0) > 0)
        def _():
            out[...] += total

    specs = [at_block(tok, k, block) for _, block in gate + up] + [at_block(f, k, 0)] * 2
    m = tok * count
    return kernel_call(
        body, "input_grads", steps, specs, pl.BlockSpec((m, f), lambda i: (0, 0)),
        jax.ShapeDtypeStruct((m, f), F32), [], (*[x for x, _ in gate + up], w_gate, w_up),
    )


def gate_up_grads(normed_t, gate, up, tok, steps):
    f, t = normed_t.shape
    width, count = gate[0][0].shape[1], len(gate)
    n = width // steps

    def body(left, *refs):
        gates, ups, (gate_out, up_out) = refs[:count], refs[count:2 * count], refs[2 * count:]
        left = left[...]
        gate_out[...] = dot(left, jnp.concatenate([p[...] for p in gates], axis=0), 1, 0).astype(BF16)
        up_out[...] = dot(left, jnp.concatenate([p[...] for p in ups], axis=0), 1, 0).astype(BF16)

    specs = [pl.BlockSpec((f, t), lambda i: (0, 0))] + [at_block(tok, n, block) for _, block in gate + up]
    return kernel_call(
        body, "gate_up_grads", steps, specs, [at_block(f, n, 0)] * 2,
        [jax.ShapeDtypeStruct((f, width), BF16)] * 2, [], (normed_t, *[x for x, _ in gate + up]),
    )


def down_grads(hid, hid_other, out, width, first, earlier, steps):
    f, (t, some) = out.shape[1], hid.shape
    n = some // steps

    def body(left, left_other, right, *refs):
        refs[-1][...] = (dot(left[...], right[:t], 0, 0) + dot(left_other[...], right[t:], 0, 0)).astype(BF16)

    specs = [at_block(t, n, 0)] * 2 + [pl.BlockSpec((2 * t, f), lambda i: (0, 0))]
    more = () if earlier is None else (earlier,)
    return pl.pallas_call(
        body,
        grid=(steps,),
        in_specs=specs + [pl.BlockSpec(memory_space=pl.ANY)] * len(more),
        out_specs=pl.BlockSpec((n, f), lambda i: (first + i, 0)),
        out_shape=jax.ShapeDtypeStruct((width, f), BF16),
        input_output_aliases={3: 0} if more else {},
        compiler_params=pltpu.CompilerParams(vmem_limit_bytes=60 * 2**20),
        name="down_grads",
    )(hid, hid_other, out, *more)


def col_to(x, name, dz=0, dx=0, dc=0):
    pairs = []
    for z in range(NZ):
        for h in range(NX):
            for c in range(NC):
                dst = (((z + dz) % NZ) * NX + (h + dx) % NX) * NC + (c + dc) % NC
                pairs.append(((z * NX + h) * NC + c, dst))
    with jax.named_scope(name):
        return lax.ppermute(x, "col", pairs)


def row_to(x, name, dy=0, dl=0):
    pairs = []
    for y in range(NY):
        for l in range(NL):
            pairs.append((y * NL + l, ((y + dy) % NY) * NL + (l + dl) % NL))
    with jax.named_scope(name):
        return lax.ppermute(x, "row", pairs)


def phase(*arrays):
    return lax.optimization_barrier(arrays)


def local(inputs, out_grad, gain, w_gate, w_up, w_down, gate_pre, up_pre):
    rows, feats = inputs.shape
    width = gate_pre.shape[1]
    tok = gate_pre.shape[0]
    half = tok // 2
    total_feats = feats * NZ * NX * NC
    steps = 2 if width % 256 == 0 else 1
    ahead = width // 4
    col, row = lax.axis_index("col"), lax.axis_index("row")
    z, h, c = col // (NX * NC), (col // NC) % NX, col % NC
    y, l = row // NL, row % NL

    same = (l + h) % NX == 0

    def order(mine, other):
        f = mine.shape[1]
        mine, other = mine.reshape(NC, tok, f), other.reshape(NC, tok, f)
        pair = jnp.stack([jnp.where(same, mine, other), jnp.where(same, other, mine)])
        return jnp.where(c == 0, pair, pair[:, ::-1])[:, :, None]

    def assemble(pairs):
        both = [jnp.zeros((NX, NZ, *pairs[0].shape[3:]), pairs[0].dtype) for _ in range(NC)]
        for ky, pair in enumerate(pairs):
            at = (0, (y + ky - z) % NZ, 0, 0)
            both = [lax.dynamic_update_slice(full, pair[:, i], at) for i, full in enumerate(both)]
        return [full.reshape(-1, full.shape[3]) for full in both]

    def neighbour(x, name):
        with jax.named_scope(name):
            return lax.ppermute(x, "col", [(i, i ^ NC * NX) for i in range(NZ * NX * NC)])

    def neighbour_row(x, name):
        with jax.named_scope(name):
            return lax.ppermute(x, "row", [(i, i ^ NL) for i in range(NY * NL)])

    def gather_hidden(x, name):
        groups = [[chip * NC + core for chip in range(NZ * NX)] for core in range(NC)]
        copies = jnp.broadcast_to(x[None], (NZ * NX, *x.shape))
        with jax.named_scope(name):
            return lax.all_to_all(copies, "col", 0, 0, axis_index_groups=groups, tiled=True).reshape(-1, x.shape[1])

    out_xl = row_to(out_grad, "out_xl", dl=1)
    w_down_other = col_to(w_down, "w_down", dc=1)
    gates = gate_pre.astype(F32)
    ups = up_pre.astype(F32)
    sig = jax.nn.sigmoid(gates)
    hidden = (gates * sig * ups).astype(BF16)
    hidden_a, hidden_b = hidden[:, :ahead], hidden[:, ahead:]
    values = inputs.astype(F32)
    squares = jnp.sum(values * values, axis=1).reshape(1, rows)
    squares = squares + col_to(squares, "squares", dc=1)
    pair = order(out_grad, out_xl)
    pair, hidden_a, hidden_b, w_down_other, squares = phase(pair, hidden_a, hidden_b, w_down_other, squares)

    out_y = [row_to(pair, "out_y", -ky) for ky in range(1, NY)]
    hid_a = gather_hidden(hidden_a, "hid_a")
    squares = squares + neighbour(squares, "squares")
    out_mine, out_theirs = assemble([pair] + out_y)
    out_mine, out_theirs, squares = phase(out_mine, out_theirs, squares)

    out_other = col_to(out_theirs, "out_core", dc=1)
    far0, far1, far2, far3 = hidden_units(
        out_mine, out_other, w_down, w_down_other, 1, (F32, BF16, BF16, BF16), steps
    )
    far0, far1, far2, far3, out_mine, out_other, hid_a, squares = phase(
        far0, far1, far2, far3, out_mine, out_other, hid_a, squares
    )

    x_in = col_to(far2, "rs_x", dx=1)
    b_in = col_to(far1, "rs_b", dz=1)
    a_in = col_to(far3, "rs_a", dz=-1)
    near0, near1, near2, near3 = hidden_units(out_mine, out_other, w_down, w_down_other, 0, (F32,) * NZ, steps)
    squares = phase(squares, near0)[0]
    squares = squares + col_to(squares, "squares", dz=2)
    x_in, b_in, a_in, near0, near1, near2, near3, squares, hid_a = phase(
        x_in, b_in, a_in, near0, near1, near2, near3, squares, hid_a
    )
    b_half = col_to((near2[:half] + x_in[:half].astype(F32)).astype(BF16), "rs_fb", dz=1)
    a_half = col_to((near2[half:] + x_in[half:].astype(F32)).astype(BF16), "rs_fa", dz=-1)
    x_last = col_to((far0 + b_in.astype(F32) + a_in.astype(F32)).astype(BF16), "rs_xl", dx=1)
    b_sum = jnp.concatenate([near1[:half] + b_half.astype(F32), near1[half:]], axis=0).astype(BF16)
    a_sum = jnp.concatenate([near3[:half], near3[half:] + a_half.astype(F32)], axis=0).astype(BF16)
    b_sum, a_sum, out_mine, out_theirs, squares, hid_a = phase(b_sum, a_sum, out_mine, out_theirs, squares, hid_a)
    b_last = col_to(b_sum, "rs_bl", dz=1)
    a_last = col_to(a_sum, "rs_al", dz=-1)
    squares = squares + col_to(squares, "squares", dx=1)
    rstd = lax.rsqrt(squares.reshape(rows) / total_feats + EPS)
    normed = (values * rstd[:, None] * gain[None, :]).astype(BF16)
    copies = jnp.broadcast_to(normed[None], (NY * NL, rows, feats))
    with jax.named_scope("normed_rows"):
        whole = lax.all_to_all(copies, "row", 0, 0, tiled=True)
    d_hidden = near0 + x_last.astype(F32) + b_last.astype(F32) + a_last.astype(F32)
    silu = gates * sig
    d_gate = (d_hidden * ups * sig * (1.0 + gates * (1.0 - sig))).astype(BF16)
    d_up = (d_hidden * silu).astype(BF16)
    both = jnp.concatenate([d_gate, d_up], axis=0)
    d_gate, d_up, both, hid_a, rstd, out_mine, out_theirs = phase(
        d_gate, d_up, both, hid_a, rstd, out_mine, out_theirs
    )

    gate_b = col_to(d_gate, "ag_gate_b", dz=1)
    up_a = col_to(d_up, "ag_up_a", dz=-1)
    up_b = col_to(d_up, "ag_up_b", dz=1)
    gate_a = col_to(d_gate, "ag_gate_a", dz=-1)
    both_x = col_to(both, "ag_x", dx=1)
    def by_chip(x):
        x = x.reshape(NX, NZ, tok, feats)
        x = jnp.where(h == 0, x, x[::-1]).transpose(1, 0, 2, 3)
        return lax.dynamic_slice_in_dim(jnp.concatenate([x, x]), (NZ - z) % NZ, NZ).reshape(-1, feats)

    out_down = jnp.concatenate([by_chip(out_mine), by_chip(out_theirs)], axis=0)
    pairs = []
    for at in range(NY):
        even, odd = whole[at * NL].reshape(NC, tok, feats), whole[at * NL + 1].reshape(NC, tok, feats)
        one = jnp.stack([jnp.where(h == 0, even, odd), jnp.where(h == 0, odd, even)])
        pairs.append(jnp.where(c == 0, one, one[:, ::-1])[:, :, None])
    normed_all = jnp.zeros((NX, NC, NZ, tok, feats), BF16)
    for at, one in enumerate(pairs):
        normed_all = lax.dynamic_update_slice(normed_all, one, (0, 0, (at - z) % NZ, 0, 0))
    normed_t = normed_all.reshape(-1, feats).T
    gate_b, up_a, up_b, gate_a, both_x, both, hid_a, normed_t, out_down = phase(
        gate_b, up_a, up_b, gate_a, both_x, both, hid_a, normed_t, out_down
    )

    gate_f = col_to(gate_b, "ag_gate_f", dz=1)
    up_f = col_to(up_a, "ag_up_f", dz=-1)
    hid_a_other = col_to(hid_a, "hid_core", dc=1)
    swap_late = phase(both, up_a, gate_a, gate_b, up_b, both_x, hid_a_other)
    swapped = [col_to(piece, "ag_core", dc=1) for piece in swap_late[:6]]
    gate_f, up_f, both, gate_b, up_a, up_b, gate_a, both_x, normed_t, hid_a, hid_a_other, *swapped = phase(
        gate_f, up_f, both, gate_b, up_a, up_b, gate_a, both_x, normed_t, hid_a, hid_a_other, *swapped
    )

    both_xb = col_to(both_x, "ag_xb", dz=1)
    both_xa = col_to(both_x, "ag_xa", dz=-1)
    gate_xf = col_to(gate_f, "ag_gate_xf", dx=1)
    up_xf = col_to(up_f, "ag_up_xf", dx=1)
    swapped_f = [col_to(piece, "ag_core", dc=1) for piece in (gate_f, up_f)]

    near_ones = [both, up_a, gate_a, gate_f, up_f, gate_b, up_b, both_x]
    swapped = swapped[:3] + swapped_f + swapped[3:]

    def by_k(both, up_a, gate_a, gate_f, up_f, gate_b, up_b, both_x):
        gate = [(both, 0), (gate_a, 0), (gate_f, 0), (gate_b, 0)]
        up = [(both, 1), (up_a, 0), (up_f, 0), (up_b, 0)]
        return gate, up, [(both_x, 0)], [(both_x, 1)]

    gate_mine, up_mine, gate_x, up_x = by_k(*near_ones)
    gate_theirs, up_theirs, gate_xt, up_xt = by_k(*swapped)
    gate_first = gate_mine + gate_theirs + gate_x + gate_xt
    up_first = up_mine + up_theirs + up_x + up_xt
    term_first = input_grads(gate_first, up_first, w_gate, w_up, tok, steps)

    term_first, hid_a = phase(term_first, hid_a)
    down_a = down_grads(hid_a, hid_a_other, out_down, width, 0, None, 1)
    both_xb, both_xa, gate_xf, up_xf, term_first, hidden_b, down_a = phase(
        both_xb, both_xa, gate_xf, up_xf, term_first, hidden_b, down_a
    )
    hid_b = gather_hidden(hidden_b, "hid_b")

    far_ones = [both_xa, gate_xf, up_xf, both_xb]
    swapped_far = [col_to(piece, "ag_core", dc=1) for piece in far_ones]

    def by_k_far(both_xa, gate_xf, up_xf, both_xb):
        return [(both_xa, 0), (gate_xf, 0), (both_xb, 0)], [(both_xa, 1), (up_xf, 0), (both_xb, 1)]

    gate_xmine, up_xmine = by_k_far(*far_ones)
    gate_xtheirs, up_xtheirs = by_k_far(*swapped_far)
    term_second = input_grads(gate_xmine + gate_xtheirs, up_xmine + up_xtheirs, w_gate, w_up, tok, steps)
    gate_all = gate_mine + gate_theirs + gate_x + gate_xmine + gate_xt + gate_xtheirs
    up_all = up_mine + up_theirs + up_x + up_xmine + up_xt + up_xtheirs
    term = jnp.concatenate([
        term_first[:9 * tok], term_second[:3 * tok], term_first[9 * tok:], term_second[3 * tok:]
    ], axis=0).reshape(NX, NC, NZ, tok, feats)
    def term_of(ky):
        return lax.dynamic_slice(term, (0, 0, (y + ky - z) % NZ, 0, 0), (NX, NC, 1, tok, feats))[:, :, 0]

    mine, normed_t, *sent = phase(term_of(0), normed_t, *[term_of(ky).astype(BF16) for ky in range(1, NY)])
    received = [row_to(piece, "dn_y", ky + 1) for ky, piece in enumerate(sent)]
    grad_gate, grad_up = gate_up_grads(normed_t, gate_all, up_all, tok, steps)
    d_normed = mine
    for piece in received:
        d_normed = d_normed + piece.astype(F32)
    near, far = (jnp.where(same, d_normed[i], d_normed[1 - i]) for i in range(2))
    near, far, grad_gate, grad_up = phase(near, far.astype(BF16), grad_gate, grad_up)

    d_normed = near + row_to(far, "dn_xl", dl=1).astype(F32)
    d_normed = jnp.where(c == 0, d_normed, d_normed[::-1]).reshape(rows, feats)
    proj = jnp.sum(d_normed * gain[None, :] * values, axis=1).reshape(1, rows)
    grad_gain = jnp.sum(d_normed * values * rstd[:, None], axis=0).reshape(1, feats)
    proj, grad_gain = phase(proj, grad_gain)

    proj = proj + col_to(proj, "proj", dc=1)
    proj, grad_gain = phase(proj, grad_gain)
    proj = proj + col_to(proj, "proj", dx=1)
    grad_gain = grad_gain + row_to(grad_gain, "gain", dl=1)
    proj, grad_gain, hid_b = phase(proj, grad_gain, hid_b)
    hid_b_other = col_to(hid_b, "hid_core", dc=1)
    proj = proj + neighbour(proj, "proj")
    grad_gain = grad_gain + neighbour_row(grad_gain, "gain")
    proj, grad_gain, hid_b, hid_b_other = phase(proj, grad_gain, hid_b, hid_b_other)
    grad_gain = grad_gain + row_to(grad_gain, "gain", dy=2)
    grad_down = down_grads(hid_b, hid_b_other, out_down, width, 1, down_a, 3)
    proj = (proj + col_to(proj, "proj", dz=2)).reshape(rows)
    scaled = rstd * rstd * rstd * proj / total_feats
    d_input = (
        out_grad.astype(F32) + rstd[:, None] * d_normed * gain[None, :] - values * scaled[:, None]
    ).astype(BF16)
    return (d_input, grad_gain.reshape(feats), grad_gate, grad_up, grad_down)


def solution(mesh):
    in_specs = (
        P("row", "col"),
        P("row", "col"),
        P("col"),
        P("col", "row"),
        P("col", "row"),
        P("row", "col"),
        P("col", "row"),
        P("col", "row"),
    )
    out_specs = (P("row", "col"), P("col"), P("col", "row"), P("col", "row"), P("row", "col"))
    return jax.shard_map(local, mesh=mesh, in_specs=in_specs, out_specs=out_specs, check_vma=False)
```

time: 230 us -> 226 us (0.983)
  starting transfers between devices: 67.1 us -> 75.5 us
  waiting for transfers between devices: 74.2 us -> 68 us
  local copies, waits for them, and re-layouts: 15.6 us -> 12 us
  other arithmetic: 18.5 us -> 16 us
    pallas_call x7 -> x5, Pallas kernels: 52.7 us -> 41.7 us  [kernel_call(): pl.pallas_call(body, grid=(steps,), in_specs=in_specs, out_specs=out_spec...]
    pallas_call x0 -> x2, Pallas kernels: none -> 10.7 us  [down_grads(): pl.pallas_call(body, grid=(steps,), in_specs=specs + [pl.BlockSpec(memory...]
    ppermute x34 -> x41, starting transfers between devices: 27.5 us -> 38 us  [col_to(): return lax.ppermute(x, 'col', pairs)]
    slice x12 -> x2, local copies, waits for them, and re-layouts: 7.46 us -> 0.76 us  [local(): hidden_a, hidden_b = (hidden[:, :ahead], hidden[:, ahead:])]
    all_to_all x2, waiting for transfers between devices: 7.71 us -> 1.31 us  [gather_hidden(): lax.all_to_all(copies, 'col', 0, 0, axis_index_groups=groups, tiled=True)]
    ppermute x34 -> x41, waiting for transfers between devices: 50.1 us -> 56.1 us  [col_to(): return lax.ppermute(x, 'col', pairs)]
    ppermute x10, waiting for transfers between devices: 13.5 us -> 7.7 us  [row_to(): return lax.ppermute(x, 'row', pairs)]
    concatenate x4, other arithmetic: 6.19 us -> 2.66 us  [the longest x1 1.22 us: local(): both = jnp.concatenate([d_gate, d_up], axis=0)]
  transfers between devices with their start and end apart: 50 -> 57, of which waited for: 23 -> 20; matrix products, arithmetic and copies ran while one was open for 13% -> 10% of each run, Pallas kernels for 23% -> 23%
where the time goes in v2:
time: 226 us; the launch traced here: 225 us
  starting transfers between devices  75.5 us (33%)
  waiting for transfers between devices  68 us (30%)
  Pallas kernels  52.4 us (23%)
  other arithmetic  16 us (7%)
  local copies, waits for them, and re-layouts  12 us (5%)
    ppermute x41, waiting for transfers between devices, col_to(): return lax.ppermute(x, 'col', pairs)  56.1 us
    pallas_call x5, Pallas kernels, kernel_call(): pl.pallas_call(body, grid=(steps,), in_specs=in_specs, out_specs=out_spec...  41.7 us
    ppermute x41, starting transfers between devices, col_to(): return lax.ppermute(x, 'col', pairs)  38 us
    ppermute x10, starting transfers between devices, row_to(): return lax.ppermute(x, 'row', pairs)  15.6 us
    all_to_all x2, starting transfers between devices, gather_hidden(): lax.all_to_all(copies, 'col', 0, 0, axis_index_groups=groups, tiled=True)  13.3 us
    pallas_call x2, Pallas kernels, down_grads(): pl.pallas_call(body, grid=(steps,), in_specs=specs + [pl.BlockSpec(memory...  10.7 us
    ppermute x10, waiting for transfers between devices, row_to(): return lax.ppermute(x, 'row', pairs)  7.7 us
    all_to_all x1, starting transfers between devices, local(): whole = lax.all_to_all(copies, 'row', 0, 0, tiled=True)  4.78 us
  transfers between devices with their start and end apart: 57, of which 20 were waited for; matrix products, arithmetic and copies ran while one was open for 10% of the time, Pallas kernels for 23%

profile of v2, /device:TPU:6, one launch (start us, length us, event | category | flops | bytes accessed | tf_op | source)
XLA Modules:
  0.0 225.3 jit_solution(17273336692307118677)
XLA Ops:
  2.9 1.4 fusion
  5.1 2.0 collective-permute-done.2
  7.5 3.0 %collective-permute-start.3 = (bf16[2,2,1,64,512]{4,3,0,2,1:T(8,128)(2,1)S(1)}, bf16[2,2,1,64,512]{4,3,0,2,1:T(8,128)(2,1)S(1)}, u32[]{:S(2)}, u32[]{:S(2)}) collective-permute-start(bf16[2,2,1,64,512]{4,3,0,2,1:T(8,128)(2,1)S(1)} %fusion.12), channel_id=1, source_target_pairs={{0,96},{16,112},{32,0},{48,16},{64,32},{80,48},{96,64},{112,80},{1... | collective-permute-start | bytes 786440 | tf_op jit(solution)/shard_map/out_y/ppermute | solution.py:133
  12.1 1.9 collective-permute-start.6
  15.2 7.8 %all-to-all-start = ((bf16[8,64,896]{2,1,0:T(8,128)(2,1)}), bf16[8,64,896]{2,1,0:T(8,128)(2,1)S(1)}, u32[]{:S(2)}, u32[]{:S(2)}) async-start(bf16[8,64,896]{2,1,0:T(8,128)(2,1)} %broadcast_in_dim.19), calls=%async_computation | async-start | bytes 1835008 | tf_op jit(solution)/shard_map/hid_a/all_to_all | solution.py:179
  23.1 2.6 %collective-permute-done.5 = bf16[2,2,1,64,512]{4,3,0,2,1:T(8,128)(2,1)S(1)} collective-permute-done((bf16[2,2,1,64,512]{4,3,0,2,1:T(8,128)(2,1)S(1)}, bf16[2,2,1,64,512]{4,3,0,2,1:T(8,128)(2,1)S(1)}, u32[]{:S(2)}, u32[]{:S(2)}) %collective-permute-start.5) | collective-permute-done | bytes 262176 | tf_op jit(solution)/shard_map/out_y/ppermute | solution.py:133
  25.8 1.9 collective-permute-done.7.lo
  28.5 5.5 %hidden_units.2 = (f32[64,3584]{1,0:T(8,128)}, bf16[64,3584]{1,0:T(8,128)(2,1)}, bf16[64,3584]{1,0:T(8,128)(2,1)}, bf16[64,3584]{1,0:T(8,128)(2,1)}) custom-call(bf16[512,512]{1,0:T(8,128)(2,1)} %bitcast.138, bf16[512,512]{1,0:T(8,128)(2,1)} %copy-done.11, bf16[3584,512]{1,0:T(8,128)(2,1)} %w.3, bf16[3584,512]{1,0:T(8,128)(2,1)} %collective-permute-done.1.wo), custom_call_target="tpu_custom_call" | custom-call | tf_op jit(solution)/shard_map/hidden_units/pallas_call | solution.py:19
  34.0 1.3 all-to-all-done
  35.3 2.7 %collective-permute-start.8 = (bf16[64,3584]{1,0:T(8,128)(2,1)}, bf16[64,3584]{1,0:T(8,128)(2,1)S(1)}, u32[]{:S(2)}, u32[]{:S(2)}) collective-permute-start(bf16[64,3584]{1,0:T(8,128)(2,1)} %get-tuple-element.126), channel_id=1, source_target_pairs={{0,2},{1,3},{2,0},{3,1},{4,6},{5,7},{6,4},{7,5},{8,10},{9,11},{10,... | collective-permute-start | bytes 1376264 | tf_op jit(solution)/shard_map/rs_x/ppermute | solution.py:124
  38.0 3.2 %collective-permute-start.10 = (bf16[64,3584]{1,0:T(8,128)(2,1)}, bf16[64,3584]{1,0:T(8,128)(2,1)}, u32[]{:S(2)}, u32[]{:S(2)}) collective-permute-start(bf16[64,3584]{1,0:T(8,128)(2,1)} %get-tuple-element.128), channel_id=1, source_target_pairs={{0,12},{1,13},{2,14},{3,15},{4,0},{5,1},{6,2},{7,3},{8,4},{9,5},{1... | collective-permute-start | bytes 1376264 | tf_op jit(solution)/shard_map/rs_a/ppermute | solution.py:124
  41.3 5.7 %hidden_units.3 = (f32[64,3584]{1,0:T(8,128)}, f32[64,3584]{1,0:T(8,128)}, f32[64,3584]{1,0:T(8,128)}, f32[64,3584]{1,0:T(8,128)}) custom-call(bf16[512,512]{1,0:T(8,128)(2,1)} %bitcast.139, bf16[512,512]{1,0:T(8,128)(2,1)} %copy-done.11, bf16[3584,512]{1,0:T(8,128)(2,1)} %w.3, bf16[3584,512]{1,0:T(8,128)(2,1)} %collective-permute-done.1.wo), custom_call_target="tpu_custom_call" | custom-call | tf_op jit(solution)/shard_map/hidden_units/pallas_call | solution.py:19
  47.2 4.9 %collective-permute-done.11 = f32[1,128]{1,0:T(1,128)S(1)} collective-permute-done((f32[1,128]{1,0:T(1,128)S(1)}, f32[1,128]{1,0:T(1,128)S(1)}, u32[]{:S(2)}, u32[]{:S(2)}) %collective-permute-start.11) | collective-permute-done | bytes 544 | tf_op jit(solution)/shard_map/squares/ppermute | solution.py:124
  53.1 1.4 add_convert_fusion.2
  55.1 2.7 %collective-permute-start.14 = (bf16[32,3584]{1,0:T(8,128)(2,1)S(1)}, bf16[32,3584]{1,0:T(8,128)(2,1)S(1)}, u32[]{:S(2)}, u32[]{:S(2)}) collective-permute-start(bf16[32,3584]{1,0:T(8,128)(2,1)S(1)} %get-tuple-element.232), channel_id=1, source_target_pairs={{0,12},{1,13},{2,14},{3,15},{4,0},{5,1},{6,2},{7,3},{8,4},{9,5},{1... | collective-permute-start | bytes 688136 | tf_op jit(solution)/shard_map/rs_fa/ppermute | solution.py:124
  57.8 2.1 add_convert_fusion
  60.0 1.6 collective-permute-start.12
  63.5 2.4 %collective-permute-start.16 = (bf16[64,3584]{1,0:T(8,128)(2,1)}, bf16[64,3584]{1,0:T(8,128)(2,1)}, u32[]{:S(2)}, u32[]{:S(2)}) collective-permute-start(bf16[64,3584]{1,0:T(8,128)(2,1)} %pad_maximum_fusion.4), channel_id=1, source_target_pairs={{0,12},{1,13},{2,14},{3,15},{4,0},{5,1},{6,2},{7,3},{8,4},{9,5},{1... | collective-permute-start | bytes 1376264 | tf_op jit(solution)/shard_map/rs_al/ppermute | solution.py:124
  65.9 1.5 collective-permute-start.17
  67.4 4.4 %collective-permute-done.17 = f32[1,128]{1,0:T(1,128)S(1)} collective-permute-done((f32[1,128]{1,0:T(1,128)S(1)}, f32[1,128]{1,0:T(1,128)S(1)}, u32[]{:S(2)}, u32[]{:S(2)}) %collective-permute-start.17) | collective-permute-done | bytes 544 | tf_op jit(solution)/shard_map/squares/ppermute | solution.py:124
  73.0 4.8 %all-to-all-start.1 = ((bf16[8,128,512]{2,1,0:T(8,128)(2,1)}), bf16[8,128,512]{2,1,0:T(8,128)(2,1)S(1)}, u32[]{:S(2)}, u32[]{:S(2)}) async-start(bf16[8,128,512]{2,1,0:T(8,128)(2,1)} %broadcast_in_dim.21), calls=%async_computation.1 | async-start | bytes 2097152 | tf_op jit(solution)/shard_map/normed_rows/all_to_all | solution.py:230
  77.9 2.9 %multiply_convert_fusion = (bf16[64,3584]{1,0:T(8,128)(2,1)}, bf16[64,3584]{1,0:T(8,128)(2,1)}) fusion(bf16[64,3584]{1,0:T(8,128)(2,1)S(1)} %copy-done.13, bf16[64,3584]{1,0:T(8,128)(2,1)} %collective-permute-done.16, bf16[64,3584]{1,0:T(8,128)(2,1)} %collective-permute-done.15, f32[64,3584]{1,0:T(8,128)S(1)} %copy-done.24, ...), kind=kLoop, calls=%fused_computation.20 | loop fusion | flops 4816896 | bytes 4128768 | tf_op jit(solution)/shard_map/convert_element_type | solution.py:234
  82.0 3.3 %collective-permute-start.19 = (bf16[64,3584]{1,0:T(8,128)(2,1)}, bf16[64,3584]{1,0:T(8,128)(2,1)}, u32[]{:S(2)}, u32[]{:S(2)}) collective-permute-start(bf16[64,3584]{1,0:T(8,128)(2,1)} %get-tuple-element.156), channel_id=1, source_target_pairs={{0,12},{1,13},{2,14},{3,15},{4,0},{5,1},{6,2},{7,3},{8,4},{9,5},{1... | collective-permute-start | bytes 1376264 | tf_op jit(solution)/shard_map/ag_up_a/ppermute | solution.py:124
  85.3 3.3 %collective-permute-start.21 = (bf16[64,3584]{1,0:T(8,128)(2,1)}, bf16[64,3584]{1,0:T(8,128)(2,1)}, u32[]{:S(2)}, u32[]{:S(2)}) collective-permute-start(bf16[64,3584]{1,0:T(8,128)(2,1)} %get-tuple-element.155), channel_id=1, source_target_pairs={{0,12},{1,13},{2,14},{3,15},{4,0},{5,1},{6,2},{7,3},{8,4},{9,5},{1... | collective-permute-start | bytes 1376264 | tf_op jit(solution)/shard_map/ag_gate_a/ppermute | solution.py:124
  92.0 1.4 copy.55
  93.3 8.9 %collective-permute-done.18.refs_3_ = bf16[64,3584]{1,0:T(8,128)(2,1)} collective-permute-done((bf16[64,3584]{1,0:T(8,128)(2,1)}, bf16[64,3584]{1,0:T(8,128)(2,1)}, u32[]{:S(2)}, u32[]{:S(2)}) %collective-permute-start.18) | collective-permute-done | bytes 458784 | tf_op jit(solution)/shard_map/ag_gate_b/ppermute | solution.py:124
  102.3 6.8 %collective-permute-done.22.refs_8_.refs_18_.refs_24_ = bf16[128,3584]{1,0:T(8,128)(2,1)S(1)} collective-permute-done((bf16[128,3584]{1,0:T(8,128)(2,1)S(1)}, bf16[128,3584]{1,0:T(8,128)(2,1)S(1)}, u32[]{:S(2)}, u32[]{:S(2)}) %collective-permute-start.22) | collective-permute-done | bytes 917536 | tf_op jit(solution)/shard_map/ag_x/ppermute | solution.py:124
  109.1 3.2 %collective-permute-start.24 = (bf16[64,3584]{1,0:T(8,128)(2,1)}, bf16[64,3584]{1,0:T(8,128)(2,1)}, u32[]{:S(2)}, u32[]{:S(2)}) collective-permute-start(bf16[64,3584]{1,0:T(8,128)(2,1)} %collective-permute-done.19.refs_11_.refs_17_), channel_id=1, source_target_pairs={{0,12},{1,13},{2,14},{3,15},{4,0},{5,1},{6,2},{7,3},{8,4},{9,5},{1... | collective-permute-start | bytes 1376264 | tf_op jit(solution)/shard_map/ag_up_f/ppermute | solution.py:124
  112.9 10.5 %collective-permute-done.23.refs_2_ = bf16[64,3584]{1,0:T(8,128)(2,1)S(1)} collective-permute-done((bf16[64,3584]{1,0:T(8,128)(2,1)}, bf16[64,3584]{1,0:T(8,128)(2,1)S(1)}, u32[]{:S(2)}, u32[]{:S(2)}) %collective-permute-start.23) | collective-permute-done | bytes 458784 | tf_op jit(solution)/shard_map/ag_gate_f/ppermute | solution.py:124
  124.1 1.4 collective-permute-done.28.refs_5_
  128.1 2.9 %collective-permute-start.33 = (bf16[128,3584]{1,0:T(8,128)(2,1)S(1)}, bf16[128,3584]{1,0:T(8,128)(2,1)S(1)}, u32[]{:S(2)}, u32[]{:S(2)}) collective-permute-start(bf16[128,3584]{1,0:T(8,128)(2,1)S(1)} %collective-permute-done.22.refs_8_.refs_18_.refs_24_), channel_id=1, source_target_pairs={{0,12},{1,13},{2,14},{3,15},{4,0},{5,1},{6,2},{7,3},{8,4},{9,5},{1... | collective-permute-start | bytes 2752520 | tf_op jit(solution)/shard_map/ag_xa/ppermute | solution.py:124
  131.2 3.4 %collective-permute-start.35 = (bf16[64,3584]{1,0:T(8,128)(2,1)}, bf16[64,3584]{1,0:T(8,128)(2,1)}, u32[]{:S(2)}, u32[]{:S(2)}) collective-permute-start(bf16[64,3584]{1,0:T(8,128)(2,1)} %collective-permute-done.24.refs_12_.refs_18_), channel_id=1, source_target_pairs={{0,2},{1,3},{2,0},{3,1},{4,6},{5,7},{6,4},{7,5},{8,10},{9,11},{10,... | collective-permute-start | bytes 1376264 | tf_op jit(solution)/shard_map/ag_up_xf/ppermute | solution.py:124
  134.7 10.0 %input_grads.2 = f32[640,512]{1,0:T(8,128)} custom-call(bf16[128,3584]{1,0:T(8,128)(2,1)} %copy-done, bf16[64,3584]{1,0:T(8,128)(2,1)} %collective-permute-done.21.refs_1_, bf16[64,3584]{1,0:T(8,128)(2,1)} %copy-done.16, bf16[64,3584]{1,0:T(8,128)(2,1)} %collective-permute-done.18.refs_3_, bf16[128,3584]{1,0:T(8,128)(2,1)} %copy-done.5, ...), custom_call_target="tpu_custom_call" | custom-call | tf_op jit(solution)/shard_map/input_grads/pallas_call | solution.py:19
  144.7 3.8 %down_grads.2.refs_0_ = bf16[3584,512]{1,0:T(8,128)(2,1)} custom-call(bf16[512,896]{1,0:T(8,128)(2,1)} %bitcast.145, bf16[512,896]{1,0:T(8,128)(2,1)} %collective-permute-done.25.left_other, bf16[1024,512]{1,0:T(8,128)(2,1)} %pad_maximum_fusion.1.right), custom_call_target="tpu_custom_call" | custom-call | tf_op jit(solution)/shard_map/down_grads/pallas_call | solution.py:104
  148.5 6.8 %collective-permute-done.35.refs_7_.refs_26_ = bf16[64,3584]{1,0:T(8,128)(2,1)} collective-permute-done((bf16[64,3584]{1,0:T(8,128)(2,1)}, bf16[64,3584]{1,0:T(8,128)(2,1)}, u32[]{:S(2)}, u32[]{:S(2)}) %collective-permute-start.35) | collective-permute-done | bytes 458784 | tf_op jit(solution)/shard_map/ag_up_xf/ppermute | solution.py:124
  156.5 1.8 broadcast_in_dim.51
  158.3 5.4 %all-to-all-start.2 = ((bf16[8,64,2688]{2,1,0:T(8,128)(2,1)}), bf16[8,64,2688]{2,1,0:T(8,128)(2,1)}, u32[]{:S(2)}, u32[]{:S(2)}) async-start(bf16[8,64,2688]{2,1,0:T(8,128)(2,1)} %broadcast_in_dim.51), calls=%async_computation.2 | async-start | bytes 5505024 | tf_op jit(solution)/shard_map/hid_b/all_to_all | solution.py:179
  164.7 7.5 %input_grads.3 = f32[384,512]{1,0:T(8,128)} custom-call(bf16[128,3584]{1,0:T(8,128)(2,1)} %copy-done.2, bf16[64,3584]{1,0:T(8,128)(2,1)} %copy-done.15, bf16[128,3584]{1,0:T(8,128)(2,1)} %copy-done.1, bf16[128,3584]{1,0:T(8,128)(2,1)} %copy-done.3, bf16[64,3584]{1,0:T(8,128)(2,1)} %collective-permute-done.39.refs_4_.refs_14_, ...), custom_call_target="tpu_custom_call" | custom-call | tf_op jit(solution)/shard_map/input_grads/pallas_call | solution.py:19
  174.0 2.6 %collective-permute-start.44 = (bf16[2,2,64,512]{3,2,1,0:T(8,128)(2,1)S(1)}, bf16[2,2,64,512]{3,2,1,0:T(8,128)(2,1)S(1)}, u32[]{:S(2)}, u32[]{:S(2)}) collective-permute-start(bf16[2,2,64,512]{3,2,1,0:T(8,128)(2,1)S(1)} %get-tuple-element.204), channel_id=1, source_target_pairs={{0,96},{16,112},{32,0},{48,16},{64,32},{80,48},{96,64},{112,80},{1... | collective-permute-start | bytes 786440 | tf_op jit(solution)/shard_map/dn_y/ppermute | solution.py:133
  178.5 13.1 %gate_up_grads.1 = (bf16[512,3584]{1,0:T(8,128)(2,1)}, bf16[512,3584]{1,0:T(8,128)(2,1)}) custom-call(bf16[512,1024]{1,0:T(8,128)(2,1)} %bitcast.142, bf16[128,3584]{1,0:T(8,128)(2,1)} %copy-done, bf16[64,3584]{1,0:T(8,128)(2,1)} %collective-permute-done.21.refs_1_, bf16[64,3584]{1,0:T(8,128)(2,1)} %copy-done.16, ...), custom_call_target="tpu_custom_call" | custom-call | tf_op jit(solution)/shard_map/gate_up_grads/pallas_call | solution.py:19
  192.0 5.1 %collective-permute-done.45 = bf16[2,64,512]{2,1,0:T(8,128)(2,1)S(1)} collective-permute-done((bf16[2,64,512]{2,1,0:T(8,128)(2,1)S(1)}, bf16[2,64,512]{2,1,0:T(8,128)(2,1)S(1)}, u32[]{:S(2)}, u32[]{:S(2)}) %collective-permute-start.45) | collective-permute-done | bytes 131104 | tf_op jit(solution)/shard_map/dn_xl/ppermute | solution.py:133
  198.5 2.5 %collective-permute-start.48 = (f32[1,512]{1,0:T(1,128)S(1)}, f32[1,512]{1,0:T(1,128)S(1)}, u32[]{:S(2)}, u32[]{:S(2)}) collective-permute-start(f32[1,512]{1,0:T(1,128)S(1)} %bitcast.159), channel_id=1, source_target_pairs={{0,16},{16,0},{32,48},{48,32},{64,80},{80,64},{96,112},{112,96},{1... | collective-permute-start | bytes 6152 | tf_op jit(solution)/shard_map/gain/ppermute | solution.py:133
  200.9 5.0 %collective-permute-done.47 = f32[1,128]{1,0:T(1,128)S(1)} collective-permute-done((f32[1,128]{1,0:T(1,128)S(1)}, f32[1,128]{1,0:T(1,128)S(1)}, u32[]{:S(2)}, u32[]{:S(2)}) %collective-permute-start.47) | collective-permute-done | bytes 544 | tf_op jit(solution)/shard_map/proj/ppermute | solution.py:124
  206.1 1.4 collective-permute-start.50
  208.1 3.0 %collective-permute-done.49 = f32[1,128]{1,0:T(1,128)S(1)} collective-permute-done((f32[1,128]{1,0:T(1,128)S(1)}, f32[1,128]{1,0:T(1,128)S(1)}, u32[]{:S(2)}, u32[]{:S(2)}) %collective-permute-start.49) | collective-permute-done | bytes 544 | tf_op jit(solution)/shard_map/proj/ppermute | solution.py:169
  211.4 2.7 %collective-permute-start.52 = (f32[1,128]{1,0:T(1,128)S(1)}, f32[1,128]{1,0:T(1,128)S(1)}, u32[]{:S(2)}, u32[]{:S(2)}) collective-permute-start(f32[1,128]{1,0:T(1,128)S(1)} %add.242), channel_id=1, source_target_pairs={{0,8},{1,9},{2,10},{3,11},{4,12},{5,13},{6,14},{7,15},{8,0},{9,1},... | collective-permute-start | bytes 1544 | tf_op jit(solution)/shard_map/proj/ppermute | solution.py:124
  214.1 3.0 %collective-permute-start.53 = (f32[1,512]{1,0:T(1,128)S(1)}, f32[1,512]{1,0:T(1,128)S(1)}, u32[]{:S(2)}, u32[]{:S(2)}) collective-permute-start(f32[1,512]{1,0:T(1,128)S(1)} %add.243), channel_id=1, source_target_pairs={{0,64},{16,80},{32,96},{48,112},{64,0},{80,16},{96,32},{112,48},{1... | collective-permute-start | bytes 6152 | tf_op jit(solution)/shard_map/gain/ppermute | solution.py:133
  217.1 6.8 %down_grads.3 = bf16[3584,512]{1,0:T(8,128)(2,1)} custom-call(bf16[512,2688]{1,0:T(8,128)(2,1)} %bitcast.62.left, bf16[512,2688]{1,0:T(8,128)(2,1)} %copy-done.10, bf16[1024,512]{1,0:T(8,128)(2,1)} %pad_maximum_fusion.1.right, bf16[3584,512]{1,0:T(8,128)(2,1)} %down_grads.2.refs_0_), custom_call_target="tpu_custom_call", output_to_operand_aliasing={{}: (3, {})} | custom-call | tf_op jit(solution)/shard_map/down_grads/pallas_call | solution.py:104
  (210 shorter events, 30.4 us)
Async XLA Ops:
  0.6 6.8 %collective-permute-start.1 = (bf16[3584,512]{1,0:T(8,128)(2,1)}, bf16[3584,512]{1,0:T(8,128)(2,1)}, u32[]{:S(2)}, u32[]{:S(2)}) collective-permute-start(bf16[3584,512]{1,0:T(8,128)(2,1)} %w.3), channel_id=1, source_target_pairs={{0,1},{1,0},{2,3},{3,2},{4,5},{5,4},{6,7},{7,6},{8,9},{9,8},{10,11... | collective-permute-start | bytes 11010056 | tf_op jit(solution)/shard_map/w_down/ppermute | solution.py:124
  0.7 6.4 %collective-permute-start = (bf16[128,512]{1,0:T(8,128)(2,1)}, bf16[128,512]{1,0:T(8,128)(2,1)S(1)}, u32[]{:S(2)}, u32[]{:S(2)}) collective-permute-start(bf16[128,512]{1,0:T(8,128)(2,1)} %param.9), channel_id=1, source_target_pairs={{0,16},{16,0},{32,48},{48,32},{64,80},{80,64},{96,112},{112,96},{1... | collective-permute-start | bytes 393224 | tf_op jit(solution)/shard_map/out_xl/ppermute | solution.py:133
  2.7 4.4 %collective-permute-start.2 = (f32[1,128]{1,0:T(1,128)S(1)}, f32[1,128]{1,0:T(1,128)S(1)}, u32[]{:S(2)}, u32[]{:S(2)}) collective-permute-start(f32[1,128]{1,0:T(1,128)S(1)} %bitcast.162), channel_id=1, source_target_pairs={{0,1},{1,0},{2,3},{3,2},{4,5},{5,4},{6,7},{7,6},{8,9},{9,8},{10,11... | collective-permute-start | bytes 1544 | tf_op jit(solution)/shard_map/squares/ppermute | solution.py:124
  7.5 15.5 %collective-permute-start.3 = (bf16[2,2,1,64,512]{4,3,0,2,1:T(8,128)(2,1)S(1)}, bf16[2,2,1,64,512]{4,3,0,2,1:T(8,128)(2,1)S(1)}, u32[]{:S(2)}, u32[]{:S(2)}) collective-permute-start(bf16[2,2,1,64,512]{4,3,0,2,1:T(8,128)(2,1)S(1)} %fusion.12), channel_id=1, source_target_pairs={{0,96},{16,112},{32,0},{48,16},{64,32},{80,48},{96,64},{112,80},{1... | collective-permute-start | bytes 786440 | tf_op jit(solution)/shard_map/out_y/ppermute | solution.py:133
  10.5 12.6 %collective-permute-start.4 = (bf16[2,2,1,64,512]{4,3,0,2,1:T(8,128)(2,1)S(1)}, bf16[2,2,1,64,512]{4,3,0,2,1:T(8,128)(2,1)S(1)}, u32[]{:S(2)}, u32[]{:S(2)}) collective-permute-start(bf16[2,2,1,64,512]{4,3,0,2,1:T(8,128)(2,1)S(1)} %fusion.12), channel_id=1, source_target_pairs={{0,64},{16,80},{32,96},{48,112},{64,0},{80,16},{96,32},{112,48},{1... | collective-permute-start | bytes 786440 | tf_op jit(solution)/shard_map/out_y/ppermute | solution.py:133
  11.1 14.6 %collective-permute-start.5 = (bf16[2,2,1,64,512]{4,3,0,2,1:T(8,128)(2,1)S(1)}, bf16[2,2,1,64,512]{4,3,0,2,1:T(8,128)(2,1)S(1)}, u32[]{:S(2)}, u32[]{:S(2)}) collective-permute-start(bf16[2,2,1,64,512]{4,3,0,2,1:T(8,128)(2,1)S(1)} %fusion.12), channel_id=1, source_target_pairs={{0,32},{16,48},{32,64},{48,80},{64,96},{80,112},{96,0},{112,16},{1... | collective-permute-start | bytes 786440 | tf_op jit(solution)/shard_map/out_y/ppermute | solution.py:133
  12.1 10.9 %collective-permute-start.6 = (f32[1,128]{1,0:T(1,128)S(1)}, f32[1,128]{1,0:T(1,128)S(1)}, u32[]{:S(2)}, u32[]{:S(2)}) collective-permute-start(f32[1,128]{1,0:T(1,128)S(1)} %bitcast_add_fusion), channel_id=1, source_target_pairs={{0,4},{1,5},{2,6},{3,7},{4,0},{5,1},{6,2},{7,3},{8,12},{9,13},{10,... | collective-permute-start | bytes 1544 | tf_op jit(solution)/shard_map/squares/ppermute | solution.py:169
  15.2 20.1 %all-to-all-start = ((bf16[8,64,896]{2,1,0:T(8,128)(2,1)}), bf16[8,64,896]{2,1,0:T(8,128)(2,1)S(1)}, u32[]{:S(2)}, u32[]{:S(2)}) async-start(bf16[8,64,896]{2,1,0:T(8,128)(2,1)} %broadcast_in_dim.19), calls=%async_computation | async-start | bytes 1835008 | tf_op jit(solution)/shard_map/hid_a/all_to_all | solution.py:179
  35.3 16.8 %collective-permute-start.8 = (bf16[64,3584]{1,0:T(8,128)(2,1)}, bf16[64,3584]{1,0:T(8,128)(2,1)S(1)}, u32[]{:S(2)}, u32[]{:S(2)}) collective-permute-start(bf16[64,3584]{1,0:T(8,128)(2,1)} %get-tuple-element.126), channel_id=1, source_target_pairs={{0,2},{1,3},{2,0},{3,1},{4,6},{5,7},{6,4},{7,5},{8,10},{9,11},{10,... | collective-permute-start | bytes 1376264 | tf_op jit(solution)/shard_map/rs_x/ppermute | solution.py:124
  38.0 14.1 %collective-permute-start.9 = (bf16[64,3584]{1,0:T(8,128)(2,1)}, bf16[64,3584]{1,0:T(8,128)(2,1)S(1)}, u32[]{:S(2)}, u32[]{:S(2)}) collective-permute-start(bf16[64,3584]{1,0:T(8,128)(2,1)} %get-tuple-element.127), channel_id=1, source_target_pairs={{0,4},{1,5},{2,6},{3,7},{4,8},{5,9},{6,10},{7,11},{8,12},{9,13},{1... | collective-permute-start | bytes 1376264 | tf_op jit(solution)/shard_map/rs_b/ppermute | solution.py:124
  38.0 14.1 %collective-permute-start.10 = (bf16[64,3584]{1,0:T(8,128)(2,1)}, bf16[64,3584]{1,0:T(8,128)(2,1)}, u32[]{:S(2)}, u32[]{:S(2)}) collective-permute-start(bf16[64,3584]{1,0:T(8,128)(2,1)} %get-tuple-element.128), channel_id=1, source_target_pairs={{0,12},{1,13},{2,14},{3,15},{4,0},{5,1},{6,2},{7,3},{8,4},{9,5},{1... | collective-permute-start | bytes 1376264 | tf_op jit(solution)/shard_map/rs_a/ppermute | solution.py:124
  47.0 5.1 %collective-permute-start.11 = (f32[1,128]{1,0:T(1,128)S(1)}, f32[1,128]{1,0:T(1,128)S(1)}, u32[]{:S(2)}, u32[]{:S(2)}) collective-permute-start(f32[1,128]{1,0:T(1,128)S(1)} %add.209), channel_id=1, source_target_pairs={{0,8},{1,9},{2,10},{3,11},{4,12},{5,13},{6,14},{7,15},{8,0},{9,1},... | collective-permute-start | bytes 1544 | tf_op jit(solution)/shard_map/squares/ppermute | solution.py:124
  54.5 7.3 %collective-permute-start.13 = (bf16[32,3584]{1,0:T(8,128)(2,1)S(1)}, bf16[32,3584]{1,0:T(8,128)(2,1)S(1)}, u32[]{:S(2)}, u32[]{:S(2)}) collective-permute-start(bf16[32,3584]{1,0:T(8,128)(2,1)S(1)} %get-tuple-element.233), channel_id=1, source_target_pairs={{0,4},{1,5},{2,6},{3,7},{4,8},{5,9},{6,10},{7,11},{8,12},{9,13},{1... | collective-permute-start | bytes 688136 | tf_op jit(solution)/shard_map/rs_fb/ppermute | solution.py:124
  55.1 7.6 %collective-permute-start.14 = (bf16[32,3584]{1,0:T(8,128)(2,1)S(1)}, bf16[32,3584]{1,0:T(8,128)(2,1)S(1)}, u32[]{:S(2)}, u32[]{:S(2)}) collective-permute-start(bf16[32,3584]{1,0:T(8,128)(2,1)S(1)} %get-tuple-element.232), channel_id=1, source_target_pairs={{0,12},{1,13},{2,14},{3,15},{4,0},{5,1},{6,2},{7,3},{8,4},{9,5},{1... | collective-permute-start | bytes 688136 | tf_op jit(solution)/shard_map/rs_fa/ppermute | solution.py:124
  60.0 17.8 %collective-permute-start.12 = (bf16[64,3584]{1,0:T(8,128)(2,1)}, bf16[64,3584]{1,0:T(8,128)(2,1)}, u32[]{:S(2)}, u32[]{:S(2)}) collective-permute-start(bf16[64,3584]{1,0:T(8,128)(2,1)} %add_convert_fusion), channel_id=1, source_target_pairs={{0,2},{1,3},{2,0},{3,1},{4,6},{5,7},{6,4},{7,5},{8,10},{9,11},{10,... | collective-permute-start | bytes 1376264 | tf_op jit(solution)/shard_map/rs_xl/ppermute | solution.py:124
  63.5 14.3 %collective-permute-start.16 = (bf16[64,3584]{1,0:T(8,128)(2,1)}, bf16[64,3584]{1,0:T(8,128)(2,1)}, u32[]{:S(2)}, u32[]{:S(2)}) collective-permute-start(bf16[64,3584]{1,0:T(8,128)(2,1)} %pad_maximum_fusion.4), channel_id=1, source_target_pairs={{0,12},{1,13},{2,14},{3,15},{4,0},{5,1},{6,2},{7,3},{8,4},{9,5},{1... | collective-permute-start | bytes 1376264 | tf_op jit(solution)/shard_map/rs_al/ppermute | solution.py:124
  65.9 11.9 %collective-permute-start.15 = (bf16[64,3584]{1,0:T(8,128)(2,1)}, bf16[64,3584]{1,0:T(8,128)(2,1)}, u32[]{:S(2)}, u32[]{:S(2)}) collective-permute-start(bf16[64,3584]{1,0:T(8,128)(2,1)} %pad_maximum_fusion.3), channel_id=1, source_target_pairs={{0,4},{1,5},{2,6},{3,7},{4,8},{5,9},{6,10},{7,11},{8,12},{9,13},{1... | collective-permute-start | bytes 1376264 | tf_op jit(solution)/shard_map/rs_bl/ppermute | solution.py:124
  65.9 5.9 %collective-permute-start.17 = (f32[1,128]{1,0:T(1,128)S(1)}, f32[1,128]{1,0:T(1,128)S(1)}, u32[]{:S(2)}, u32[]{:S(2)}) collective-permute-start(f32[1,128]{1,0:T(1,128)S(1)} %add.210), channel_id=1, source_target_pairs={{0,2},{1,3},{2,0},{3,1},{4,6},{5,7},{6,4},{7,5},{8,10},{9,11},{10,... | collective-permute-start | bytes 1544 | tf_op jit(solution)/shard_map/squares/ppermute | solution.py:124
  73.0 18.3 %all-to-all-start.1 = ((bf16[8,128,512]{2,1,0:T(8,128)(2,1)}), bf16[8,128,512]{2,1,0:T(8,128)(2,1)S(1)}, u32[]{:S(2)}, u32[]{:S(2)}) async-start(bf16[8,128,512]{2,1,0:T(8,128)(2,1)} %broadcast_in_dim.21), calls=%async_computation.1 | async-start | bytes 2097152 | tf_op jit(solution)/shard_map/normed_rows/all_to_all | solution.py:230
  82.0 20.3 %collective-permute-start.19 = (bf16[64,3584]{1,0:T(8,128)(2,1)}, bf16[64,3584]{1,0:T(8,128)(2,1)}, u32[]{:S(2)}, u32[]{:S(2)}) collective-permute-start(bf16[64,3584]{1,0:T(8,128)(2,1)} %get-tuple-element.156), channel_id=1, source_target_pairs={{0,12},{1,13},{2,14},{3,15},{4,0},{5,1},{6,2},{7,3},{8,4},{9,5},{1... | collective-permute-start | bytes 1376264 | tf_op jit(solution)/shard_map/ag_up_a/ppermute | solution.py:124
  85.3 17.0 %collective-permute-start.20 = (bf16[64,3584]{1,0:T(8,128)(2,1)}, bf16[64,3584]{1,0:T(8,128)(2,1)}, u32[]{:S(2)}, u32[]{:S(2)}) collective-permute-start(bf16[64,3584]{1,0:T(8,128)(2,1)} %get-tuple-element.156), channel_id=1, source_target_pairs={{0,4},{1,5},{2,6},{3,7},{4,8},{5,9},{6,10},{7,11},{8,12},{9,13},{1... | collective-permute-start | bytes 1376264 | tf_op jit(solution)/shard_map/ag_up_b/ppermute | solution.py:124
  85.3 17.0 %collective-permute-start.18 = (bf16[64,3584]{1,0:T(8,128)(2,1)}, bf16[64,3584]{1,0:T(8,128)(2,1)}, u32[]{:S(2)}, u32[]{:S(2)}) collective-permute-start(bf16[64,3584]{1,0:T(8,128)(2,1)} %get-tuple-element.155), channel_id=1, source_target_pairs={{0,4},{1,5},{2,6},{3,7},{4,8},{5,9},{6,10},{7,11},{8,12},{9,13},{1... | collective-permute-start | bytes 1376264 | tf_op jit(solution)/shard_map/ag_gate_b/ppermute | solution.py:124
  85.3 17.0 %collective-permute-start.21 = (bf16[64,3584]{1,0:T(8,128)(2,1)}, bf16[64,3584]{1,0:T(8,128)(2,1)}, u32[]{:S(2)}, u32[]{:S(2)}) collective-permute-start(bf16[64,3584]{1,0:T(8,128)(2,1)} %get-tuple-element.155), channel_id=1, source_target_pairs={{0,12},{1,13},{2,14},{3,15},{4,0},{5,1},{6,2},{7,3},{8,4},{9,5},{1... | collective-permute-start | bytes 1376264 | tf_op jit(solution)/shard_map/ag_gate_a/ppermute | solution.py:124
  88.5 20.6 %collective-permute-start.22 = (bf16[128,3584]{1,0:T(8,128)(2,1)S(1)}, bf16[128,3584]{1,0:T(8,128)(2,1)S(1)}, u32[]{:S(2)}, u32[]{:S(2)}) collective-permute-start(bf16[128,3584]{1,0:T(8,128)(2,1)S(1)} %pad_maximum_fusion.2.refs_0_.refs_10_.refs_16_), channel_id=1, source_target_pairs={{0,2},{1,3},{2,0},{3,1},{4,6},{5,7},{6,4},{7,5},{8,10},{9,11},{10,... | collective-permute-start | bytes 2752520 | tf_op jit(solution)/shard_map/ag_x/ppermute | solution.py:124
  109.1 14.4 %collective-permute-start.23 = (bf16[64,3584]{1,0:T(8,128)(2,1)}, bf16[64,3584]{1,0:T(8,128)(2,1)S(1)}, u32[]{:S(2)}, u32[]{:S(2)}) collective-permute-start(bf16[64,3584]{1,0:T(8,128)(2,1)} %collective-permute-done.18.refs_3_), channel_id=1, source_target_pairs={{0,4},{1,5},{2,6},{3,7},{4,8},{5,9},{6,10},{7,11},{8,12},{9,13},{1... | collective-permute-start | bytes 1376264 | tf_op jit(solution)/shard_map/ag_gate_f/ppermute | solution.py:124
  109.1 14.4 %collective-permute-start.24 = (bf16[64,3584]{1,0:T(8,128)(2,1)}, bf16[64,3584]{1,0:T(8,128)(2,1)}, u32[]{:S(2)}, u32[]{:S(2)}) collective-permute-start(bf16[64,3584]{1,0:T(8,128)(2,1)} %collective-permute-done.19.refs_11_.refs_17_), channel_id=1, source_target_pairs={{0,12},{1,13},{2,14},{3,15},{4,0},{5,1},{6,2},{7,3},{8,4},{9,5},{1... | collective-permute-start | bytes 1376264 | tf_op jit(solution)/shard_map/ag_up_f/ppermute | solution.py:124
  112.3 11.6 %collective-permute-start.27 = (bf16[64,3584]{1,0:T(8,128)(2,1)}, bf16[64,3584]{1,0:T(8,128)(2,1)S(1)}, u32[]{:S(2)}, u32[]{:S(2)}) collective-permute-start(bf16[64,3584]{1,0:T(8,128)(2,1)} %collective-permute-done.19.refs_11_.refs_17_), channel_id=1, source_target_pairs={{0,1},{1,0},{2,3},{3,2},{4,5},{5,4},{6,7},{7,6},{8,9},{9,8},{10,11... | collective-permute-start | bytes 1376264 | tf_op jit(solution)/shard_map/ag_core/ppermute | solution.py:124
  112.4 14.5 %collective-permute-start.26 = (bf16[128,3584]{1,0:T(8,128)(2,1)S(1)}, bf16[128,3584]{1,0:T(8,128)(2,1)S(1)}, u32[]{:S(2)}, u32[]{:S(2)}) collective-permute-start(bf16[128,3584]{1,0:T(8,128)(2,1)S(1)} %pad_maximum_fusion.2.refs_0_.refs_10_.refs_16_), channel_id=1, source_target_pairs={{0,1},{1,0},{2,3},{3,2},{4,5},{5,4},{6,7},{7,6},{8,9},{9,8},{10,11... | collective-permute-start | bytes 2752520 | tf_op jit(solution)/shard_map/ag_core/ppermute | solution.py:124
  112.9 13.9 %collective-permute-start.31 = (bf16[128,3584]{1,0:T(8,128)(2,1)S(1)}, bf16[128,3584]{1,0:T(8,128)(2,1)S(1)}, u32[]{:S(2)}, u32[]{:S(2)}) collective-permute-start(bf16[128,3584]{1,0:T(8,128)(2,1)S(1)} %collective-permute-done.22.refs_8_.refs_18_.refs_24_), channel_id=1, source_target_pairs={{0,1},{1,0},{2,3},{3,2},{4,5},{5,4},{6,7},{7,6},{8,9},{9,8},{10,11... | collective-permute-start | bytes 2752520 | tf_op jit(solution)/shard_map/ag_core/ppermute | solution.py:124
  127.8 27.6 %collective-permute-start.32 = (bf16[128,3584]{1,0:T(8,128)(2,1)S(1)}, bf16[128,3584]{1,0:T(8,128)(2,1)S(1)}, u32[]{:S(2)}, u32[]{:S(2)}) collective-permute-start(bf16[128,3584]{1,0:T(8,128)(2,1)S(1)} %collective-permute-done.22.refs_8_.refs_18_.refs_24_), channel_id=1, source_target_pairs={{0,4},{1,5},{2,6},{3,7},{4,8},{5,9},{6,10},{7,11},{8,12},{9,13},{1... | collective-permute-start | bytes 2752520 | tf_op jit(solution)/shard_map/ag_xb/ppermute | solution.py:124
  128.1 27.3 %collective-permute-start.33 = (bf16[128,3584]{1,0:T(8,128)(2,1)S(1)}, bf16[128,3584]{1,0:T(8,128)(2,1)S(1)}, u32[]{:S(2)}, u32[]{:S(2)}) collective-permute-start(bf16[128,3584]{1,0:T(8,128)(2,1)S(1)} %collective-permute-done.22.refs_8_.refs_18_.refs_24_), channel_id=1, source_target_pairs={{0,12},{1,13},{2,14},{3,15},{4,0},{5,1},{6,2},{7,3},{8,4},{9,5},{1... | collective-permute-start | bytes 2752520 | tf_op jit(solution)/shard_map/ag_xa/ppermute | solution.py:124
  131.0 17.5 %collective-permute-start.34 = (bf16[64,3584]{1,0:T(8,128)(2,1)S(1)}, bf16[64,3584]{1,0:T(8,128)(2,1)S(1)}, u32[]{:S(2)}, u32[]{:S(2)}) collective-permute-start(bf16[64,3584]{1,0:T(8,128)(2,1)S(1)} %collective-permute-done.23.refs_2_), channel_id=1, source_target_pairs={{0,2},{1,3},{2,0},{3,1},{4,6},{5,7},{6,4},{7,5},{8,10},{9,11},{10,... | collective-permute-start | bytes 1376264 | tf_op jit(solution)/shard_map/ag_gate_xf/ppermute | solution.py:124
  131.2 24.2 %collective-permute-start.35 = (bf16[64,3584]{1,0:T(8,128)(2,1)}, bf16[64,3584]{1,0:T(8,128)(2,1)}, u32[]{:S(2)}, u32[]{:S(2)}) collective-permute-start(bf16[64,3584]{1,0:T(8,128)(2,1)} %collective-permute-done.24.refs_12_.refs_18_), channel_id=1, source_target_pairs={{0,2},{1,3},{2,0},{3,1},{4,6},{5,7},{6,4},{7,5},{8,10},{9,11},{10,... | collective-permute-start | bytes 1376264 | tf_op jit(solution)/shard_map/ag_up_xf/ppermute | solution.py:124
  155.4 8.3 %collective-permute-start.38 = (bf16[128,3584]{1,0:T(8,128)(2,1)S(1)}, bf16[128,3584]{1,0:T(8,128)(2,1)S(1)}, u32[]{:S(2)}, u32[]{:S(2)}) collective-permute-start(bf16[128,3584]{1,0:T(8,128)(2,1)S(1)} %collective-permute-done.33.refs_0_.refs_6_.refs_9_.refs_25_), channel_id=1, source_target_pairs={{0,1},{1,0},{2,3},{3,2},{4,5},{5,4},{6,7},{7,6},{8,9},{9,8},{10,11... | collective-permute-start | bytes 2752520 | tf_op jit(solution)/shard_map/ag_core/ppermute | solution.py:124
  155.5 8.3 %collective-permute-start.40 = (bf16[128,3584]{1,0:T(8,128)(2,1)S(1)}, bf16[128,3584]{1,0:T(8,128)(2,1)}, u32[]{:S(2)}, u32[]{:S(2)}) collective-permute-start(bf16[128,3584]{1,0:T(8,128)(2,1)S(1)} %collective-permute-done.32.refs_2_.refs_8_.refs_11_.refs_27_), channel_id=1, source_target_pairs={{0,1},{1,0},{2,3},{3,2},{4,5},{5,4},{6,7},{7,6},{8,9},{9,8},{10,11... | collective-permute-start | bytes 2752520 | tf_op jit(solution)/shard_map/ag_core/ppermute | solution.py:124
  156.0 7.7 %collective-permute-start.39 = (bf16[64,3584]{1,0:T(8,128)(2,1)S(1)}, bf16[64,3584]{1,0:T(8,128)(2,1)}, u32[]{:S(2)}, u32[]{:S(2)}) collective-permute-start(bf16[64,3584]{1,0:T(8,128)(2,1)S(1)} %collective-permute-done.34.refs_1_.refs_10_), channel_id=1, source_target_pairs={{0,1},{1,0},{2,3},{3,2},{4,5},{5,4},{6,7},{7,6},{8,9},{9,8},{10,11... | collective-permute-start | bytes 1376264 | tf_op jit(solution)/shard_map/ag_core/ppermute | solution.py:124
  156.1 7.6 %collective-permute-start.41 = (bf16[64,3584]{1,0:T(8,128)(2,1)}, bf16[64,3584]{1,0:T(8,128)(2,1)}, u32[]{:S(2)}, u32[]{:S(2)}) collective-permute-start(bf16[64,3584]{1,0:T(8,128)(2,1)} %collective-permute-done.35.refs_7_.refs_26_), channel_id=1, source_target_pairs={{0,1},{1,0},{2,3},{3,2},{4,5},{5,4},{6,7},{7,6},{8,9},{9,8},{10,11... | collective-permute-start | bytes 1376264 | tf_op jit(solution)/shard_map/ag_core/ppermute | solution.py:124
  158.3 47.7 %all-to-all-start.2 = ((bf16[8,64,2688]{2,1,0:T(8,128)(2,1)}), bf16[8,64,2688]{2,1,0:T(8,128)(2,1)}, u32[]{:S(2)}, u32[]{:S(2)}) async-start(bf16[8,64,2688]{2,1,0:T(8,128)(2,1)} %broadcast_in_dim.51), calls=%async_computation.2 | async-start | bytes 5505024 | tf_op jit(solution)/shard_map/hid_b/all_to_all | solution.py:179
  174.0 17.6 %collective-permute-start.44 = (bf16[2,2,64,512]{3,2,1,0:T(8,128)(2,1)S(1)}, bf16[2,2,64,512]{3,2,1,0:T(8,128)(2,1)S(1)}, u32[]{:S(2)}, u32[]{:S(2)}) collective-permute-start(bf16[2,2,64,512]{3,2,1,0:T(8,128)(2,1)S(1)} %get-tuple-element.204), channel_id=1, source_target_pairs={{0,96},{16,112},{32,0},{48,16},{64,32},{80,48},{96,64},{112,80},{1... | collective-permute-start | bytes 786440 | tf_op jit(solution)/shard_map/dn_y/ppermute | solution.py:133
  176.6 15.0 %collective-permute-start.43 = (bf16[2,2,64,512]{3,2,1,0:T(8,128)(2,1)S(1)}, bf16[2,2,64,512]{3,2,1,0:T(8,128)(2,1)S(1)}, u32[]{:S(2)}, u32[]{:S(2)}) collective-permute-start(bf16[2,2,64,512]{3,2,1,0:T(8,128)(2,1)S(1)} %get-tuple-element.203), channel_id=1, source_target_pairs={{0,64},{16,80},{32,96},{48,112},{64,0},{80,16},{96,32},{112,48},{1... | collective-permute-start | bytes 786440 | tf_op jit(solution)/shard_map/dn_y/ppermute | solution.py:133
  177.5 14.2 %collective-permute-start.42 = (bf16[2,2,64,512]{3,2,1,0:T(8,128)(2,1)S(1)}, bf16[2,2,64,512]{3,2,1,0:T(8,128)(2,1)S(1)}, u32[]{:S(2)}, u32[]{:S(2)}) collective-permute-start(bf16[2,2,64,512]{3,2,1,0:T(8,128)(2,1)S(1)} %get-tuple-element.202), channel_id=1, source_target_pairs={{0,32},{16,48},{32,64},{48,80},{64,96},{80,112},{96,0},{112,16},{1... | collective-permute-start | bytes 786440 | tf_op jit(solution)/shard_map/dn_y/ppermute | solution.py:133
  191.9 5.2 %collective-permute-start.45 = (bf16[2,64,512]{2,1,0:T(8,128)(2,1)S(1)}, bf16[2,64,512]{2,1,0:T(8,128)(2,1)S(1)}, u32[]{:S(2)}, u32[]{:S(2)}) collective-permute-start(bf16[2,64,512]{2,1,0:T(8,128)(2,1)S(1)} %fusion.30), channel_id=1, source_target_pairs={{0,16},{16,0},{32,48},{48,32},{64,80},{80,64},{96,112},{112,96},{1... | collective-permute-start | bytes 393224 | tf_op jit(solution)/shard_map/dn_xl/ppermute | solution.py:133
  198.5 7.5 %collective-permute-start.48 = (f32[1,512]{1,0:T(1,128)S(1)}, f32[1,512]{1,0:T(1,128)S(1)}, u32[]{:S(2)}, u32[]{:S(2)}) collective-permute-start(f32[1,512]{1,0:T(1,128)S(1)} %bitcast.159), channel_id=1, source_target_pairs={{0,16},{16,0},{32,48},{48,32},{64,80},{80,64},{96,112},{112,96},{1... | collective-permute-start | bytes 6152 | tf_op jit(solution)/shard_map/gain/ppermute | solution.py:133
  200.9 5.0 %collective-permute-start.47 = (f32[1,128]{1,0:T(1,128)S(1)}, f32[1,128]{1,0:T(1,128)S(1)}, u32[]{:S(2)}, u32[]{:S(2)}) collective-permute-start(f32[1,128]{1,0:T(1,128)S(1)} %add.239), channel_id=1, source_target_pairs={{0,2},{1,3},{2,0},{3,1},{4,6},{5,7},{6,4},{7,5},{8,10},{9,11},{10,... | collective-permute-start | bytes 1544 | tf_op jit(solution)/shard_map/proj/ppermute | solution.py:124
  206.0 5.4 %collective-permute-start.51 = (bf16[512,2688]{1,0:T(8,128)(2,1)}, bf16[512,2688]{1,0:T(8,128)(2,1)S(1)}, u32[]{:S(2)}, u32[]{:S(2)}) collective-permute-start(bf16[512,2688]{1,0:T(8,128)(2,1)} %bitcast.62.left), channel_id=1, source_target_pairs={{0,1},{1,0},{2,3},{3,2},{4,5},{5,4},{6,7},{7,6},{8,9},{9,8},{10,11... | collective-permute-start | bytes 8257544 | tf_op jit(solution)/shard_map/hid_core/ppermute | solution.py:124
  206.1 4.9 %collective-permute-start.50 = (f32[1,512]{1,0:T(1,128)S(1)}, f32[1,512]{1,0:T(1,128)S(1)}, u32[]{:S(2)}, u32[]{:S(2)}) collective-permute-start(f32[1,512]{1,0:T(1,128)S(1)} %add.241), channel_id=1, source_target_pairs={{0,32},{16,48},{32,0},{48,16},{64,96},{80,112},{96,64},{112,80},{1... | collective-permute-start | bytes 6152 | tf_op jit(solution)/shard_map/gain/ppermute | solution.py:173
  211.4 12.5 %collective-permute-start.52 = (f32[1,128]{1,0:T(1,128)S(1)}, f32[1,128]{1,0:T(1,128)S(1)}, u32[]{:S(2)}, u32[]{:S(2)}) collective-permute-start(f32[1,128]{1,0:T(1,128)S(1)} %add.242), channel_id=1, source_target_pairs={{0,8},{1,9},{2,10},{3,11},{4,12},{5,13},{6,14},{7,15},{8,0},{9,1},... | collective-permute-start | bytes 1544 | tf_op jit(solution)/shard_map/proj/ppermute | solution.py:124
  214.1 10.6 %collective-permute-start.53 = (f32[1,512]{1,0:T(1,128)S(1)}, f32[1,512]{1,0:T(1,128)S(1)}, u32[]{:S(2)}, u32[]{:S(2)}) collective-permute-start(f32[1,512]{1,0:T(1,128)S(1)} %add.243), channel_id=1, source_target_pairs={{0,64},{16,80},{32,96},{48,112},{64,0},{80,16},{96,32},{112,48},{1... | collective-permute-start | bytes 6152 | tf_op jit(solution)/shard_map/gain/ppermute | solution.py:133
  (43 other events, 303.4 us)

commit v3 on v2

--- a/solution.py
+++ b/solution.py
@@ -174,9 +174,9 @@
 
     def gather_hidden(x, name):
         groups = [[chip * NC + core for chip in range(NZ * NX)] for core in range(NC)]
-        copies = jnp.broadcast_to(x[None], (NZ * NX, *x.shape))
+        copies = x if x.ndim == 3 else jnp.broadcast_to(x[None], (NZ * NX, *x.shape))
         with jax.named_scope(name):
-            return lax.all_to_all(copies, "col", 0, 0, axis_index_groups=groups, tiled=True).reshape(-1, x.shape[1])
+            return lax.all_to_all(copies, "col", 0, 0, axis_index_groups=groups, tiled=True).reshape(-1, x.shape[-1])
 
     out_xl = row_to(out_grad, "out_xl", dl=1)
     w_down_other = col_to(w_down, "w_down", dc=1)
@@ -195,7 +195,8 @@
     hid_a = gather_hidden(hidden_a, "hid_a")
     squares = squares + neighbour(squares, "squares")
     out_mine, out_theirs = assemble([pair] + out_y)
-    out_mine, out_theirs, squares = phase(out_mine, out_theirs, squares)
+    hid_copies = jnp.broadcast_to(hidden_b[None], (NZ * NX, *hidden_b.shape))
+    out_mine, out_theirs, squares, hid_copies = phase(out_mine, out_theirs, squares, hid_copies)
 
     out_other = col_to(out_theirs, "out_core", dc=1)
     far0, far1, far2, far3 = hidden_units(
@@ -257,15 +258,15 @@
     for at, one in enumerate(pairs):
         normed_all = lax.dynamic_update_slice(normed_all, one, (0, 0, (at - z) % NZ, 0, 0))
     normed_t = normed_all.reshape(-1, feats).T
-    gate_b, up_a, up_b, gate_a, both_x, both, hid_a, normed_t, out_down = phase(
-        gate_b, up_a, up_b, gate_a, both_x, both, hid_a, normed_t, out_down
+    swapped = [col_to(piece, "ag_core", dc=1) for piece in (up_a, gate_a, gate_b, up_b)]
+    gate_b, up_a, up_b, gate_a, both_x, both, hid_a, normed_t, out_down, *swapped = phase(
+        gate_b, up_a, up_b, gate_a, both_x, both, hid_a, normed_t, out_down, *swapped
     )
 
     gate_f = col_to(gate_b, "ag_gate_f", dz=1)
     up_f = col_to(up_a, "ag_up_f", dz=-1)
     hid_a_other = col_to(hid_a, "hid_core", dc=1)
-    swap_late = phase(both, up_a, gate_a, gate_b, up_b, both_x, hid_a_other)
-    swapped = [col_to(piece, "ag_core", dc=1) for piece in swap_late[:6]]
+    swapped = [col_to(both, "ag_core", dc=1), *swapped, col_to(both_x, "ag_core", dc=1)]
     gate_f, up_f, both, gate_b, up_a, up_b, gate_a, both_x, normed_t, hid_a, hid_a_other, *swapped = phase(
         gate_f, up_f, both, gate_b, up_a, up_b, gate_a, both_x, normed_t, hid_a, hid_a_other, *swapped
     )
@@ -292,10 +293,10 @@
 
     term_first, hid_a = phase(term_first, hid_a)
     down_a = down_grads(hid_a, hid_a_other, out_down, width, 0, None, 1)
-    both_xb, both_xa, gate_xf, up_xf, term_first, hidden_b, down_a = phase(
-        both_xb, both_xa, gate_xf, up_xf, term_first, hidden_b, down_a
-    )
-    hid_b = gather_hidden(hidden_b, "hid_b")
+    both_xb, both_xa, gate_xf, up_xf, term_first, hid_copies, down_a = phase(
+        both_xb, both_xa, gate_xf, up_xf, term_first, hid_copies, down_a
+    )
+    hid_b = gather_hidden(hid_copies, "hid_b")
 
     far_ones = [both_xa, gate_xf, up_xf, both_xb]
     swapped_far = [col_to(piece, "ag_core", dc=1) for piece in far_ones]

time: 226 us -> 224 us (level)
  waiting for transfers between devices: 68 us -> 65 us
  starting transfers between devices: 75.5 us -> 77.9 us
    ppermute x41, starting transfers between devices: 38 us -> 41.3 us  [col_to(): return lax.ppermute(x, 'col', pairs)]
    unnamed x64 -> x58, local copies, waits for them, and re-layouts: 3.84 us -> 5.08 us
  transfers between devices with their start and end apart: 57 -> 57, of which waited for: 20 -> 17; matrix products, arithmetic and copies ran while one was open for 10% -> 9% of each run, Pallas kernels for 23% -> 23%
where the time goes in v3:
time: 224 us; the launch traced here: 223 us
  starting transfers between devices  77.9 us (35%)
  waiting for transfers between devices  65 us (29%)
  Pallas kernels  52.4 us (23%)
  other arithmetic  14 us (6%)
  local copies, waits for them, and re-layouts  12.4 us (6%)
    ppermute x41, waiting for transfers between devices, col_to(): return lax.ppermute(x, 'col', pairs)  54.3 us
    pallas_call x5, Pallas kernels, kernel_call(): pl.pallas_call(body, grid=(steps,), in_specs=in_specs, out_specs=out_spec...  41.7 us
    ppermute x41, starting transfers between devices, col_to(): return lax.ppermute(x, 'col', pairs)  41.3 us
    ppermute x10, starting transfers between devices, row_to(): return lax.ppermute(x, 'row', pairs)  15.5 us
    all_to_all x2, starting transfers between devices, gather_hidden(): lax.all_to_all(copies, 'col', 0, 0, axis_index_groups=groups, tiled=True)  13.7 us
    pallas_call x2, Pallas kernels, down_grads(): pl.pallas_call(body, grid=(steps,), in_specs=specs + [pl.BlockSpec(memory...  10.7 us
    ppermute x10, waiting for transfers between devices, row_to(): return lax.ppermute(x, 'row', pairs)  7.68 us
    unnamed x58, local copies, waits for them, and re-layouts  5.08 us
  transfers between devices with their start and end apart: 57, of which 17 were waited for; matrix products, arithmetic and copies ran while one was open for 9% of the time, Pallas kernels for 23%

profile of v3, /device:TPU:6, one launch (start us, length us, event | category | flops | bytes accessed | tf_op | source)
XLA Modules:
  0.0 223.3 jit_solution(14517187216619201641)
XLA Ops:
  2.9 1.4 fusion
  4.5 2.6 %collective-permute-done.2 = f32[1,128]{1,0:T(1,128)S(1)} collective-permute-done((f32[1,128]{1,0:T(1,128)S(1)}, f32[1,128]{1,0:T(1,128)S(1)}, u32[]{:S(2)}, u32[]{:S(2)}) %collective-permute-start.2) | collective-permute-done | bytes 544 | tf_op jit(solution)/shard_map/squares/ppermute | solution.py:124
  7.5 3.0 %collective-permute-start.3 = (bf16[2,2,1,64,512]{4,3,0,2,1:T(8,128)(2,1)S(1)}, bf16[2,2,1,64,512]{4,3,0,2,1:T(8,128)(2,1)S(1)}, u32[]{:S(2)}, u32[]{:S(2)}) collective-permute-start(bf16[2,2,1,64,512]{4,3,0,2,1:T(8,128)(2,1)S(1)} %fusion.12), channel_id=1, source_target_pairs={{0,96},{16,112},{32,0},{48,16},{64,32},{80,48},{96,64},{112,80},{1... | collective-permute-start | bytes 786440 | tf_op jit(solution)/shard_map/out_y/ppermute | solution.py:133
  12.1 1.9 collective-permute-start.6
  15.2 7.8 %all-to-all-start = ((bf16[8,64,896]{2,1,0:T(8,128)(2,1)}), bf16[8,64,896]{2,1,0:T(8,128)(2,1)S(1)}, u32[]{:S(2)}, u32[]{:S(2)}) async-start(bf16[8,64,896]{2,1,0:T(8,128)(2,1)} %broadcast_in_dim.20), calls=%async_computation | async-start | bytes 1835008 | tf_op jit(solution)/shard_map/hid_a/all_to_all | solution.py:179
  23.1 2.6 %collective-permute-done.5 = bf16[2,2,1,64,512]{4,3,0,2,1:T(8,128)(2,1)S(1)} collective-permute-done((bf16[2,2,1,64,512]{4,3,0,2,1:T(8,128)(2,1)S(1)}, bf16[2,2,1,64,512]{4,3,0,2,1:T(8,128)(2,1)S(1)}, u32[]{:S(2)}, u32[]{:S(2)}) %collective-permute-start.5) | collective-permute-done | bytes 262176 | tf_op jit(solution)/shard_map/out_y/ppermute | solution.py:133
  25.7 1.7 broadcast_in_dim.19
  27.5 1.9 collective-permute-done.7.lo
  30.1 5.5 %hidden_units.2 = (f32[64,3584]{1,0:T(8,128)}, bf16[64,3584]{1,0:T(8,128)(2,1)}, bf16[64,3584]{1,0:T(8,128)(2,1)}, bf16[64,3584]{1,0:T(8,128)(2,1)}) custom-call(bf16[512,512]{1,0:T(8,128)(2,1)} %bitcast.138, bf16[512,512]{1,0:T(8,128)(2,1)} %copy-done.11, bf16[3584,512]{1,0:T(8,128)(2,1)} %w.3, bf16[3584,512]{1,0:T(8,128)(2,1)} %collective-permute-done.1.wo), custom_call_target="tpu_custom_call" | custom-call | tf_op jit(solution)/shard_map/hidden_units/pallas_call | solution.py:19
  35.7 2.4 %collective-permute-start.8 = (bf16[64,3584]{1,0:T(8,128)(2,1)}, bf16[64,3584]{1,0:T(8,128)(2,1)S(1)}, u32[]{:S(2)}, u32[]{:S(2)}) collective-permute-start(bf16[64,3584]{1,0:T(8,128)(2,1)} %get-tuple-element.126), channel_id=1, source_target_pairs={{0,2},{1,3},{2,0},{3,1},{4,6},{5,7},{6,4},{7,5},{8,10},{9,11},{10,... | collective-permute-start | bytes 1376264 | tf_op jit(solution)/shard_map/rs_x/ppermute | solution.py:124
  39.1 2.2 collective-permute-start.10
  41.3 5.7 %hidden_units.3 = (f32[64,3584]{1,0:T(8,128)}, f32[64,3584]{1,0:T(8,128)}, f32[64,3584]{1,0:T(8,128)}, f32[64,3584]{1,0:T(8,128)}) custom-call(bf16[512,512]{1,0:T(8,128)(2,1)} %bitcast.139, bf16[512,512]{1,0:T(8,128)(2,1)} %copy-done.11, bf16[3584,512]{1,0:T(8,128)(2,1)} %w.3, bf16[3584,512]{1,0:T(8,128)(2,1)} %collective-permute-done.1.wo), custom_call_target="tpu_custom_call" | custom-call | tf_op jit(solution)/shard_map/hidden_units/pallas_call | solution.py:19
  47.0 1.9 collective-permute-start.11
  48.8 4.3 %collective-permute-done.11 = f32[1,128]{1,0:T(1,128)S(1)} collective-permute-done((f32[1,128]{1,0:T(1,128)S(1)}, f32[1,128]{1,0:T(1,128)S(1)}, u32[]{:S(2)}, u32[]{:S(2)}) %collective-permute-start.11) | collective-permute-done | bytes 544 | tf_op jit(solution)/shard_map/squares/ppermute | solution.py:124
  54.0 1.4 add_convert_fusion.2
  56.7 2.1 collective-permute-start.14
  58.8 2.1 add_convert_fusion
  61.0 2.2 collective-permute-start.12
  64.9 2.0 collective-permute-start.16
  66.9 2.1 collective-permute-start.17
  69.0 4.4 %collective-permute-done.17 = f32[1,128]{1,0:T(1,128)S(1)} collective-permute-done((f32[1,128]{1,0:T(1,128)S(1)}, f32[1,128]{1,0:T(1,128)S(1)}, u32[]{:S(2)}, u32[]{:S(2)}) %collective-permute-start.17) | collective-permute-done | bytes 544 | tf_op jit(solution)/shard_map/squares/ppermute | solution.py:124
  74.6 3.5 %all-to-all-start.1 = ((bf16[8,128,512]{2,1,0:T(8,128)(2,1)}), bf16[8,128,512]{2,1,0:T(8,128)(2,1)S(1)}, u32[]{:S(2)}, u32[]{:S(2)}) async-start(bf16[8,128,512]{2,1,0:T(8,128)(2,1)} %broadcast_in_dim.22), calls=%async_computation.1 | async-start | bytes 2097152 | tf_op jit(solution)/shard_map/normed_rows/all_to_all | solution.py:231
  78.2 2.0 multiply_convert_fusion
  80.2 2.3 %collective-permute-start.19 = (bf16[64,3584]{1,0:T(8,128)(2,1)S(1)}, bf16[64,3584]{1,0:T(8,128)(2,1)}, u32[]{:S(2)}, u32[]{:S(2)}) collective-permute-start(bf16[64,3584]{1,0:T(8,128)(2,1)S(1)} %get-tuple-element.156), channel_id=1, source_target_pairs={{0,12},{1,13},{2,14},{3,15},{4,0},{5,1},{6,2},{7,3},{8,4},{9,5},{1... | collective-permute-start | bytes 1376264 | tf_op jit(solution)/shard_map/ag_up_a/ppermute | solution.py:124
  82.5 3.3 %collective-permute-start.21 = (bf16[64,3584]{1,0:T(8,128)(2,1)S(1)}, bf16[64,3584]{1,0:T(8,128)(2,1)}, u32[]{:S(2)}, u32[]{:S(2)}) collective-permute-start(bf16[64,3584]{1,0:T(8,128)(2,1)S(1)} %get-tuple-element.155), channel_id=1, source_target_pairs={{0,12},{1,13},{2,14},{3,15},{4,0},{5,1},{6,2},{7,3},{8,4},{9,5},{1... | collective-permute-start | bytes 1376264 | tf_op jit(solution)/shard_map/ag_gate_a/ppermute | solution.py:124
  85.8 3.2 %collective-permute-start.22 = (bf16[128,3584]{1,0:T(8,128)(2,1)S(1)}, bf16[128,3584]{1,0:T(8,128)(2,1)S(1)}, u32[]{:S(2)}, u32[]{:S(2)}) collective-permute-start(bf16[128,3584]{1,0:T(8,128)(2,1)S(1)} %pad_maximum_fusion.2.refs_0_.refs_10_.refs_16_), channel_id=1, source_target_pairs={{0,2},{1,3},{2,0},{3,1},{4,6},{5,7},{6,4},{7,5},{8,10},{9,11},{10,... | collective-permute-start | bytes 2752520 | tf_op jit(solution)/shard_map/ag_x/ppermute | solution.py:124
  90.9 3.0 %collective-permute-done.19.refs_11_.refs_17_ = bf16[64,3584]{1,0:T(8,128)(2,1)} collective-permute-done((bf16[64,3584]{1,0:T(8,128)(2,1)S(1)}, bf16[64,3584]{1,0:T(8,128)(2,1)}, u32[]{:S(2)}, u32[]{:S(2)}) %collective-permute-start.19) | collective-permute-done | bytes 458784 | tf_op jit(solution)/shard_map/ag_up_a/ppermute | solution.py:124
  93.9 6.0 %collective-permute-done.21.refs_1_ = bf16[64,3584]{1,0:T(8,128)(2,1)} collective-permute-done((bf16[64,3584]{1,0:T(8,128)(2,1)S(1)}, bf16[64,3584]{1,0:T(8,128)(2,1)}, u32[]{:S(2)}, u32[]{:S(2)}) %collective-permute-start.21) | collective-permute-done | bytes 458784 | tf_op jit(solution)/shard_map/ag_gate_a/ppermute | solution.py:124
  99.9 2.6 %collective-permute-done.18.refs_3_ = bf16[64,3584]{1,0:T(8,128)(2,1)} collective-permute-done((bf16[64,3584]{1,0:T(8,128)(2,1)S(1)}, bf16[64,3584]{1,0:T(8,128)(2,1)}, u32[]{:S(2)}, u32[]{:S(2)}) %collective-permute-start.18) | collective-permute-done | bytes 458784 | tf_op jit(solution)/shard_map/ag_gate_b/ppermute | solution.py:124
  105.0 5.7 %collective-permute-done.22.refs_8_.refs_18_.refs_24_ = bf16[128,3584]{1,0:T(8,128)(2,1)S(1)} collective-permute-done((bf16[128,3584]{1,0:T(8,128)(2,1)S(1)}, bf16[128,3584]{1,0:T(8,128)(2,1)S(1)}, u32[]{:S(2)}, u32[]{:S(2)}) %collective-permute-start.22) | collective-permute-done | bytes 917536 | tf_op jit(solution)/shard_map/ag_x/ppermute | solution.py:124
  111.4 3.2 %collective-permute-start.28 = (bf16[64,3584]{1,0:T(8,128)(2,1)}, bf16[64,3584]{1,0:T(8,128)(2,1)}, u32[]{:S(2)}, u32[]{:S(2)}) collective-permute-start(bf16[64,3584]{1,0:T(8,128)(2,1)} %collective-permute-done.19.refs_11_.refs_17_), channel_id=1, source_target_pairs={{0,12},{1,13},{2,14},{3,15},{4,0},{5,1},{6,2},{7,3},{8,4},{9,5},{1... | collective-permute-start | bytes 1376264 | tf_op jit(solution)/shard_map/ag_up_f/ppermute | solution.py:124
  114.6 11.0 %collective-permute-done.27.refs_2_ = bf16[64,3584]{1,0:T(8,128)(2,1)S(1)} collective-permute-done((bf16[64,3584]{1,0:T(8,128)(2,1)}, bf16[64,3584]{1,0:T(8,128)(2,1)S(1)}, u32[]{:S(2)}, u32[]{:S(2)}) %collective-permute-start.27) | collective-permute-done | bytes 458784 | tf_op jit(solution)/shard_map/ag_gate_f/ppermute | solution.py:124
  127.3 3.1 %collective-permute-start.33 = (bf16[128,3584]{1,0:T(8,128)(2,1)S(1)}, bf16[128,3584]{1,0:T(8,128)(2,1)S(1)}, u32[]{:S(2)}, u32[]{:S(2)}) collective-permute-start(bf16[128,3584]{1,0:T(8,128)(2,1)S(1)} %collective-permute-done.22.refs_8_.refs_18_.refs_24_), channel_id=1, source_target_pairs={{0,12},{1,13},{2,14},{3,15},{4,0},{5,1},{6,2},{7,3},{8,4},{9,5},{1... | collective-permute-start | bytes 2752520 | tf_op jit(solution)/shard_map/ag_xa/ppermute | solution.py:124
  131.2 3.4 %collective-permute-start.35 = (bf16[64,3584]{1,0:T(8,128)(2,1)}, bf16[64,3584]{1,0:T(8,128)(2,1)}, u32[]{:S(2)}, u32[]{:S(2)}) collective-permute-start(bf16[64,3584]{1,0:T(8,128)(2,1)} %collective-permute-done.28.refs_12_.refs_18_), channel_id=1, source_target_pairs={{0,2},{1,3},{2,0},{3,1},{4,6},{5,7},{6,4},{7,5},{8,10},{9,11},{10,... | collective-permute-start | bytes 1376264 | tf_op jit(solution)/shard_map/ag_up_xf/ppermute | solution.py:124
  134.7 10.0 %input_grads.2 = f32[640,512]{1,0:T(8,128)} custom-call(bf16[128,3584]{1,0:T(8,128)(2,1)} %copy-done, bf16[64,3584]{1,0:T(8,128)(2,1)} %collective-permute-done.21.refs_1_, bf16[64,3584]{1,0:T(8,128)(2,1)} %copy-done.17, bf16[64,3584]{1,0:T(8,128)(2,1)} %collective-permute-done.18.refs_3_, bf16[128,3584]{1,0:T(8,128)(2,1)} %copy-done.5, ...), custom_call_target="tpu_custom_call" | custom-call | tf_op jit(solution)/shard_map/input_grads/pallas_call | solution.py:19
  144.7 3.8 %down_grads.2.refs_0_ = bf16[3584,512]{1,0:T(8,128)(2,1)} custom-call(bf16[512,896]{1,0:T(8,128)(2,1)} %bitcast.145, bf16[512,896]{1,0:T(8,128)(2,1)} %copy-done.19, bf16[1024,512]{1,0:T(8,128)(2,1)} %pad_maximum_fusion.1.right), custom_call_target="tpu_custom_call" | custom-call | tf_op jit(solution)/shard_map/down_grads/pallas_call | solution.py:104
  148.6 6.2 %collective-permute-done.35.refs_7_.refs_26_ = bf16[64,3584]{1,0:T(8,128)(2,1)} collective-permute-done((bf16[64,3584]{1,0:T(8,128)(2,1)}, bf16[64,3584]{1,0:T(8,128)(2,1)}, u32[]{:S(2)}, u32[]{:S(2)}) %collective-permute-start.35) | collective-permute-done | bytes 458784 | tf_op jit(solution)/shard_map/ag_up_xf/ppermute | solution.py:124
  155.9 5.9 %all-to-all-start.2 = ((bf16[8,64,2688]{2,1,0:T(8,128)(2,1)}), bf16[8,64,2688]{2,1,0:T(8,128)(2,1)}, u32[]{:S(2)}, u32[]{:S(2)}) async-start(bf16[8,64,2688]{2,1,0:T(8,128)(2,1)} %broadcast_in_dim.19), calls=%async_computation.2 | async-start | bytes 5505024 | tf_op jit(solution)/shard_map/hid_b/all_to_all | solution.py:179
  162.8 7.5 %input_grads.3 = f32[384,512]{1,0:T(8,128)} custom-call(bf16[128,3584]{1,0:T(8,128)(2,1)} %copy-done.2, bf16[64,3584]{1,0:T(8,128)(2,1)} %copy-done.15, bf16[128,3584]{1,0:T(8,128)(2,1)} %copy-done.1, bf16[128,3584]{1,0:T(8,128)(2,1)} %copy-done.3, bf16[64,3584]{1,0:T(8,128)(2,1)} %collective-permute-done.39.refs_4_.refs_14_, ...), custom_call_target="tpu_custom_call" | custom-call | tf_op jit(solution)/shard_map/input_grads/pallas_call | solution.py:19
  172.1 2.7 %collective-permute-start.44 = (bf16[2,2,64,512]{3,2,1,0:T(8,128)(2,1)S(1)}, bf16[2,2,64,512]{3,2,1,0:T(8,128)(2,1)S(1)}, u32[]{:S(2)}, u32[]{:S(2)}) collective-permute-start(bf16[2,2,64,512]{3,2,1,0:T(8,128)(2,1)S(1)} %get-tuple-element.202), channel_id=1, source_target_pairs={{0,96},{16,112},{32,0},{48,16},{64,32},{80,48},{96,64},{112,80},{1... | collective-permute-start | bytes 786440 | tf_op jit(solution)/shard_map/dn_y/ppermute | solution.py:133
  176.6 13.1 %gate_up_grads.1 = (bf16[512,3584]{1,0:T(8,128)(2,1)}, bf16[512,3584]{1,0:T(8,128)(2,1)}) custom-call(bf16[512,1024]{1,0:T(8,128)(2,1)} %bitcast.142, bf16[128,3584]{1,0:T(8,128)(2,1)} %copy-done, bf16[64,3584]{1,0:T(8,128)(2,1)} %collective-permute-done.21.refs_1_, bf16[64,3584]{1,0:T(8,128)(2,1)} %copy-done.17, ...), custom_call_target="tpu_custom_call" | custom-call | tf_op jit(solution)/shard_map/gate_up_grads/pallas_call | solution.py:19
  190.0 5.1 %collective-permute-done.45 = bf16[2,64,512]{2,1,0:T(8,128)(2,1)S(1)} collective-permute-done((bf16[2,64,512]{2,1,0:T(8,128)(2,1)S(1)}, bf16[2,64,512]{2,1,0:T(8,128)(2,1)S(1)}, u32[]{:S(2)}, u32[]{:S(2)}) %collective-permute-start.45) | collective-permute-done | bytes 131104 | tf_op jit(solution)/shard_map/dn_xl/ppermute | solution.py:133
  196.5 2.4 %collective-permute-start.48 = (f32[1,512]{1,0:T(1,128)S(1)}, f32[1,512]{1,0:T(1,128)S(1)}, u32[]{:S(2)}, u32[]{:S(2)}) collective-permute-start(f32[1,512]{1,0:T(1,128)S(1)} %bitcast.159), channel_id=1, source_target_pairs={{0,16},{16,0},{32,48},{48,32},{64,80},{80,64},{96,112},{112,96},{1... | collective-permute-start | bytes 6152 | tf_op jit(solution)/shard_map/gain/ppermute | solution.py:133
  198.9 5.0 %collective-permute-done.47 = f32[1,128]{1,0:T(1,128)S(1)} collective-permute-done((f32[1,128]{1,0:T(1,128)S(1)}, f32[1,128]{1,0:T(1,128)S(1)}, u32[]{:S(2)}, u32[]{:S(2)}) %collective-permute-start.47) | collective-permute-done | bytes 544 | tf_op jit(solution)/shard_map/proj/ppermute | solution.py:124
  206.1 3.0 %collective-permute-done.49 = f32[1,128]{1,0:T(1,128)S(1)} collective-permute-done((f32[1,128]{1,0:T(1,128)S(1)}, f32[1,128]{1,0:T(1,128)S(1)}, u32[]{:S(2)}, u32[]{:S(2)}) %collective-permute-start.49) | collective-permute-done | bytes 544 | tf_op jit(solution)/shard_map/proj/ppermute | solution.py:169
  209.4 2.7 %collective-permute-start.52 = (f32[1,128]{1,0:T(1,128)S(1)}, f32[1,128]{1,0:T(1,128)S(1)}, u32[]{:S(2)}, u32[]{:S(2)}) collective-permute-start(f32[1,128]{1,0:T(1,128)S(1)} %add.242), channel_id=1, source_target_pairs={{0,8},{1,9},{2,10},{3,11},{4,12},{5,13},{6,14},{7,15},{8,0},{9,1},... | collective-permute-start | bytes 1544 | tf_op jit(solution)/shard_map/proj/ppermute | solution.py:124
  212.1 3.0 %collective-permute-start.53 = (f32[1,512]{1,0:T(1,128)S(1)}, f32[1,512]{1,0:T(1,128)S(1)}, u32[]{:S(2)}, u32[]{:S(2)}) collective-permute-start(f32[1,512]{1,0:T(1,128)S(1)} %add.243), channel_id=1, source_target_pairs={{0,64},{16,80},{32,96},{48,112},{64,0},{80,16},{96,32},{112,48},{1... | collective-permute-start | bytes 6152 | tf_op jit(solution)/shard_map/gain/ppermute | solution.py:133
  215.1 6.8 %down_grads.3 = bf16[3584,512]{1,0:T(8,128)(2,1)} custom-call(bf16[512,2688]{1,0:T(8,128)(2,1)} %bitcast.62.left, bf16[512,2688]{1,0:T(8,128)(2,1)} %copy-done.10, bf16[1024,512]{1,0:T(8,128)(2,1)} %pad_maximum_fusion.1.right, bf16[3584,512]{1,0:T(8,128)(2,1)} %down_grads.2.refs_0_), custom_call_target="tpu_custom_call", output_to_operand_aliasing={{}: (3, {})} | custom-call | tf_op jit(solution)/shard_map/down_grads/pallas_call | solution.py:104
  (204 shorter events, 31.1 us)
Async XLA Ops:
  0.6 6.8 %collective-permute-start.1 = (bf16[3584,512]{1,0:T(8,128)(2,1)}, bf16[3584,512]{1,0:T(8,128)(2,1)}, u32[]{:S(2)}, u32[]{:S(2)}) collective-permute-start(bf16[3584,512]{1,0:T(8,128)(2,1)} %w.3), channel_id=1, source_target_pairs={{0,1},{1,0},{2,3},{3,2},{4,5},{5,4},{6,7},{7,6},{8,9},{9,8},{10,11... | collective-permute-start | bytes 11010056 | tf_op jit(solution)/shard_map/w_down/ppermute | solution.py:124
  0.7 6.4 %collective-permute-start = (bf16[128,512]{1,0:T(8,128)(2,1)}, bf16[128,512]{1,0:T(8,128)(2,1)S(1)}, u32[]{:S(2)}, u32[]{:S(2)}) collective-permute-start(bf16[128,512]{1,0:T(8,128)(2,1)} %param.9), channel_id=1, source_target_pairs={{0,16},{16,0},{32,48},{48,32},{64,80},{80,64},{96,112},{112,96},{1... | collective-permute-start | bytes 393224 | tf_op jit(solution)/shard_map/out_xl/ppermute | solution.py:133
  7.5 15.5 %collective-permute-start.3 = (bf16[2,2,1,64,512]{4,3,0,2,1:T(8,128)(2,1)S(1)}, bf16[2,2,1,64,512]{4,3,0,2,1:T(8,128)(2,1)S(1)}, u32[]{:S(2)}, u32[]{:S(2)}) collective-permute-start(bf16[2,2,1,64,512]{4,3,0,2,1:T(8,128)(2,1)S(1)} %fusion.12), channel_id=1, source_target_pairs={{0,96},{16,112},{32,0},{48,16},{64,32},{80,48},{96,64},{112,80},{1... | collective-permute-start | bytes 786440 | tf_op jit(solution)/shard_map/out_y/ppermute | solution.py:133
  10.5 12.6 %collective-permute-start.4 = (bf16[2,2,1,64,512]{4,3,0,2,1:T(8,128)(2,1)S(1)}, bf16[2,2,1,64,512]{4,3,0,2,1:T(8,128)(2,1)S(1)}, u32[]{:S(2)}, u32[]{:S(2)}) collective-permute-start(bf16[2,2,1,64,512]{4,3,0,2,1:T(8,128)(2,1)S(1)} %fusion.12), channel_id=1, source_target_pairs={{0,64},{16,80},{32,96},{48,112},{64,0},{80,16},{96,32},{112,48},{1... | collective-permute-start | bytes 786440 | tf_op jit(solution)/shard_map/out_y/ppermute | solution.py:133
  11.1 14.6 %collective-permute-start.5 = (bf16[2,2,1,64,512]{4,3,0,2,1:T(8,128)(2,1)S(1)}, bf16[2,2,1,64,512]{4,3,0,2,1:T(8,128)(2,1)S(1)}, u32[]{:S(2)}, u32[]{:S(2)}) collective-permute-start(bf16[2,2,1,64,512]{4,3,0,2,1:T(8,128)(2,1)S(1)} %fusion.12), channel_id=1, source_target_pairs={{0,32},{16,48},{32,64},{48,80},{64,96},{80,112},{96,0},{112,16},{1... | collective-permute-start | bytes 786440 | tf_op jit(solution)/shard_map/out_y/ppermute | solution.py:133
  12.1 10.9 %collective-permute-start.6 = (f32[1,128]{1,0:T(1,128)S(1)}, f32[1,128]{1,0:T(1,128)S(1)}, u32[]{:S(2)}, u32[]{:S(2)}) collective-permute-start(f32[1,128]{1,0:T(1,128)S(1)} %bitcast_add_fusion), channel_id=1, source_target_pairs={{0,4},{1,5},{2,6},{3,7},{4,0},{5,1},{6,2},{7,3},{8,12},{9,13},{10,... | collective-permute-start | bytes 1544 | tf_op jit(solution)/shard_map/squares/ppermute | solution.py:169
  15.2 20.5 %all-to-all-start = ((bf16[8,64,896]{2,1,0:T(8,128)(2,1)}), bf16[8,64,896]{2,1,0:T(8,128)(2,1)S(1)}, u32[]{:S(2)}, u32[]{:S(2)}) async-start(bf16[8,64,896]{2,1,0:T(8,128)(2,1)} %broadcast_in_dim.20), calls=%async_computation | async-start | bytes 1835008 | tf_op jit(solution)/shard_map/hid_a/all_to_all | solution.py:179
  35.7 17.4 %collective-permute-start.8 = (bf16[64,3584]{1,0:T(8,128)(2,1)}, bf16[64,3584]{1,0:T(8,128)(2,1)S(1)}, u32[]{:S(2)}, u32[]{:S(2)}) collective-permute-start(bf16[64,3584]{1,0:T(8,128)(2,1)} %get-tuple-element.126), channel_id=1, source_target_pairs={{0,2},{1,3},{2,0},{3,1},{4,6},{5,7},{6,4},{7,5},{8,10},{9,11},{10,... | collective-permute-start | bytes 1376264 | tf_op jit(solution)/shard_map/rs_x/ppermute | solution.py:124
  38.0 15.1 %collective-permute-start.9 = (bf16[64,3584]{1,0:T(8,128)(2,1)}, bf16[64,3584]{1,0:T(8,128)(2,1)S(1)}, u32[]{:S(2)}, u32[]{:S(2)}) collective-permute-start(bf16[64,3584]{1,0:T(8,128)(2,1)} %get-tuple-element.127), channel_id=1, source_target_pairs={{0,4},{1,5},{2,6},{3,7},{4,8},{5,9},{6,10},{7,11},{8,12},{9,13},{1... | collective-permute-start | bytes 1376264 | tf_op jit(solution)/shard_map/rs_b/ppermute | solution.py:124
  39.1 14.1 %collective-permute-start.10 = (bf16[64,3584]{1,0:T(8,128)(2,1)}, bf16[64,3584]{1,0:T(8,128)(2,1)}, u32[]{:S(2)}, u32[]{:S(2)}) collective-permute-start(bf16[64,3584]{1,0:T(8,128)(2,1)} %get-tuple-element.128), channel_id=1, source_target_pairs={{0,12},{1,13},{2,14},{3,15},{4,0},{5,1},{6,2},{7,3},{8,4},{9,5},{1... | collective-permute-start | bytes 1376264 | tf_op jit(solution)/shard_map/rs_a/ppermute | solution.py:124
  47.0 6.1 %collective-permute-start.11 = (f32[1,128]{1,0:T(1,128)S(1)}, f32[1,128]{1,0:T(1,128)S(1)}, u32[]{:S(2)}, u32[]{:S(2)}) collective-permute-start(f32[1,128]{1,0:T(1,128)S(1)} %add.209), channel_id=1, source_target_pairs={{0,8},{1,9},{2,10},{3,11},{4,12},{5,13},{6,14},{7,15},{8,0},{9,1},... | collective-permute-start | bytes 1544 | tf_op jit(solution)/shard_map/squares/ppermute | solution.py:124
  55.5 7.7 %collective-permute-start.13 = (bf16[32,3584]{1,0:T(8,128)(2,1)S(1)}, bf16[32,3584]{1,0:T(8,128)(2,1)S(1)}, u32[]{:S(2)}, u32[]{:S(2)}) collective-permute-start(bf16[32,3584]{1,0:T(8,128)(2,1)S(1)} %get-tuple-element.231), channel_id=1, source_target_pairs={{0,4},{1,5},{2,6},{3,7},{4,8},{5,9},{6,10},{7,11},{8,12},{9,13},{1... | collective-permute-start | bytes 688136 | tf_op jit(solution)/shard_map/rs_fb/ppermute | solution.py:124
  56.7 7.3 %collective-permute-start.14 = (bf16[32,3584]{1,0:T(8,128)(2,1)S(1)}, bf16[32,3584]{1,0:T(8,128)(2,1)S(1)}, u32[]{:S(2)}, u32[]{:S(2)}) collective-permute-start(bf16[32,3584]{1,0:T(8,128)(2,1)S(1)} %get-tuple-element.230), channel_id=1, source_target_pairs={{0,12},{1,13},{2,14},{3,15},{4,0},{5,1},{6,2},{7,3},{8,4},{9,5},{1... | collective-permute-start | bytes 688136 | tf_op jit(solution)/shard_map/rs_fa/ppermute | solution.py:124
  61.0 17.2 %collective-permute-start.12 = (bf16[64,3584]{1,0:T(8,128)(2,1)}, bf16[64,3584]{1,0:T(8,128)(2,1)}, u32[]{:S(2)}, u32[]{:S(2)}) collective-permute-start(bf16[64,3584]{1,0:T(8,128)(2,1)} %add_convert_fusion), channel_id=1, source_target_pairs={{0,2},{1,3},{2,0},{3,1},{4,6},{5,7},{6,4},{7,5},{8,10},{9,11},{10,... | collective-permute-start | bytes 1376264 | tf_op jit(solution)/shard_map/rs_xl/ppermute | solution.py:124
  64.9 13.2 %collective-permute-start.16 = (bf16[64,3584]{1,0:T(8,128)(2,1)}, bf16[64,3584]{1,0:T(8,128)(2,1)}, u32[]{:S(2)}, u32[]{:S(2)}) collective-permute-start(bf16[64,3584]{1,0:T(8,128)(2,1)} %pad_maximum_fusion.4), channel_id=1, source_target_pairs={{0,12},{1,13},{2,14},{3,15},{4,0},{5,1},{6,2},{7,3},{8,4},{9,5},{1... | collective-permute-start | bytes 1376264 | tf_op jit(solution)/shard_map/rs_al/ppermute | solution.py:124
  66.9 11.2 %collective-permute-start.15 = (bf16[64,3584]{1,0:T(8,128)(2,1)}, bf16[64,3584]{1,0:T(8,128)(2,1)}, u32[]{:S(2)}, u32[]{:S(2)}) collective-permute-start(bf16[64,3584]{1,0:T(8,128)(2,1)} %pad_maximum_fusion.3), channel_id=1, source_target_pairs={{0,4},{1,5},{2,6},{3,7},{4,8},{5,9},{6,10},{7,11},{8,12},{9,13},{1... | collective-permute-start | bytes 1376264 | tf_op jit(solution)/shard_map/rs_bl/ppermute | solution.py:124
  66.9 6.5 %collective-permute-start.17 = (f32[1,128]{1,0:T(1,128)S(1)}, f32[1,128]{1,0:T(1,128)S(1)}, u32[]{:S(2)}, u32[]{:S(2)}) collective-permute-start(f32[1,128]{1,0:T(1,128)S(1)} %add.210), channel_id=1, source_target_pairs={{0,2},{1,3},{2,0},{3,1},{4,6},{5,7},{6,4},{7,5},{8,10},{9,11},{10,... | collective-permute-start | bytes 1544 | tf_op jit(solution)/shard_map/squares/ppermute | solution.py:124
  74.6 28.4 %all-to-all-start.1 = ((bf16[8,128,512]{2,1,0:T(8,128)(2,1)}), bf16[8,128,512]{2,1,0:T(8,128)(2,1)S(1)}, u32[]{:S(2)}, u32[]{:S(2)}) async-start(bf16[8,128,512]{2,1,0:T(8,128)(2,1)} %broadcast_in_dim.22), calls=%async_computation.1 | async-start | bytes 2097152 | tf_op jit(solution)/shard_map/normed_rows/all_to_all | solution.py:231
  80.2 13.6 %collective-permute-start.19 = (bf16[64,3584]{1,0:T(8,128)(2,1)S(1)}, bf16[64,3584]{1,0:T(8,128)(2,1)}, u32[]{:S(2)}, u32[]{:S(2)}) collective-permute-start(bf16[64,3584]{1,0:T(8,128)(2,1)S(1)} %get-tuple-element.156), channel_id=1, source_target_pairs={{0,12},{1,13},{2,14},{3,15},{4,0},{5,1},{6,2},{7,3},{8,4},{9,5},{1... | collective-permute-start | bytes 1376264 | tf_op jit(solution)/shard_map/ag_up_a/ppermute | solution.py:124
  82.5 19.9 %collective-permute-start.20 = (bf16[64,3584]{1,0:T(8,128)(2,1)S(1)}, bf16[64,3584]{1,0:T(8,128)(2,1)}, u32[]{:S(2)}, u32[]{:S(2)}) collective-permute-start(bf16[64,3584]{1,0:T(8,128)(2,1)S(1)} %get-tuple-element.156), channel_id=1, source_target_pairs={{0,4},{1,5},{2,6},{3,7},{4,8},{5,9},{6,10},{7,11},{8,12},{9,13},{1... | collective-permute-start | bytes 1376264 | tf_op jit(solution)/shard_map/ag_up_b/ppermute | solution.py:124
  82.5 19.9 %collective-permute-start.18 = (bf16[64,3584]{1,0:T(8,128)(2,1)S(1)}, bf16[64,3584]{1,0:T(8,128)(2,1)}, u32[]{:S(2)}, u32[]{:S(2)}) collective-permute-start(bf16[64,3584]{1,0:T(8,128)(2,1)S(1)} %get-tuple-element.155), channel_id=1, source_target_pairs={{0,4},{1,5},{2,6},{3,7},{4,8},{5,9},{6,10},{7,11},{8,12},{9,13},{1... | collective-permute-start | bytes 1376264 | tf_op jit(solution)/shard_map/ag_gate_b/ppermute | solution.py:124
  82.5 17.3 %collective-permute-start.21 = (bf16[64,3584]{1,0:T(8,128)(2,1)S(1)}, bf16[64,3584]{1,0:T(8,128)(2,1)}, u32[]{:S(2)}, u32[]{:S(2)}) collective-permute-start(bf16[64,3584]{1,0:T(8,128)(2,1)S(1)} %get-tuple-element.155), channel_id=1, source_target_pairs={{0,12},{1,13},{2,14},{3,15},{4,0},{5,1},{6,2},{7,3},{8,4},{9,5},{1... | collective-permute-start | bytes 1376264 | tf_op jit(solution)/shard_map/ag_gate_a/ppermute | solution.py:124
  85.8 24.8 %collective-permute-start.22 = (bf16[128,3584]{1,0:T(8,128)(2,1)S(1)}, bf16[128,3584]{1,0:T(8,128)(2,1)S(1)}, u32[]{:S(2)}, u32[]{:S(2)}) collective-permute-start(bf16[128,3584]{1,0:T(8,128)(2,1)S(1)} %pad_maximum_fusion.2.refs_0_.refs_10_.refs_16_), channel_id=1, source_target_pairs={{0,2},{1,3},{2,0},{3,1},{4,6},{5,7},{6,4},{7,5},{8,10},{9,11},{10,... | collective-permute-start | bytes 2752520 | tf_op jit(solution)/shard_map/ag_x/ppermute | solution.py:124
  93.9 16.8 %collective-permute-start.23 = (bf16[64,3584]{1,0:T(8,128)(2,1)}, bf16[64,3584]{1,0:T(8,128)(2,1)S(1)}, u32[]{:S(2)}, u32[]{:S(2)}) collective-permute-start(bf16[64,3584]{1,0:T(8,128)(2,1)} %collective-permute-done.19.refs_11_.refs_17_), channel_id=1, source_target_pairs={{0,1},{1,0},{2,3},{3,2},{4,5},{5,4},{6,7},{7,6},{8,9},{9,8},{10,11... | collective-permute-start | bytes 1376264 | tf_op jit(solution)/shard_map/ag_core/ppermute | solution.py:124
  99.9 10.8 %collective-permute-start.24 = (bf16[64,3584]{1,0:T(8,128)(2,1)}, bf16[64,3584]{1,0:T(8,128)(2,1)}, u32[]{:S(2)}, u32[]{:S(2)}) collective-permute-start(bf16[64,3584]{1,0:T(8,128)(2,1)} %collective-permute-done.21.refs_1_), channel_id=1, source_target_pairs={{0,1},{1,0},{2,3},{3,2},{4,5},{5,4},{6,7},{7,6},{8,9},{9,8},{10,11... | collective-permute-start | bytes 1376264 | tf_op jit(solution)/shard_map/ag_core/ppermute | solution.py:124
  102.4 8.2 %collective-permute-start.25 = (bf16[64,3584]{1,0:T(8,128)(2,1)}, bf16[64,3584]{1,0:T(8,128)(2,1)}, u32[]{:S(2)}, u32[]{:S(2)}) collective-permute-start(bf16[64,3584]{1,0:T(8,128)(2,1)} %collective-permute-done.18.refs_3_), channel_id=1, source_target_pairs={{0,1},{1,0},{2,3},{3,2},{4,5},{5,4},{6,7},{7,6},{8,9},{9,8},{10,11... | collective-permute-start | bytes 1376264 | tf_op jit(solution)/shard_map/ag_core/ppermute | solution.py:124
  102.5 8.2 %collective-permute-start.26 = (bf16[64,3584]{1,0:T(8,128)(2,1)}, bf16[64,3584]{1,0:T(8,128)(2,1)}, u32[]{:S(2)}, u32[]{:S(2)}) collective-permute-start(bf16[64,3584]{1,0:T(8,128)(2,1)} %collective-permute-done.20.refs_13_.refs_19_), channel_id=1, source_target_pairs={{0,1},{1,0},{2,3},{3,2},{4,5},{5,4},{6,7},{7,6},{8,9},{9,8},{10,11... | collective-permute-start | bytes 1376264 | tf_op jit(solution)/shard_map/ag_core/ppermute | solution.py:124
  110.7 15.0 %collective-permute-start.29 = (bf16[512,896]{1,0:T(8,128)(2,1)}, bf16[512,896]{1,0:T(8,128)(2,1)S(1)}, u32[]{:S(2)}, u32[]{:S(2)}) collective-permute-start(bf16[512,896]{1,0:T(8,128)(2,1)} %bitcast.144), channel_id=1, source_target_pairs={{0,1},{1,0},{2,3},{3,2},{4,5},{5,4},{6,7},{7,6},{8,9},{9,8},{10,11... | collective-permute-start | bytes 2752520 | tf_op jit(solution)/shard_map/hid_core/ppermute | solution.py:124
  110.8 14.9 %collective-permute-start.30 = (bf16[128,3584]{1,0:T(8,128)(2,1)S(1)}, bf16[128,3584]{1,0:T(8,128)(2,1)S(1)}, u32[]{:S(2)}, u32[]{:S(2)}) collective-permute-start(bf16[128,3584]{1,0:T(8,128)(2,1)S(1)} %pad_maximum_fusion.2.refs_0_.refs_10_.refs_16_), channel_id=1, source_target_pairs={{0,1},{1,0},{2,3},{3,2},{4,5},{5,4},{6,7},{7,6},{8,9},{9,8},{10,11... | collective-permute-start | bytes 2752520 | tf_op jit(solution)/shard_map/ag_core/ppermute | solution.py:124
  111.3 14.4 %collective-permute-start.31 = (bf16[128,3584]{1,0:T(8,128)(2,1)S(1)}, bf16[128,3584]{1,0:T(8,128)(2,1)S(1)}, u32[]{:S(2)}, u32[]{:S(2)}) collective-permute-start(bf16[128,3584]{1,0:T(8,128)(2,1)S(1)} %collective-permute-done.22.refs_8_.refs_18_.refs_24_), channel_id=1, source_target_pairs={{0,1},{1,0},{2,3},{3,2},{4,5},{5,4},{6,7},{7,6},{8,9},{9,8},{10,11... | collective-permute-start | bytes 2752520 | tf_op jit(solution)/shard_map/ag_core/ppermute | solution.py:124
  111.4 14.3 %collective-permute-start.27 = (bf16[64,3584]{1,0:T(8,128)(2,1)}, bf16[64,3584]{1,0:T(8,128)(2,1)S(1)}, u32[]{:S(2)}, u32[]{:S(2)}) collective-permute-start(bf16[64,3584]{1,0:T(8,128)(2,1)} %collective-permute-done.18.refs_3_), channel_id=1, source_target_pairs={{0,4},{1,5},{2,6},{3,7},{4,8},{5,9},{6,10},{7,11},{8,12},{9,13},{1... | collective-permute-start | bytes 1376264 | tf_op jit(solution)/shard_map/ag_gate_f/ppermute | solution.py:124
  111.4 14.3 %collective-permute-start.28 = (bf16[64,3584]{1,0:T(8,128)(2,1)}, bf16[64,3584]{1,0:T(8,128)(2,1)}, u32[]{:S(2)}, u32[]{:S(2)}) collective-permute-start(bf16[64,3584]{1,0:T(8,128)(2,1)} %collective-permute-done.19.refs_11_.refs_17_), channel_id=1, source_target_pairs={{0,12},{1,13},{2,14},{3,15},{4,0},{5,1},{6,2},{7,3},{8,4},{9,5},{1... | collective-permute-start | bytes 1376264 | tf_op jit(solution)/shard_map/ag_up_f/ppermute | solution.py:124
  126.9 27.8 %collective-permute-start.32 = (bf16[128,3584]{1,0:T(8,128)(2,1)S(1)}, bf16[128,3584]{1,0:T(8,128)(2,1)S(1)}, u32[]{:S(2)}, u32[]{:S(2)}) collective-permute-start(bf16[128,3584]{1,0:T(8,128)(2,1)S(1)} %collective-permute-done.22.refs_8_.refs_18_.refs_24_), channel_id=1, source_target_pairs={{0,4},{1,5},{2,6},{3,7},{4,8},{5,9},{6,10},{7,11},{8,12},{9,13},{1... | collective-permute-start | bytes 2752520 | tf_op jit(solution)/shard_map/ag_xb/ppermute | solution.py:124
  127.3 27.4 %collective-permute-start.33 = (bf16[128,3584]{1,0:T(8,128)(2,1)S(1)}, bf16[128,3584]{1,0:T(8,128)(2,1)S(1)}, u32[]{:S(2)}, u32[]{:S(2)}) collective-permute-start(bf16[128,3584]{1,0:T(8,128)(2,1)S(1)} %collective-permute-done.22.refs_8_.refs_18_.refs_24_), channel_id=1, source_target_pairs={{0,12},{1,13},{2,14},{3,15},{4,0},{5,1},{6,2},{7,3},{8,4},{9,5},{1... | collective-permute-start | bytes 2752520 | tf_op jit(solution)/shard_map/ag_xa/ppermute | solution.py:124
  130.3 18.2 %collective-permute-start.34 = (bf16[64,3584]{1,0:T(8,128)(2,1)S(1)}, bf16[64,3584]{1,0:T(8,128)(2,1)S(1)}, u32[]{:S(2)}, u32[]{:S(2)}) collective-permute-start(bf16[64,3584]{1,0:T(8,128)(2,1)S(1)} %collective-permute-done.27.refs_2_), channel_id=1, source_target_pairs={{0,2},{1,3},{2,0},{3,1},{4,6},{5,7},{6,4},{7,5},{8,10},{9,11},{10,... | collective-permute-start | bytes 1376264 | tf_op jit(solution)/shard_map/ag_gate_xf/ppermute | solution.py:124
  131.2 23.5 %collective-permute-start.35 = (bf16[64,3584]{1,0:T(8,128)(2,1)}, bf16[64,3584]{1,0:T(8,128)(2,1)}, u32[]{:S(2)}, u32[]{:S(2)}) collective-permute-start(bf16[64,3584]{1,0:T(8,128)(2,1)} %collective-permute-done.28.refs_12_.refs_18_), channel_id=1, source_target_pairs={{0,2},{1,3},{2,0},{3,1},{4,6},{5,7},{6,4},{7,5},{8,10},{9,11},{10,... | collective-permute-start | bytes 1376264 | tf_op jit(solution)/shard_map/ag_up_xf/ppermute | solution.py:124
  154.7 7.1 %collective-permute-start.38 = (bf16[128,3584]{1,0:T(8,128)(2,1)S(1)}, bf16[128,3584]{1,0:T(8,128)(2,1)S(1)}, u32[]{:S(2)}, u32[]{:S(2)}) collective-permute-start(bf16[128,3584]{1,0:T(8,128)(2,1)S(1)} %collective-permute-done.33.refs_0_.refs_6_.refs_9_.refs_25_), channel_id=1, source_target_pairs={{0,1},{1,0},{2,3},{3,2},{4,5},{5,4},{6,7},{7,6},{8,9},{9,8},{10,11... | collective-permute-start | bytes 2752520 | tf_op jit(solution)/shard_map/ag_core/ppermute | solution.py:124
  154.8 7.0 %collective-permute-start.40 = (bf16[128,3584]{1,0:T(8,128)(2,1)S(1)}, bf16[128,3584]{1,0:T(8,128)(2,1)}, u32[]{:S(2)}, u32[]{:S(2)}) collective-permute-start(bf16[128,3584]{1,0:T(8,128)(2,1)S(1)} %collective-permute-done.32.refs_2_.refs_8_.refs_11_.refs_27_), channel_id=1, source_target_pairs={{0,1},{1,0},{2,3},{3,2},{4,5},{5,4},{6,7},{7,6},{8,9},{9,8},{10,11... | collective-permute-start | bytes 2752520 | tf_op jit(solution)/shard_map/ag_core/ppermute | solution.py:124
  155.3 6.5 %collective-permute-start.39 = (bf16[64,3584]{1,0:T(8,128)(2,1)S(1)}, bf16[64,3584]{1,0:T(8,128)(2,1)}, u32[]{:S(2)}, u32[]{:S(2)}) collective-permute-start(bf16[64,3584]{1,0:T(8,128)(2,1)S(1)} %collective-permute-done.34.refs_1_.refs_10_), channel_id=1, source_target_pairs={{0,1},{1,0},{2,3},{3,2},{4,5},{5,4},{6,7},{7,6},{8,9},{9,8},{10,11... | collective-permute-start | bytes 1376264 | tf_op jit(solution)/shard_map/ag_core/ppermute | solution.py:124
  155.4 6.4 %collective-permute-start.41 = (bf16[64,3584]{1,0:T(8,128)(2,1)}, bf16[64,3584]{1,0:T(8,128)(2,1)}, u32[]{:S(2)}, u32[]{:S(2)}) collective-permute-start(bf16[64,3584]{1,0:T(8,128)(2,1)} %collective-permute-done.35.refs_7_.refs_26_), channel_id=1, source_target_pairs={{0,1},{1,0},{2,3},{3,2},{4,5},{5,4},{6,7},{7,6},{8,9},{9,8},{10,11... | collective-permute-start | bytes 1376264 | tf_op jit(solution)/shard_map/ag_core/ppermute | solution.py:124
  155.9 48.1 %all-to-all-start.2 = ((bf16[8,64,2688]{2,1,0:T(8,128)(2,1)}), bf16[8,64,2688]{2,1,0:T(8,128)(2,1)}, u32[]{:S(2)}, u32[]{:S(2)}) async-start(bf16[8,64,2688]{2,1,0:T(8,128)(2,1)} %broadcast_in_dim.19), calls=%async_computation.2 | async-start | bytes 5505024 | tf_op jit(solution)/shard_map/hid_b/all_to_all | solution.py:179
  172.1 17.6 %collective-permute-start.44 = (bf16[2,2,64,512]{3,2,1,0:T(8,128)(2,1)S(1)}, bf16[2,2,64,512]{3,2,1,0:T(8,128)(2,1)S(1)}, u32[]{:S(2)}, u32[]{:S(2)}) collective-permute-start(bf16[2,2,64,512]{3,2,1,0:T(8,128)(2,1)S(1)} %get-tuple-element.202), channel_id=1, source_target_pairs={{0,96},{16,112},{32,0},{48,16},{64,32},{80,48},{96,64},{112,80},{1... | collective-permute-start | bytes 786440 | tf_op jit(solution)/shard_map/dn_y/ppermute | solution.py:133
  174.8 14.9 %collective-permute-start.43 = (bf16[2,2,64,512]{3,2,1,0:T(8,128)(2,1)S(1)}, bf16[2,2,64,512]{3,2,1,0:T(8,128)(2,1)S(1)}, u32[]{:S(2)}, u32[]{:S(2)}) collective-permute-start(bf16[2,2,64,512]{3,2,1,0:T(8,128)(2,1)S(1)} %get-tuple-element.201), channel_id=1, source_target_pairs={{0,64},{16,80},{32,96},{48,112},{64,0},{80,16},{96,32},{112,48},{1... | collective-permute-start | bytes 786440 | tf_op jit(solution)/shard_map/dn_y/ppermute | solution.py:133
  175.6 14.1 %collective-permute-start.42 = (bf16[2,2,64,512]{3,2,1,0:T(8,128)(2,1)S(1)}, bf16[2,2,64,512]{3,2,1,0:T(8,128)(2,1)S(1)}, u32[]{:S(2)}, u32[]{:S(2)}) collective-permute-start(bf16[2,2,64,512]{3,2,1,0:T(8,128)(2,1)S(1)} %get-tuple-element.200), channel_id=1, source_target_pairs={{0,32},{16,48},{32,64},{48,80},{64,96},{80,112},{96,0},{112,16},{1... | collective-permute-start | bytes 786440 | tf_op jit(solution)/shard_map/dn_y/ppermute | solution.py:133
  196.5 7.5 %collective-permute-start.48 = (f32[1,512]{1,0:T(1,128)S(1)}, f32[1,512]{1,0:T(1,128)S(1)}, u32[]{:S(2)}, u32[]{:S(2)}) collective-permute-start(f32[1,512]{1,0:T(1,128)S(1)} %bitcast.159), channel_id=1, source_target_pairs={{0,16},{16,0},{32,48},{48,32},{64,80},{80,64},{96,112},{112,96},{1... | collective-permute-start | bytes 6152 | tf_op jit(solution)/shard_map/gain/ppermute | solution.py:133
  204.0 5.4 %collective-permute-start.51 = (bf16[512,2688]{1,0:T(8,128)(2,1)}, bf16[512,2688]{1,0:T(8,128)(2,1)S(1)}, u32[]{:S(2)}, u32[]{:S(2)}) collective-permute-start(bf16[512,2688]{1,0:T(8,128)(2,1)} %bitcast.62.left), channel_id=1, source_target_pairs={{0,1},{1,0},{2,3},{3,2},{4,5},{5,4},{6,7},{7,6},{8,9},{9,8},{10,11... | collective-permute-start | bytes 8257544 | tf_op jit(solution)/shard_map/hid_core/ppermute | solution.py:124
  209.4 12.5 %collective-permute-start.52 = (f32[1,128]{1,0:T(1,128)S(1)}, f32[1,128]{1,0:T(1,128)S(1)}, u32[]{:S(2)}, u32[]{:S(2)}) collective-permute-start(f32[1,128]{1,0:T(1,128)S(1)} %add.242), channel_id=1, source_target_pairs={{0,8},{1,9},{2,10},{3,11},{4,12},{5,13},{6,14},{7,15},{8,0},{9,1},... | collective-permute-start | bytes 1544 | tf_op jit(solution)/shard_map/proj/ppermute | solution.py:124
  212.1 10.6 %collective-permute-start.53 = (f32[1,512]{1,0:T(1,128)S(1)}, f32[1,512]{1,0:T(1,128)S(1)}, u32[]{:S(2)}, u32[]{:S(2)}) collective-permute-start(f32[1,512]{1,0:T(1,128)S(1)} %add.243), channel_id=1, source_target_pairs={{0,64},{16,80},{32,96},{48,112},{64,0},{80,16},{96,32},{112,48},{1... | collective-permute-start | bytes 6152 | tf_op jit(solution)/shard_map/gain/ppermute | solution.py:133
  (40 other events, 297.4 us)

commit v4 on v3

--- a/solution.py
+++ b/solution.py
@@ -189,6 +189,7 @@
     squares = jnp.sum(values * values, axis=1).reshape(1, rows)
     squares = squares + col_to(squares, "squares", dc=1)
     pair = order(out_grad, out_xl)
+    hidden_a = jnp.broadcast_to(hidden_a[None], (NZ * NX, *hidden_a.shape))
     pair, hidden_a, hidden_b, w_down_other, squares = phase(pair, hidden_a, hidden_b, w_down_other, squares)
 
     out_y = [row_to(pair, "out_y", -ky) for ky in range(1, NY)]

time: 224 us -> 225 us (level)
    unnamed x58 -> x60, local copies, waits for them, and re-layouts: 5.08 us -> 5.04 us
  transfers between devices with their start and end apart: 57 -> 57, of which waited for: 17 -> 17; matrix products, arithmetic and copies ran while one was open for 9% -> 8% of each run, Pallas kernels for 23% -> 23%
where the time goes in v4:
time: 225 us; the launch traced here: 224 us
  starting transfers between devices  78 us (35%)
  waiting for transfers between devices  64.9 us (29%)
  Pallas kernels  52.5 us (23%)
  other arithmetic  14 us (6%)
  local copies, waits for them, and re-layouts  13.3 us (6%)
    ppermute x41, waiting for transfers between devices, col_to(): return lax.ppermute(x, 'col', pairs)  54.4 us
    pallas_call x5, Pallas kernels, kernel_call(): pl.pallas_call(body, grid=(steps,), in_specs=in_specs, out_specs=out_spec...  41.8 us
    ppermute x41, starting transfers between devices, col_to(): return lax.ppermute(x, 'col', pairs)  41 us
    ppermute x10, starting transfers between devices, row_to(): return lax.ppermute(x, 'row', pairs)  15.5 us
    all_to_all x2, starting transfers between devices, gather_hidden(): lax.all_to_all(copies, 'col', 0, 0, axis_index_groups=groups, tiled=True)  13.8 us
    pallas_call x2, Pallas kernels, down_grads(): pl.pallas_call(body, grid=(steps,), in_specs=specs + [pl.BlockSpec(memory...  10.7 us
    ppermute x10, waiting for transfers between devices, row_to(): return lax.ppermute(x, 'row', pairs)  7.59 us
    unnamed x60, local copies, waits for them, and re-layouts  5.04 us
  transfers between devices with their start and end apart: 57, of which 17 were waited for; matrix products, arithmetic and copies ran while one was open for 8% of the time, Pallas kernels for 23%

profile of v4, /device:TPU:6, one launch (start us, length us, event | category | flops | bytes accessed | tf_op | source)
XLA Modules:
  0.0 224.3 jit_solution(6068703798419971952)
XLA Ops:
  4.4 2.6 %collective-permute-done.2 = f32[1,128]{1,0:T(1,128)S(1)} collective-permute-done((f32[1,128]{1,0:T(1,128)S(1)}, f32[1,128]{1,0:T(1,128)S(1)}, u32[]{:S(2)}, u32[]{:S(2)}) %collective-permute-start.2) | collective-permute-done | bytes 544 | tf_op jit(solution)/shard_map/squares/ppermute | solution.py:124
  8.5 3.0 %collective-permute-start.3 = (bf16[2,2,1,64,512]{4,3,0,2,1:T(8,128)(2,1)S(1)}, bf16[2,2,1,64,512]{4,3,0,2,1:T(8,128)(2,1)}, u32[]{:S(2)}, u32[]{:S(2)}) collective-permute-start(bf16[2,2,1,64,512]{4,3,0,2,1:T(8,128)(2,1)S(1)} %fusion.12), channel_id=1, source_target_pairs={{0,96},{16,112},{32,0},{48,16},{64,32},{80,48},{96,64},{112,80},{1... | collective-permute-start | bytes 786440 | tf_op jit(solution)/shard_map/out_y/ppermute | solution.py:133
  13.1 1.9 collective-permute-start.6
  15.2 8.0 %all-to-all-start = ((bf16[8,64,896]{2,1,0:T(8,128)(2,1)}), bf16[8,64,896]{2,1,0:T(8,128)(2,1)S(1)}, u32[]{:S(2)}, u32[]{:S(2)}) async-start(bf16[8,64,896]{2,1,0:T(8,128)(2,1)} %broadcast_in_dim.19), calls=%async_computation | async-start | bytes 1835008 | tf_op jit(solution)/shard_map/hid_a/all_to_all | solution.py:179
  24.2 2.5 %collective-permute-done.5 = bf16[2,2,1,64,512]{4,3,0,2,1:T(8,128)(2,1)S(1)} collective-permute-done((bf16[2,2,1,64,512]{4,3,0,2,1:T(8,128)(2,1)S(1)}, bf16[2,2,1,64,512]{4,3,0,2,1:T(8,128)(2,1)S(1)}, u32[]{:S(2)}, u32[]{:S(2)}) %collective-permute-start.5) | collective-permute-done | bytes 262176 | tf_op jit(solution)/shard_map/out_y/ppermute | solution.py:133
  26.8 1.7 broadcast_in_dim.20
  28.5 1.9 collective-permute-done.7.lo
  31.2 5.5 %hidden_units.2 = (f32[64,3584]{1,0:T(8,128)}, bf16[64,3584]{1,0:T(8,128)(2,1)}, bf16[64,3584]{1,0:T(8,128)(2,1)}, bf16[64,3584]{1,0:T(8,128)(2,1)}) custom-call(bf16[512,512]{1,0:T(8,128)(2,1)} %bitcast.138, bf16[512,512]{1,0:T(8,128)(2,1)} %copy-done.11, bf16[3584,512]{1,0:T(8,128)(2,1)} %w.3, bf16[3584,512]{1,0:T(8,128)(2,1)} %collective-permute-done.1.wo), custom_call_target="tpu_custom_call" | custom-call | tf_op jit(solution)/shard_map/hidden_units/pallas_call | solution.py:19
  36.7 1.5 collective-permute-start.8
  38.2 1.9 collective-permute-start.9
  40.1 2.1 collective-permute-start.10
  42.2 5.7 %hidden_units.3 = (f32[64,3584]{1,0:T(8,128)}, f32[64,3584]{1,0:T(8,128)}, f32[64,3584]{1,0:T(8,128)}, f32[64,3584]{1,0:T(8,128)}) custom-call(bf16[512,512]{1,0:T(8,128)(2,1)} %bitcast.139, bf16[512,512]{1,0:T(8,128)(2,1)} %copy-done.11, bf16[3584,512]{1,0:T(8,128)(2,1)} %w.3, bf16[3584,512]{1,0:T(8,128)(2,1)} %collective-permute-done.1.wo), custom_call_target="tpu_custom_call" | custom-call | tf_op jit(solution)/shard_map/hidden_units/pallas_call | solution.py:19
  47.9 1.9 collective-permute-start.11
  49.9 4.2 %collective-permute-done.11 = f32[1,128]{1,0:T(1,128)S(1)} collective-permute-done((f32[1,128]{1,0:T(1,128)S(1)}, f32[1,128]{1,0:T(1,128)S(1)}, u32[]{:S(2)}, u32[]{:S(2)}) %collective-permute-start.11) | collective-permute-done | bytes 544 | tf_op jit(solution)/shard_map/squares/ppermute | solution.py:124
  55.0 1.4 add_convert_fusion.2
  57.7 2.1 collective-permute-start.14
  59.8 2.1 add_convert_fusion
  62.0 2.2 collective-permute-start.12
  65.9 2.0 collective-permute-start.16
  67.9 2.1 collective-permute-start.17
  70.0 4.4 %collective-permute-done.17 = f32[1,128]{1,0:T(1,128)S(1)} collective-permute-done((f32[1,128]{1,0:T(1,128)S(1)}, f32[1,128]{1,0:T(1,128)S(1)}, u32[]{:S(2)}, u32[]{:S(2)}) %collective-permute-start.17) | collective-permute-done | bytes 544 | tf_op jit(solution)/shard_map/squares/ppermute | solution.py:124
  75.6 3.9 %all-to-all-start.1 = ((bf16[8,128,512]{2,1,0:T(8,128)(2,1)}), bf16[8,128,512]{2,1,0:T(8,128)(2,1)S(1)}, u32[]{:S(2)}, u32[]{:S(2)}) async-start(bf16[8,128,512]{2,1,0:T(8,128)(2,1)} %broadcast_in_dim.22), calls=%async_computation.1 | async-start | bytes 2097152 | tf_op jit(solution)/shard_map/normed_rows/all_to_all | solution.py:232
  79.5 2.0 multiply_convert_fusion
  81.6 1.8 collective-permute-start.19
  83.7 3.2 %collective-permute-start.21 = (bf16[64,3584]{1,0:T(8,128)(2,1)S(1)}, bf16[64,3584]{1,0:T(8,128)(2,1)}, u32[]{:S(2)}, u32[]{:S(2)}) collective-permute-start(bf16[64,3584]{1,0:T(8,128)(2,1)S(1)} %get-tuple-element.155), channel_id=1, source_target_pairs={{0,12},{1,13},{2,14},{3,15},{4,0},{5,1},{6,2},{7,3},{8,4},{9,5},{1... | collective-permute-start | bytes 1376264 | tf_op jit(solution)/shard_map/ag_gate_a/ppermute | solution.py:124
  86.9 3.2 %collective-permute-start.22 = (bf16[128,3584]{1,0:T(8,128)(2,1)S(1)}, bf16[128,3584]{1,0:T(8,128)(2,1)S(1)}, u32[]{:S(2)}, u32[]{:S(2)}) collective-permute-start(bf16[128,3584]{1,0:T(8,128)(2,1)S(1)} %pad_maximum_fusion.2.refs_0_.refs_10_.refs_16_), channel_id=1, source_target_pairs={{0,2},{1,3},{2,0},{3,1},{4,6},{5,7},{6,4},{7,5},{8,10},{9,11},{10,... | collective-permute-start | bytes 2752520 | tf_op jit(solution)/shard_map/ag_x/ppermute | solution.py:124
  91.9 3.3 %collective-permute-done.19.refs_11_.refs_17_ = bf16[64,3584]{1,0:T(8,128)(2,1)} collective-permute-done((bf16[64,3584]{1,0:T(8,128)(2,1)S(1)}, bf16[64,3584]{1,0:T(8,128)(2,1)}, u32[]{:S(2)}, u32[]{:S(2)}) %collective-permute-start.19) | collective-permute-done | bytes 458784 | tf_op jit(solution)/shard_map/ag_up_a/ppermute | solution.py:124
  95.2 5.7 %collective-permute-done.21.refs_1_ = bf16[64,3584]{1,0:T(8,128)(2,1)} collective-permute-done((bf16[64,3584]{1,0:T(8,128)(2,1)S(1)}, bf16[64,3584]{1,0:T(8,128)(2,1)}, u32[]{:S(2)}, u32[]{:S(2)}) %collective-permute-start.21) | collective-permute-done | bytes 458784 | tf_op jit(solution)/shard_map/ag_gate_a/ppermute | solution.py:124
  100.9 2.6 %collective-permute-done.18.refs_3_ = bf16[64,3584]{1,0:T(8,128)(2,1)} collective-permute-done((bf16[64,3584]{1,0:T(8,128)(2,1)S(1)}, bf16[64,3584]{1,0:T(8,128)(2,1)}, u32[]{:S(2)}, u32[]{:S(2)}) %collective-permute-start.18) | collective-permute-done | bytes 458784 | tf_op jit(solution)/shard_map/ag_gate_b/ppermute | solution.py:124
  106.0 5.7 %collective-permute-done.22.refs_8_.refs_18_.refs_24_ = bf16[128,3584]{1,0:T(8,128)(2,1)S(1)} collective-permute-done((bf16[128,3584]{1,0:T(8,128)(2,1)S(1)}, bf16[128,3584]{1,0:T(8,128)(2,1)S(1)}, u32[]{:S(2)}, u32[]{:S(2)}) %collective-permute-start.22) | collective-permute-done | bytes 917536 | tf_op jit(solution)/shard_map/ag_x/ppermute | solution.py:124
  112.4 3.2 %collective-permute-start.28 = (bf16[64,3584]{1,0:T(8,128)(2,1)}, bf16[64,3584]{1,0:T(8,128)(2,1)}, u32[]{:S(2)}, u32[]{:S(2)}) collective-permute-start(bf16[64,3584]{1,0:T(8,128)(2,1)} %collective-permute-done.19.refs_11_.refs_17_), channel_id=1, source_target_pairs={{0,12},{1,13},{2,14},{3,15},{4,0},{5,1},{6,2},{7,3},{8,4},{9,5},{1... | collective-permute-start | bytes 1376264 | tf_op jit(solution)/shard_map/ag_up_f/ppermute | solution.py:124
  115.6 11.0 %collective-permute-done.27.refs_2_ = bf16[64,3584]{1,0:T(8,128)(2,1)S(1)} collective-permute-done((bf16[64,3584]{1,0:T(8,128)(2,1)}, bf16[64,3584]{1,0:T(8,128)(2,1)S(1)}, u32[]{:S(2)}, u32[]{:S(2)}) %collective-permute-start.27) | collective-permute-done | bytes 458784 | tf_op jit(solution)/shard_map/ag_gate_f/ppermute | solution.py:124
  128.3 3.0 %collective-permute-start.33 = (bf16[128,3584]{1,0:T(8,128)(2,1)S(1)}, bf16[128,3584]{1,0:T(8,128)(2,1)S(1)}, u32[]{:S(2)}, u32[]{:S(2)}) collective-permute-start(bf16[128,3584]{1,0:T(8,128)(2,1)S(1)} %collective-permute-done.22.refs_8_.refs_18_.refs_24_), channel_id=1, source_target_pairs={{0,12},{1,13},{2,14},{3,15},{4,0},{5,1},{6,2},{7,3},{8,4},{9,5},{1... | collective-permute-start | bytes 2752520 | tf_op jit(solution)/shard_map/ag_xa/ppermute | solution.py:124
  132.4 3.2 %collective-permute-start.35 = (bf16[64,3584]{1,0:T(8,128)(2,1)}, bf16[64,3584]{1,0:T(8,128)(2,1)}, u32[]{:S(2)}, u32[]{:S(2)}) collective-permute-start(bf16[64,3584]{1,0:T(8,128)(2,1)} %collective-permute-done.28.refs_12_.refs_18_), channel_id=1, source_target_pairs={{0,2},{1,3},{2,0},{3,1},{4,6},{5,7},{6,4},{7,5},{8,10},{9,11},{10,... | collective-permute-start | bytes 1376264 | tf_op jit(solution)/shard_map/ag_up_xf/ppermute | solution.py:124
  135.6 10.0 %input_grads.2 = f32[640,512]{1,0:T(8,128)} custom-call(bf16[128,3584]{1,0:T(8,128)(2,1)} %copy-done, bf16[64,3584]{1,0:T(8,128)(2,1)} %collective-permute-done.21.refs_1_, bf16[64,3584]{1,0:T(8,128)(2,1)} %copy-done.18, bf16[64,3584]{1,0:T(8,128)(2,1)} %collective-permute-done.18.refs_3_, bf16[128,3584]{1,0:T(8,128)(2,1)} %copy-done.5, ...), custom_call_target="tpu_custom_call" | custom-call | tf_op jit(solution)/shard_map/input_grads/pallas_call | solution.py:19
  145.7 3.8 %down_grads.2.refs_0_ = bf16[3584,512]{1,0:T(8,128)(2,1)} custom-call(bf16[512,896]{1,0:T(8,128)(2,1)} %bitcast.145, bf16[512,896]{1,0:T(8,128)(2,1)} %copy-done.20, bf16[1024,512]{1,0:T(8,128)(2,1)} %pad_maximum_fusion.1.right), custom_call_target="tpu_custom_call" | custom-call | tf_op jit(solution)/shard_map/down_grads/pallas_call | solution.py:104
  149.5 6.2 %collective-permute-done.35.refs_7_.refs_26_ = bf16[64,3584]{1,0:T(8,128)(2,1)} collective-permute-done((bf16[64,3584]{1,0:T(8,128)(2,1)}, bf16[64,3584]{1,0:T(8,128)(2,1)}, u32[]{:S(2)}, u32[]{:S(2)}) %collective-permute-start.35) | collective-permute-done | bytes 458784 | tf_op jit(solution)/shard_map/ag_up_xf/ppermute | solution.py:124
  156.9 5.9 %all-to-all-start.2 = ((bf16[8,64,2688]{2,1,0:T(8,128)(2,1)}), bf16[8,64,2688]{2,1,0:T(8,128)(2,1)}, u32[]{:S(2)}, u32[]{:S(2)}) async-start(bf16[8,64,2688]{2,1,0:T(8,128)(2,1)} %broadcast_in_dim.20), calls=%async_computation.2 | async-start | bytes 5505024 | tf_op jit(solution)/shard_map/hid_b/all_to_all | solution.py:179
  163.8 7.5 %input_grads.3 = f32[384,512]{1,0:T(8,128)} custom-call(bf16[128,3584]{1,0:T(8,128)(2,1)} %copy-done.2, bf16[64,3584]{1,0:T(8,128)(2,1)} %copy-done.16, bf16[128,3584]{1,0:T(8,128)(2,1)} %copy-done.1, bf16[128,3584]{1,0:T(8,128)(2,1)} %copy-done.3, bf16[64,3584]{1,0:T(8,128)(2,1)} %collective-permute-done.39.refs_4_.refs_14_, ...), custom_call_target="tpu_custom_call" | custom-call | tf_op jit(solution)/shard_map/input_grads/pallas_call | solution.py:19
  173.1 2.7 %collective-permute-start.44 = (bf16[2,2,64,512]{3,2,1,0:T(8,128)(2,1)S(1)}, bf16[2,2,64,512]{3,2,1,0:T(8,128)(2,1)S(1)}, u32[]{:S(2)}, u32[]{:S(2)}) collective-permute-start(bf16[2,2,64,512]{3,2,1,0:T(8,128)(2,1)S(1)} %get-tuple-element.202), channel_id=1, source_target_pairs={{0,96},{16,112},{32,0},{48,16},{64,32},{80,48},{96,64},{112,80},{1... | collective-permute-start | bytes 786440 | tf_op jit(solution)/shard_map/dn_y/ppermute | solution.py:133
  177.6 13.1 %gate_up_grads.1 = (bf16[512,3584]{1,0:T(8,128)(2,1)}, bf16[512,3584]{1,0:T(8,128)(2,1)}) custom-call(bf16[512,1024]{1,0:T(8,128)(2,1)} %bitcast.142, bf16[128,3584]{1,0:T(8,128)(2,1)} %copy-done, bf16[64,3584]{1,0:T(8,128)(2,1)} %collective-permute-done.21.refs_1_, bf16[64,3584]{1,0:T(8,128)(2,1)} %copy-done.18, ...), custom_call_target="tpu_custom_call" | custom-call | tf_op jit(solution)/shard_map/gate_up_grads/pallas_call | solution.py:19
  191.0 5.1 %collective-permute-done.45 = bf16[2,64,512]{2,1,0:T(8,128)(2,1)S(1)} collective-permute-done((bf16[2,64,512]{2,1,0:T(8,128)(2,1)S(1)}, bf16[2,64,512]{2,1,0:T(8,128)(2,1)S(1)}, u32[]{:S(2)}, u32[]{:S(2)}) %collective-permute-start.45) | collective-permute-done | bytes 131104 | tf_op jit(solution)/shard_map/dn_xl/ppermute | solution.py:133
  197.5 2.4 %collective-permute-start.48 = (f32[1,512]{1,0:T(1,128)S(1)}, f32[1,512]{1,0:T(1,128)S(1)}, u32[]{:S(2)}, u32[]{:S(2)}) collective-permute-start(f32[1,512]{1,0:T(1,128)S(1)} %bitcast.159), channel_id=1, source_target_pairs={{0,16},{16,0},{32,48},{48,32},{64,80},{80,64},{96,112},{112,96},{1... | collective-permute-start | bytes 6152 | tf_op jit(solution)/shard_map/gain/ppermute | solution.py:133
  199.9 5.0 %collective-permute-done.47 = f32[1,128]{1,0:T(1,128)S(1)} collective-permute-done((f32[1,128]{1,0:T(1,128)S(1)}, f32[1,128]{1,0:T(1,128)S(1)}, u32[]{:S(2)}, u32[]{:S(2)}) %collective-permute-start.47) | collective-permute-done | bytes 544 | tf_op jit(solution)/shard_map/proj/ppermute | solution.py:124
  207.1 3.0 %collective-permute-done.49 = f32[1,128]{1,0:T(1,128)S(1)} collective-permute-done((f32[1,128]{1,0:T(1,128)S(1)}, f32[1,128]{1,0:T(1,128)S(1)}, u32[]{:S(2)}, u32[]{:S(2)}) %collective-permute-start.49) | collective-permute-done | bytes 544 | tf_op jit(solution)/shard_map/proj/ppermute | solution.py:169
  210.4 2.7 %collective-permute-start.52 = (f32[1,128]{1,0:T(1,128)S(1)}, f32[1,128]{1,0:T(1,128)S(1)}, u32[]{:S(2)}, u32[]{:S(2)}) collective-permute-start(f32[1,128]{1,0:T(1,128)S(1)} %add.242), channel_id=1, source_target_pairs={{0,8},{1,9},{2,10},{3,11},{4,12},{5,13},{6,14},{7,15},{8,0},{9,1},... | collective-permute-start | bytes 1544 | tf_op jit(solution)/shard_map/proj/ppermute | solution.py:124
  213.1 3.0 %collective-permute-start.53 = (f32[1,512]{1,0:T(1,128)S(1)}, f32[1,512]{1,0:T(1,128)S(1)}, u32[]{:S(2)}, u32[]{:S(2)}) collective-permute-start(f32[1,512]{1,0:T(1,128)S(1)} %add.243), channel_id=1, source_target_pairs={{0,64},{16,80},{32,96},{48,112},{64,0},{80,16},{96,32},{112,48},{1... | collective-permute-start | bytes 6152 | tf_op jit(solution)/shard_map/gain/ppermute | solution.py:133
  216.0 6.8 %down_grads.3 = bf16[3584,512]{1,0:T(8,128)(2,1)} custom-call(bf16[512,2688]{1,0:T(8,128)(2,1)} %bitcast.62.left, bf16[512,2688]{1,0:T(8,128)(2,1)} %copy-done.10, bf16[1024,512]{1,0:T(8,128)(2,1)} %pad_maximum_fusion.1.right, bf16[3584,512]{1,0:T(8,128)(2,1)} %down_grads.2.refs_0_), custom_call_target="tpu_custom_call", output_to_operand_aliasing={{}: (3, {})} | custom-call | tf_op jit(solution)/shard_map/down_grads/pallas_call | solution.py:104
  (207 shorter events, 33.0 us)
Async XLA Ops:
  0.6 6.8 %collective-permute-start.1 = (bf16[3584,512]{1,0:T(8,128)(2,1)}, bf16[3584,512]{1,0:T(8,128)(2,1)}, u32[]{:S(2)}, u32[]{:S(2)}) collective-permute-start(bf16[3584,512]{1,0:T(8,128)(2,1)} %w.3), channel_id=1, source_target_pairs={{0,1},{1,0},{2,3},{3,2},{4,5},{5,4},{6,7},{7,6},{8,9},{9,8},{10,11... | collective-permute-start | bytes 11010056 | tf_op jit(solution)/shard_map/w_down/ppermute | solution.py:124
  0.7 6.4 %collective-permute-start = (bf16[128,512]{1,0:T(8,128)(2,1)}, bf16[128,512]{1,0:T(8,128)(2,1)S(1)}, u32[]{:S(2)}, u32[]{:S(2)}) collective-permute-start(bf16[128,512]{1,0:T(8,128)(2,1)} %param.9), channel_id=1, source_target_pairs={{0,16},{16,0},{32,48},{48,32},{64,80},{80,64},{96,112},{112,96},{1... | collective-permute-start | bytes 393224 | tf_op jit(solution)/shard_map/out_xl/ppermute | solution.py:133
  8.5 14.7 %collective-permute-start.3 = (bf16[2,2,1,64,512]{4,3,0,2,1:T(8,128)(2,1)S(1)}, bf16[2,2,1,64,512]{4,3,0,2,1:T(8,128)(2,1)}, u32[]{:S(2)}, u32[]{:S(2)}) collective-permute-start(bf16[2,2,1,64,512]{4,3,0,2,1:T(8,128)(2,1)S(1)} %fusion.12), channel_id=1, source_target_pairs={{0,96},{16,112},{32,0},{48,16},{64,32},{80,48},{96,64},{112,80},{1... | collective-permute-start | bytes 786440 | tf_op jit(solution)/shard_map/out_y/ppermute | solution.py:133
  11.5 12.7 %collective-permute-start.4 = (bf16[2,2,1,64,512]{4,3,0,2,1:T(8,128)(2,1)S(1)}, bf16[2,2,1,64,512]{4,3,0,2,1:T(8,128)(2,1)S(1)}, u32[]{:S(2)}, u32[]{:S(2)}) collective-permute-start(bf16[2,2,1,64,512]{4,3,0,2,1:T(8,128)(2,1)S(1)} %fusion.12), channel_id=1, source_target_pairs={{0,64},{16,80},{32,96},{48,112},{64,0},{80,16},{96,32},{112,48},{1... | collective-permute-start | bytes 786440 | tf_op jit(solution)/shard_map/out_y/ppermute | solution.py:133
  12.2 14.6 %collective-permute-start.5 = (bf16[2,2,1,64,512]{4,3,0,2,1:T(8,128)(2,1)S(1)}, bf16[2,2,1,64,512]{4,3,0,2,1:T(8,128)(2,1)S(1)}, u32[]{:S(2)}, u32[]{:S(2)}) collective-permute-start(bf16[2,2,1,64,512]{4,3,0,2,1:T(8,128)(2,1)S(1)} %fusion.12), channel_id=1, source_target_pairs={{0,32},{16,48},{32,64},{48,80},{64,96},{80,112},{96,0},{112,16},{1... | collective-permute-start | bytes 786440 | tf_op jit(solution)/shard_map/out_y/ppermute | solution.py:133
  13.1 10.0 %collective-permute-start.6 = (f32[1,128]{1,0:T(1,128)S(1)}, f32[1,128]{1,0:T(1,128)S(1)}, u32[]{:S(2)}, u32[]{:S(2)}) collective-permute-start(f32[1,128]{1,0:T(1,128)S(1)} %bitcast_add_fusion), channel_id=1, source_target_pairs={{0,4},{1,5},{2,6},{3,7},{4,0},{5,1},{6,2},{7,3},{8,12},{9,13},{10,... | collective-permute-start | bytes 1544 | tf_op jit(solution)/shard_map/squares/ppermute | solution.py:169
  15.2 21.5 %all-to-all-start = ((bf16[8,64,896]{2,1,0:T(8,128)(2,1)}), bf16[8,64,896]{2,1,0:T(8,128)(2,1)S(1)}, u32[]{:S(2)}, u32[]{:S(2)}) async-start(bf16[8,64,896]{2,1,0:T(8,128)(2,1)} %broadcast_in_dim.19), calls=%async_computation | async-start | bytes 1835008 | tf_op jit(solution)/shard_map/hid_a/all_to_all | solution.py:179
  36.7 17.4 %collective-permute-start.8 = (bf16[64,3584]{1,0:T(8,128)(2,1)}, bf16[64,3584]{1,0:T(8,128)(2,1)S(1)}, u32[]{:S(2)}, u32[]{:S(2)}) collective-permute-start(bf16[64,3584]{1,0:T(8,128)(2,1)} %get-tuple-element.126), channel_id=1, source_target_pairs={{0,2},{1,3},{2,0},{3,1},{4,6},{5,7},{6,4},{7,5},{8,10},{9,11},{10,... | collective-permute-start | bytes 1376264 | tf_op jit(solution)/shard_map/rs_x/ppermute | solution.py:124
  38.2 15.9 %collective-permute-start.9 = (bf16[64,3584]{1,0:T(8,128)(2,1)}, bf16[64,3584]{1,0:T(8,128)(2,1)S(1)}, u32[]{:S(2)}, u32[]{:S(2)}) collective-permute-start(bf16[64,3584]{1,0:T(8,128)(2,1)} %get-tuple-element.127), channel_id=1, source_target_pairs={{0,4},{1,5},{2,6},{3,7},{4,8},{5,9},{6,10},{7,11},{8,12},{9,13},{1... | collective-permute-start | bytes 1376264 | tf_op jit(solution)/shard_map/rs_b/ppermute | solution.py:124
  40.1 14.1 %collective-permute-start.10 = (bf16[64,3584]{1,0:T(8,128)(2,1)}, bf16[64,3584]{1,0:T(8,128)(2,1)}, u32[]{:S(2)}, u32[]{:S(2)}) collective-permute-start(bf16[64,3584]{1,0:T(8,128)(2,1)} %get-tuple-element.128), channel_id=1, source_target_pairs={{0,12},{1,13},{2,14},{3,15},{4,0},{5,1},{6,2},{7,3},{8,4},{9,5},{1... | collective-permute-start | bytes 1376264 | tf_op jit(solution)/shard_map/rs_a/ppermute | solution.py:124
  47.9 6.2 %collective-permute-start.11 = (f32[1,128]{1,0:T(1,128)S(1)}, f32[1,128]{1,0:T(1,128)S(1)}, u32[]{:S(2)}, u32[]{:S(2)}) collective-permute-start(f32[1,128]{1,0:T(1,128)S(1)} %add.209), channel_id=1, source_target_pairs={{0,8},{1,9},{2,10},{3,11},{4,12},{5,13},{6,14},{7,15},{8,0},{9,1},... | collective-permute-start | bytes 1544 | tf_op jit(solution)/shard_map/squares/ppermute | solution.py:124
  56.5 7.7 %collective-permute-start.13 = (bf16[32,3584]{1,0:T(8,128)(2,1)S(1)}, bf16[32,3584]{1,0:T(8,128)(2,1)S(1)}, u32[]{:S(2)}, u32[]{:S(2)}) collective-permute-start(bf16[32,3584]{1,0:T(8,128)(2,1)S(1)} %get-tuple-element.231), channel_id=1, source_target_pairs={{0,4},{1,5},{2,6},{3,7},{4,8},{5,9},{6,10},{7,11},{8,12},{9,13},{1... | collective-permute-start | bytes 688136 | tf_op jit(solution)/shard_map/rs_fb/ppermute | solution.py:124
  57.7 7.3 %collective-permute-start.14 = (bf16[32,3584]{1,0:T(8,128)(2,1)S(1)}, bf16[32,3584]{1,0:T(8,128)(2,1)S(1)}, u32[]{:S(2)}, u32[]{:S(2)}) collective-permute-start(bf16[32,3584]{1,0:T(8,128)(2,1)S(1)} %get-tuple-element.230), channel_id=1, source_target_pairs={{0,12},{1,13},{2,14},{3,15},{4,0},{5,1},{6,2},{7,3},{8,4},{9,5},{1... | collective-permute-start | bytes 688136 | tf_op jit(solution)/shard_map/rs_fa/ppermute | solution.py:124
  62.0 17.5 %collective-permute-start.12 = (bf16[64,3584]{1,0:T(8,128)(2,1)}, bf16[64,3584]{1,0:T(8,128)(2,1)}, u32[]{:S(2)}, u32[]{:S(2)}) collective-permute-start(bf16[64,3584]{1,0:T(8,128)(2,1)} %add_convert_fusion), channel_id=1, source_target_pairs={{0,2},{1,3},{2,0},{3,1},{4,6},{5,7},{6,4},{7,5},{8,10},{9,11},{10,... | collective-permute-start | bytes 1376264 | tf_op jit(solution)/shard_map/rs_xl/ppermute | solution.py:124
  65.9 13.6 %collective-permute-start.16 = (bf16[64,3584]{1,0:T(8,128)(2,1)}, bf16[64,3584]{1,0:T(8,128)(2,1)}, u32[]{:S(2)}, u32[]{:S(2)}) collective-permute-start(bf16[64,3584]{1,0:T(8,128)(2,1)} %pad_maximum_fusion.4), channel_id=1, source_target_pairs={{0,12},{1,13},{2,14},{3,15},{4,0},{5,1},{6,2},{7,3},{8,4},{9,5},{1... | collective-permute-start | bytes 1376264 | tf_op jit(solution)/shard_map/rs_al/ppermute | solution.py:124
  67.9 11.6 %collective-permute-start.15 = (bf16[64,3584]{1,0:T(8,128)(2,1)}, bf16[64,3584]{1,0:T(8,128)(2,1)}, u32[]{:S(2)}, u32[]{:S(2)}) collective-permute-start(bf16[64,3584]{1,0:T(8,128)(2,1)} %pad_maximum_fusion.3), channel_id=1, source_target_pairs={{0,4},{1,5},{2,6},{3,7},{4,8},{5,9},{6,10},{7,11},{8,12},{9,13},{1... | collective-permute-start | bytes 1376264 | tf_op jit(solution)/shard_map/rs_bl/ppermute | solution.py:124
  67.9 6.5 %collective-permute-start.17 = (f32[1,128]{1,0:T(1,128)S(1)}, f32[1,128]{1,0:T(1,128)S(1)}, u32[]{:S(2)}, u32[]{:S(2)}) collective-permute-start(f32[1,128]{1,0:T(1,128)S(1)} %add.210), channel_id=1, source_target_pairs={{0,2},{1,3},{2,0},{3,1},{4,6},{5,7},{6,4},{7,5},{8,10},{9,11},{10,... | collective-permute-start | bytes 1544 | tf_op jit(solution)/shard_map/squares/ppermute | solution.py:124
  75.6 28.4 %all-to-all-start.1 = ((bf16[8,128,512]{2,1,0:T(8,128)(2,1)}), bf16[8,128,512]{2,1,0:T(8,128)(2,1)S(1)}, u32[]{:S(2)}, u32[]{:S(2)}) async-start(bf16[8,128,512]{2,1,0:T(8,128)(2,1)} %broadcast_in_dim.22), calls=%async_computation.1 | async-start | bytes 2097152 | tf_op jit(solution)/shard_map/normed_rows/all_to_all | solution.py:232
  81.6 13.6 %collective-permute-start.19 = (bf16[64,3584]{1,0:T(8,128)(2,1)S(1)}, bf16[64,3584]{1,0:T(8,128)(2,1)}, u32[]{:S(2)}, u32[]{:S(2)}) collective-permute-start(bf16[64,3584]{1,0:T(8,128)(2,1)S(1)} %get-tuple-element.156), channel_id=1, source_target_pairs={{0,12},{1,13},{2,14},{3,15},{4,0},{5,1},{6,2},{7,3},{8,4},{9,5},{1... | collective-permute-start | bytes 1376264 | tf_op jit(solution)/shard_map/ag_up_a/ppermute | solution.py:124
  83.4 20.0 %collective-permute-start.20 = (bf16[64,3584]{1,0:T(8,128)(2,1)S(1)}, bf16[64,3584]{1,0:T(8,128)(2,1)}, u32[]{:S(2)}, u32[]{:S(2)}) collective-permute-start(bf16[64,3584]{1,0:T(8,128)(2,1)S(1)} %get-tuple-element.156), channel_id=1, source_target_pairs={{0,4},{1,5},{2,6},{3,7},{4,8},{5,9},{6,10},{7,11},{8,12},{9,13},{1... | collective-permute-start | bytes 1376264 | tf_op jit(solution)/shard_map/ag_up_b/ppermute | solution.py:124
  83.7 19.8 %collective-permute-start.18 = (bf16[64,3584]{1,0:T(8,128)(2,1)S(1)}, bf16[64,3584]{1,0:T(8,128)(2,1)}, u32[]{:S(2)}, u32[]{:S(2)}) collective-permute-start(bf16[64,3584]{1,0:T(8,128)(2,1)S(1)} %get-tuple-element.155), channel_id=1, source_target_pairs={{0,4},{1,5},{2,6},{3,7},{4,8},{5,9},{6,10},{7,11},{8,12},{9,13},{1... | collective-permute-start | bytes 1376264 | tf_op jit(solution)/shard_map/ag_gate_b/ppermute | solution.py:124
  83.7 17.2 %collective-permute-start.21 = (bf16[64,3584]{1,0:T(8,128)(2,1)S(1)}, bf16[64,3584]{1,0:T(8,128)(2,1)}, u32[]{:S(2)}, u32[]{:S(2)}) collective-permute-start(bf16[64,3584]{1,0:T(8,128)(2,1)S(1)} %get-tuple-element.155), channel_id=1, source_target_pairs={{0,12},{1,13},{2,14},{3,15},{4,0},{5,1},{6,2},{7,3},{8,4},{9,5},{1... | collective-permute-start | bytes 1376264 | tf_op jit(solution)/shard_map/ag_gate_a/ppermute | solution.py:124
  86.9 24.7 %collective-permute-start.22 = (bf16[128,3584]{1,0:T(8,128)(2,1)S(1)}, bf16[128,3584]{1,0:T(8,128)(2,1)S(1)}, u32[]{:S(2)}, u32[]{:S(2)}) collective-permute-start(bf16[128,3584]{1,0:T(8,128)(2,1)S(1)} %pad_maximum_fusion.2.refs_0_.refs_10_.refs_16_), channel_id=1, source_target_pairs={{0,2},{1,3},{2,0},{3,1},{4,6},{5,7},{6,4},{7,5},{8,10},{9,11},{10,... | collective-permute-start | bytes 2752520 | tf_op jit(solution)/shard_map/ag_x/ppermute | solution.py:124
  95.2 16.4 %collective-permute-start.23 = (bf16[64,3584]{1,0:T(8,128)(2,1)}, bf16[64,3584]{1,0:T(8,128)(2,1)S(1)}, u32[]{:S(2)}, u32[]{:S(2)}) collective-permute-start(bf16[64,3584]{1,0:T(8,128)(2,1)} %collective-permute-done.19.refs_11_.refs_17_), channel_id=1, source_target_pairs={{0,1},{1,0},{2,3},{3,2},{4,5},{5,4},{6,7},{7,6},{8,9},{9,8},{10,11... | collective-permute-start | bytes 1376264 | tf_op jit(solution)/shard_map/ag_core/ppermute | solution.py:124
  100.9 10.8 %collective-permute-start.24 = (bf16[64,3584]{1,0:T(8,128)(2,1)}, bf16[64,3584]{1,0:T(8,128)(2,1)}, u32[]{:S(2)}, u32[]{:S(2)}) collective-permute-start(bf16[64,3584]{1,0:T(8,128)(2,1)} %collective-permute-done.21.refs_1_), channel_id=1, source_target_pairs={{0,1},{1,0},{2,3},{3,2},{4,5},{5,4},{6,7},{7,6},{8,9},{9,8},{10,11... | collective-permute-start | bytes 1376264 | tf_op jit(solution)/shard_map/ag_core/ppermute | solution.py:124
  103.5 8.2 %collective-permute-start.25 = (bf16[64,3584]{1,0:T(8,128)(2,1)}, bf16[64,3584]{1,0:T(8,128)(2,1)}, u32[]{:S(2)}, u32[]{:S(2)}) collective-permute-start(bf16[64,3584]{1,0:T(8,128)(2,1)} %collective-permute-done.18.refs_3_), channel_id=1, source_target_pairs={{0,1},{1,0},{2,3},{3,2},{4,5},{5,4},{6,7},{7,6},{8,9},{9,8},{10,11... | collective-permute-start | bytes 1376264 | tf_op jit(solution)/shard_map/ag_core/ppermute | solution.py:124
  103.5 8.2 %collective-permute-start.26 = (bf16[64,3584]{1,0:T(8,128)(2,1)}, bf16[64,3584]{1,0:T(8,128)(2,1)}, u32[]{:S(2)}, u32[]{:S(2)}) collective-permute-start(bf16[64,3584]{1,0:T(8,128)(2,1)} %collective-permute-done.20.refs_13_.refs_19_), channel_id=1, source_target_pairs={{0,1},{1,0},{2,3},{3,2},{4,5},{5,4},{6,7},{7,6},{8,9},{9,8},{10,11... | collective-permute-start | bytes 1376264 | tf_op jit(solution)/shard_map/ag_core/ppermute | solution.py:124
  111.7 15.0 %collective-permute-start.29 = (bf16[512,896]{1,0:T(8,128)(2,1)}, bf16[512,896]{1,0:T(8,128)(2,1)S(1)}, u32[]{:S(2)}, u32[]{:S(2)}) collective-permute-start(bf16[512,896]{1,0:T(8,128)(2,1)} %bitcast.144), channel_id=1, source_target_pairs={{0,1},{1,0},{2,3},{3,2},{4,5},{5,4},{6,7},{7,6},{8,9},{9,8},{10,11... | collective-permute-start | bytes 2752520 | tf_op jit(solution)/shard_map/hid_core/ppermute | solution.py:124
  111.8 14.9 %collective-permute-start.30 = (bf16[128,3584]{1,0:T(8,128)(2,1)S(1)}, bf16[128,3584]{1,0:T(8,128)(2,1)S(1)}, u32[]{:S(2)}, u32[]{:S(2)}) collective-permute-start(bf16[128,3584]{1,0:T(8,128)(2,1)S(1)} %pad_maximum_fusion.2.refs_0_.refs_10_.refs_16_), channel_id=1, source_target_pairs={{0,1},{1,0},{2,3},{3,2},{4,5},{5,4},{6,7},{7,6},{8,9},{9,8},{10,11... | collective-permute-start | bytes 2752520 | tf_op jit(solution)/shard_map/ag_core/ppermute | solution.py:124
  112.3 14.4 %collective-permute-start.31 = (bf16[128,3584]{1,0:T(8,128)(2,1)S(1)}, bf16[128,3584]{1,0:T(8,128)(2,1)S(1)}, u32[]{:S(2)}, u32[]{:S(2)}) collective-permute-start(bf16[128,3584]{1,0:T(8,128)(2,1)S(1)} %collective-permute-done.22.refs_8_.refs_18_.refs_24_), channel_id=1, source_target_pairs={{0,1},{1,0},{2,3},{3,2},{4,5},{5,4},{6,7},{7,6},{8,9},{9,8},{10,11... | collective-permute-start | bytes 2752520 | tf_op jit(solution)/shard_map/ag_core/ppermute | solution.py:124
  112.4 14.3 %collective-permute-start.27 = (bf16[64,3584]{1,0:T(8,128)(2,1)}, bf16[64,3584]{1,0:T(8,128)(2,1)S(1)}, u32[]{:S(2)}, u32[]{:S(2)}) collective-permute-start(bf16[64,3584]{1,0:T(8,128)(2,1)} %collective-permute-done.18.refs_3_), channel_id=1, source_target_pairs={{0,4},{1,5},{2,6},{3,7},{4,8},{5,9},{6,10},{7,11},{8,12},{9,13},{1... | collective-permute-start | bytes 1376264 | tf_op jit(solution)/shard_map/ag_gate_f/ppermute | solution.py:124
  112.4 14.3 %collective-permute-start.28 = (bf16[64,3584]{1,0:T(8,128)(2,1)}, bf16[64,3584]{1,0:T(8,128)(2,1)}, u32[]{:S(2)}, u32[]{:S(2)}) collective-permute-start(bf16[64,3584]{1,0:T(8,128)(2,1)} %collective-permute-done.19.refs_11_.refs_17_), channel_id=1, source_target_pairs={{0,12},{1,13},{2,14},{3,15},{4,0},{5,1},{6,2},{7,3},{8,4},{9,5},{1... | collective-permute-start | bytes 1376264 | tf_op jit(solution)/shard_map/ag_up_f/ppermute | solution.py:124
  127.9 27.8 %collective-permute-start.32 = (bf16[128,3584]{1,0:T(8,128)(2,1)S(1)}, bf16[128,3584]{1,0:T(8,128)(2,1)S(1)}, u32[]{:S(2)}, u32[]{:S(2)}) collective-permute-start(bf16[128,3584]{1,0:T(8,128)(2,1)S(1)} %collective-permute-done.22.refs_8_.refs_18_.refs_24_), channel_id=1, source_target_pairs={{0,4},{1,5},{2,6},{3,7},{4,8},{5,9},{6,10},{7,11},{8,12},{9,13},{1... | collective-permute-start | bytes 2752520 | tf_op jit(solution)/shard_map/ag_xb/ppermute | solution.py:124
  128.3 27.4 %collective-permute-start.33 = (bf16[128,3584]{1,0:T(8,128)(2,1)S(1)}, bf16[128,3584]{1,0:T(8,128)(2,1)S(1)}, u32[]{:S(2)}, u32[]{:S(2)}) collective-permute-start(bf16[128,3584]{1,0:T(8,128)(2,1)S(1)} %collective-permute-done.22.refs_8_.refs_18_.refs_24_), channel_id=1, source_target_pairs={{0,12},{1,13},{2,14},{3,15},{4,0},{5,1},{6,2},{7,3},{8,4},{9,5},{1... | collective-permute-start | bytes 2752520 | tf_op jit(solution)/shard_map/ag_xa/ppermute | solution.py:124
  131.3 18.2 %collective-permute-start.34 = (bf16[64,3584]{1,0:T(8,128)(2,1)S(1)}, bf16[64,3584]{1,0:T(8,128)(2,1)S(1)}, u32[]{:S(2)}, u32[]{:S(2)}) collective-permute-start(bf16[64,3584]{1,0:T(8,128)(2,1)S(1)} %collective-permute-done.27.refs_2_), channel_id=1, source_target_pairs={{0,2},{1,3},{2,0},{3,1},{4,6},{5,7},{6,4},{7,5},{8,10},{9,11},{10,... | collective-permute-start | bytes 1376264 | tf_op jit(solution)/shard_map/ag_gate_xf/ppermute | solution.py:124
  132.4 23.3 %collective-permute-start.35 = (bf16[64,3584]{1,0:T(8,128)(2,1)}, bf16[64,3584]{1,0:T(8,128)(2,1)}, u32[]{:S(2)}, u32[]{:S(2)}) collective-permute-start(bf16[64,3584]{1,0:T(8,128)(2,1)} %collective-permute-done.28.refs_12_.refs_18_), channel_id=1, source_target_pairs={{0,2},{1,3},{2,0},{3,1},{4,6},{5,7},{6,4},{7,5},{8,10},{9,11},{10,... | collective-permute-start | bytes 1376264 | tf_op jit(solution)/shard_map/ag_up_xf/ppermute | solution.py:124
  155.7 7.1 %collective-permute-start.38 = (bf16[128,3584]{1,0:T(8,128)(2,1)S(1)}, bf16[128,3584]{1,0:T(8,128)(2,1)S(1)}, u32[]{:S(2)}, u32[]{:S(2)}) collective-permute-start(bf16[128,3584]{1,0:T(8,128)(2,1)S(1)} %collective-permute-done.33.refs_0_.refs_6_.refs_9_.refs_25_), channel_id=1, source_target_pairs={{0,1},{1,0},{2,3},{3,2},{4,5},{5,4},{6,7},{7,6},{8,9},{9,8},{10,11... | collective-permute-start | bytes 2752520 | tf_op jit(solution)/shard_map/ag_core/ppermute | solution.py:124
  155.8 7.0 %collective-permute-start.40 = (bf16[128,3584]{1,0:T(8,128)(2,1)S(1)}, bf16[128,3584]{1,0:T(8,128)(2,1)}, u32[]{:S(2)}, u32[]{:S(2)}) collective-permute-start(bf16[128,3584]{1,0:T(8,128)(2,1)S(1)} %collective-permute-done.32.refs_2_.refs_8_.refs_11_.refs_27_), channel_id=1, source_target_pairs={{0,1},{1,0},{2,3},{3,2},{4,5},{5,4},{6,7},{7,6},{8,9},{9,8},{10,11... | collective-permute-start | bytes 2752520 | tf_op jit(solution)/shard_map/ag_core/ppermute | solution.py:124
  156.3 6.5 %collective-permute-start.39 = (bf16[64,3584]{1,0:T(8,128)(2,1)S(1)}, bf16[64,3584]{1,0:T(8,128)(2,1)}, u32[]{:S(2)}, u32[]{:S(2)}) collective-permute-start(bf16[64,3584]{1,0:T(8,128)(2,1)S(1)} %collective-permute-done.34.refs_1_.refs_10_), channel_id=1, source_target_pairs={{0,1},{1,0},{2,3},{3,2},{4,5},{5,4},{6,7},{7,6},{8,9},{9,8},{10,11... | collective-permute-start | bytes 1376264 | tf_op jit(solution)/shard_map/ag_core/ppermute | solution.py:124
  156.4 6.4 %collective-permute-start.41 = (bf16[64,3584]{1,0:T(8,128)(2,1)}, bf16[64,3584]{1,0:T(8,128)(2,1)}, u32[]{:S(2)}, u32[]{:S(2)}) collective-permute-start(bf16[64,3584]{1,0:T(8,128)(2,1)} %collective-permute-done.35.refs_7_.refs_26_), channel_id=1, source_target_pairs={{0,1},{1,0},{2,3},{3,2},{4,5},{5,4},{6,7},{7,6},{8,9},{9,8},{10,11... | collective-permute-start | bytes 1376264 | tf_op jit(solution)/shard_map/ag_core/ppermute | solution.py:124
  156.9 48.1 %all-to-all-start.2 = ((bf16[8,64,2688]{2,1,0:T(8,128)(2,1)}), bf16[8,64,2688]{2,1,0:T(8,128)(2,1)}, u32[]{:S(2)}, u32[]{:S(2)}) async-start(bf16[8,64,2688]{2,1,0:T(8,128)(2,1)} %broadcast_in_dim.20), calls=%async_computation.2 | async-start | bytes 5505024 | tf_op jit(solution)/shard_map/hid_b/all_to_all | solution.py:179
  173.1 17.6 %collective-permute-start.44 = (bf16[2,2,64,512]{3,2,1,0:T(8,128)(2,1)S(1)}, bf16[2,2,64,512]{3,2,1,0:T(8,128)(2,1)S(1)}, u32[]{:S(2)}, u32[]{:S(2)}) collective-permute-start(bf16[2,2,64,512]{3,2,1,0:T(8,128)(2,1)S(1)} %get-tuple-element.202), channel_id=1, source_target_pairs={{0,96},{16,112},{32,0},{48,16},{64,32},{80,48},{96,64},{112,80},{1... | collective-permute-start | bytes 786440 | tf_op jit(solution)/shard_map/dn_y/ppermute | solution.py:133
  175.8 14.9 %collective-permute-start.43 = (bf16[2,2,64,512]{3,2,1,0:T(8,128)(2,1)S(1)}, bf16[2,2,64,512]{3,2,1,0:T(8,128)(2,1)S(1)}, u32[]{:S(2)}, u32[]{:S(2)}) collective-permute-start(bf16[2,2,64,512]{3,2,1,0:T(8,128)(2,1)S(1)} %get-tuple-element.201), channel_id=1, source_target_pairs={{0,64},{16,80},{32,96},{48,112},{64,0},{80,16},{96,32},{112,48},{1... | collective-permute-start | bytes 786440 | tf_op jit(solution)/shard_map/dn_y/ppermute | solution.py:133
  176.6 14.1 %collective-permute-start.42 = (bf16[2,2,64,512]{3,2,1,0:T(8,128)(2,1)S(1)}, bf16[2,2,64,512]{3,2,1,0:T(8,128)(2,1)S(1)}, u32[]{:S(2)}, u32[]{:S(2)}) collective-permute-start(bf16[2,2,64,512]{3,2,1,0:T(8,128)(2,1)S(1)} %get-tuple-element.200), channel_id=1, source_target_pairs={{0,32},{16,48},{32,64},{48,80},{64,96},{80,112},{96,0},{112,16},{1... | collective-permute-start | bytes 786440 | tf_op jit(solution)/shard_map/dn_y/ppermute | solution.py:133
  197.5 7.5 %collective-permute-start.48 = (f32[1,512]{1,0:T(1,128)S(1)}, f32[1,512]{1,0:T(1,128)S(1)}, u32[]{:S(2)}, u32[]{:S(2)}) collective-permute-start(f32[1,512]{1,0:T(1,128)S(1)} %bitcast.159), channel_id=1, source_target_pairs={{0,16},{16,0},{32,48},{48,32},{64,80},{80,64},{96,112},{112,96},{1... | collective-permute-start | bytes 6152 | tf_op jit(solution)/shard_map/gain/ppermute | solution.py:133
  205.0 5.4 %collective-permute-start.51 = (bf16[512,2688]{1,0:T(8,128)(2,1)}, bf16[512,2688]{1,0:T(8,128)(2,1)S(1)}, u32[]{:S(2)}, u32[]{:S(2)}) collective-permute-start(bf16[512,2688]{1,0:T(8,128)(2,1)} %bitcast.62.left), channel_id=1, source_target_pairs={{0,1},{1,0},{2,3},{3,2},{4,5},{5,4},{6,7},{7,6},{8,9},{9,8},{10,11... | collective-permute-start | bytes 8257544 | tf_op jit(solution)/shard_map/hid_core/ppermute | solution.py:124
  210.4 12.5 %collective-permute-start.52 = (f32[1,128]{1,0:T(1,128)S(1)}, f32[1,128]{1,0:T(1,128)S(1)}, u32[]{:S(2)}, u32[]{:S(2)}) collective-permute-start(f32[1,128]{1,0:T(1,128)S(1)} %add.242), channel_id=1, source_target_pairs={{0,8},{1,9},{2,10},{3,11},{4,12},{5,13},{6,14},{7,15},{8,0},{9,1},... | collective-permute-start | bytes 1544 | tf_op jit(solution)/shard_map/proj/ppermute | solution.py:124
  213.1 10.6 %collective-permute-start.53 = (f32[1,512]{1,0:T(1,128)S(1)}, f32[1,512]{1,0:T(1,128)S(1)}, u32[]{:S(2)}, u32[]{:S(2)}) collective-permute-start(f32[1,512]{1,0:T(1,128)S(1)} %add.243), channel_id=1, source_target_pairs={{0,64},{16,80},{32,96},{48,112},{64,0},{80,16},{96,32},{112,48},{1... | collective-permute-start | bytes 6152 | tf_op jit(solution)/shard_map/gain/ppermute | solution.py:133
  (42 other events, 320.2 us)
